TPU v7x, 256 devices: a whole 4x4x8 slice. The times are simulated.
256 devices in a mesh: prow: 16 (over z, y_lo), pcol: 16 (over x, y_hi, core).
Axes of the slice: x: 4, y: 4 (y_hi: 2, y_lo: 2; y = y_hi * 2 + y_lo), z: 8, core: 2. Of those that a mesh axis runs over, the one named last changes fastest.
Arguments:
- ainv: bfloat16 [16384, 16384], P('prow', 'pcol'), may hold values from -6 to 6
- l_panels: bfloat16 [16, 16384, 256], P('pcol', 'prow'), may hold values from -0.046875 to 0.046875
- dinv: float32 [16, 256, 256], P('pcol'), may hold values from -6 to 6
- ancestors: int32 [16, 64], replicated, may hold values from 0 to 127, as said below
- block_slot: int32 [128], replicated, may hold values from 0 to 127, each once
Outputs:
- inverse_column: bfloat16 [16, 16384, 256], P('pcol', 'prow')
- diagonal_block: float32 [16, 256, 256], P('pcol')
Inputs may be any that keep to these rules, and one draw needn't show every extreme that they name: `ancestors`: each row holds 64 distinct block numbers.
All inputs are finite; a program needn't handle non-finite values.
Results may differ from a plain program's by a relative error of at most 0.0095.
Values may be sent and summed in bfloat16 or wider, within the bound.
No kernel may reach another device: no remote copies, remote signals or barrier semaphores. Data moves between devices by JAX's collectives and lax.ppermute only.
A program may use at most 128 MiB of HBM per device.

v0:
```python
import jax
import jax.numpy as jnp
from jax import lax
from jax.sharding import PartitionSpec as P

BS = 128


def membership(ancestors, block_slot):
    numbers = jnp.arange(block_slot.shape[0], dtype=jnp.int32)
    chosen = (ancestors[:, :, None] == numbers[None, None, :]).astype(jnp.int32)
    slots_used = jnp.sum(chosen * block_slot[None, None, :], axis=2)
    present = jnp.any(slots_used[:, :, None] == numbers[None, None, :], axis=1)
    return jnp.repeat(present, BS, axis=1)


def body(ainv, l_panels, dinv, ancestors, block_slot):
    row_flags = membership(ancestors, block_slot)
    per_device = l_panels.shape[0]
    local_rows = l_panels.shape[1]
    row_index = lax.axis_index("prow")
    column_index = lax.axis_index("pcol")
    own_flags = lax.dynamic_slice_in_dim(row_flags, column_index * per_device, per_device, 0)
    local_flags = lax.dynamic_slice_in_dim(own_flags, row_index * local_rows, local_rows, 1)
    masked_local = jnp.where(local_flags[:, :, None], l_panels, jnp.zeros((), l_panels.dtype))
    panel_full = lax.all_gather(masked_local, "prow", axis=1, tiled=True)
    partial_terms = jnp.einsum(
        "rc,kcw->krw",
        ainv,
        lax.all_to_all(panel_full, "pcol", split_axis=1, concat_axis=0, tiled=True),
        preferred_element_type=jnp.float32,
    )
    summed = lax.psum_scatter(partial_terms, "pcol", scatter_dimension=0, tiled=True)
    inverse_column = jnp.where(local_flags[:, :, None], -summed, jnp.zeros((), jnp.float32)).astype(
        jnp.bfloat16
    )
    local_terms = jnp.einsum(
        "kiw,kiv->kwv", masked_local, inverse_column, preferred_element_type=jnp.float32
    )
    diagonal_block = dinv - lax.psum(local_terms.astype(jnp.bfloat16), "prow").astype(jnp.float32)
    return (inverse_column, diagonal_block)


def solution(mesh):
    return jax.shard_map(
        body,
        mesh=mesh,
        in_specs=(P("prow", "pcol"), P("pcol", "prow", None), P("pcol", None, None), P(), P()),
        out_specs=(P("pcol", "prow", None), P("pcol", None, None)),
        check_vma=False,
    )
```

profile of v0, /device:TPU:2, one launch (start us, length us, event | category | flops | bytes accessed | tf_op | source)
XLA Modules:
  0.0 767.2 jit_solution(9509320759858148023)
XLA Ops:
  7.2 0.0 copy-start
  7.2 0.0 all-gather.2.cloned.1.call-start
  7.2 1.4 select_reduce_fusion
  8.6 0.2 fusion.4
  8.8 0.3 broadcast_in_dim.34
  9.2 0.2 copy.25
  9.4 1.2 copy.17
  10.7 0.1 dynamic-slice_reduce_fusion
  10.8 0.8 broadcast_select_fusion
  11.6 0.0 all-gather.2.cloned.1.call-update
  11.6 0.0 reduce-scatter.2.cloned.1.call-start
  11.7 185.6 %all-gather.2.cloned.1.call-done = bf16[1,16384,256]{1,2,0:T(8,128)(2,1)} async-done(((bf16[1,1024,256]{1,2,0:T(8,128)(2,1)}), bf16[1,16384,256]{1,2,0:T(8,128)(2,1)}) %all-gather.2.cloned.1.call-update) | async-done | bytes 8388624 | tf_op jit(solution)/shard_map/all_gather | solution.py:26
  197.2 34.5 %copy.18 = bf16[1,16384,256]{2,0,1:T(2,128)(2,1)} copy(bf16[1,16384,256]{1,2,0:T(8,128)(2,1)} %all-gather.2.cloned.1.call-done) | data formatting | bytes 16777216 | tf_op jit(solution)/shard_map/all_gather | solution.py:26
  231.7 0.5 broadcast.10
  232.2 84.6 %reduce.2 = bf16[16384,256]{1,0:T(8,128)(2,1)} reduce(bf16[16384,1,256]{2,1,0:T(2,128)(2,1)} %bitcast.22, bf16[]{:T(256)} %broadcast.10), dimensions={1}, to_apply=%bitcast.17.reduce_sub_computation | reduce | bytes 16777218
  316.8 12.7 %reshape.29 = bf16[16,2,131072]{2,1,0:T(2,128)(2,1)} reshape(bf16[16384,256]{1,0:T(8,128)(2,1)} %reduce.2) | data formatting | bytes 16777216
  329.5 101.4 %all_to_all.12 = bf16[16,2,131072]{2,1,0:T(2,128)(2,1)} all-to-all(bf16[16,2,131072]{2,1,0:T(2,128)(2,1)} %reshape.29), channel_id=1, replica_groups=mesh['prow'=16,'pcol'=16] {'pcol'}, dimensions={0} | all-to-all | bytes 16777216 | tf_op jit(solution)/shard_map/all_to_all | solution.py:30
  430.9 16.4 %reshape.30 = bf16[16384,1,256]{2,1,0:T(2,128)(2,1)} reshape(bf16[16,2,131072]{2,1,0:T(2,128)(2,1)} %all_to_all.12) | data formatting | bytes 16777216
  447.3 8.9 %copy.22 = bf16[1,16384,256]{2,1,0:T(8,128)(2,1)S(1)} copy(bf16[1,16384,256]{2,0,1:T(2,128)(2,1)} %bitcast.21) | data formatting | bytes 16777216
  456.2 0.0 copy-done
  456.2 11.7 %convolution_bitcast_fusion = f32[16,1024,256]{1,2,0:T(8,128)} fusion(bf16[16,1024,256]{2,1,0:T(8,128)(2,1)S(1)} %bitcast.23, bf16[1024,1024]{1,0:T(8,128)(2,1)S(1)} %copy-done), kind=kOutput, calls=%fused_computation | convolution fusion | flops 8589934592 | bytes 27262976 | tf_op jit(solution)/shard_map/rc,kcw->krw/dot_general | solution.py:27
  467.9 0.0 reduce-scatter.2.cloned.1.call-update
  467.9 0.0 all-reduce.2.cloned.1.call-start
  467.9 154.0 %reduce-scatter.2.cloned.1.call-done = f32[1,1024,256]{1,2,0:T(8,128)} async-done(((f32[16,1024,256]{1,2,0:T(8,128)}), f32[1,1024,256]{1,2,0:T(8,128)}) %reduce-scatter.2.cloned.1.call-update) | async-done | bytes 1048592 | tf_op jit(solution)/shard_map/reduce_scatter | solution.py:33
  621.9 1.3 select_convert_fusion
  623.3 0.0 copy-done.1
  623.3 1.0 fusion.1
  624.3 0.0 all-reduce.2.cloned.1.call-update
  624.3 1.0 copy.20
  625.3 133.7 %all-reduce.2.cloned.1.call-done = bf16[1,256,256]{2,1,0:T(8,128)(2,1)} async-done(((bf16[1,256,256]{2,1,0:T(8,128)(2,1)}), bf16[1,256,256]{2,1,0:T(8,128)(2,1)}) %all-reduce.2.cloned.1.call-update) | async-done | bytes 131088 | tf_op jit(solution)/shard_map/psum | solution.py:40
  759.0 0.0 copy-done.2
  759.0 1.6 convert_subtract_fusion
  (2 shorter events, 0.0 us)
Async XLA Ops:
  7.2 449.0 %copy-start = (bf16[1024,1024]{1,0:T(8,128)(2,1)S(1)}, bf16[1024,1024]{1,0:T(8,128)(2,1)}, u32[]{:S(2)}) copy-start(bf16[1024,1024]{1,0:T(8,128)(2,1)} %param.5) | copy-start | bytes 6291460
  7.2 190.1 %all-gather.2.cloned.1.call-start = ((), (), s32[]{:S(2)}) async-start(), calls=%async_computation.2 | async-start | bytes 8912896 | tf_op jit(solution)/shard_map/all_gather | solution.py:26
  11.6 610.3 %reduce-scatter.2.cloned.1.call-start = ((), (), s32[]{:S(2)}) async-start(), calls=%async_computation.3 | async-start | bytes 17825792 | tf_op jit(solution)/shard_map/reduce_scatter | solution.py:33
  467.9 155.4 %copy-start.1 = (bf16[1,1024,256]{1,2,0:T(8,128)(2,1)S(1)}, bf16[1,1024,256]{1,2,0:T(8,128)(2,1)}, u32[]{:S(2)}) copy-start(bf16[1,1024,256]{1,2,0:T(8,128)(2,1)} %broadcast_select_fusion) | copy-start | bytes 1572868
  467.9 291.2 %copy-start.2 = (f32[1,256,256]{2,1,0:T(8,128)S(1)}, f32[1,256,256]{2,1,0:T(8,128)}, u32[]{:S(2)}) copy-start(f32[1,256,256]{2,1,0:T(8,128)} %param.7) | copy-start | bytes 786436
  467.9 291.2 %all-reduce.2.cloned.1.call-start = ((), (), s32[]{:S(2)}) async-start(), calls=%async_computation.4 | async-start | bytes 262144 | tf_op jit(solution)/shard_map/psum | solution.py:40
Sparse Core Ops, SparseCore 0:
  11.8 185.4 all-gather.1
  468.0 153.8 reduce-scatter.1
  625.3 133.7 all-reduce.1
where the time goes:
time: 769 us; the launch traced here: 767 us
  waiting for transfers between devices  473 us (62%)
  blocking collectives  101 us (13%)
  other arithmetic  90 us (12%)
  local copies, waits for them, and re-layouts  75.8 us (10%)
  between operations  13.8 us (2%)
  matrix products  12.7 us (2%)
    all_gather x1, waiting for transfers between devices, body(): panel_full = lax.all_gather(masked_local, 'prow', axis=1, tiled=True)  186 us
    reduce_scatter x1, waiting for transfers between devices, body(): lax.psum_scatter(partial_terms, 'pcol', scatter_dimension=0, tiled=True)  154 us
    psum x1, waiting for transfers between devices, body(): lax.psum(local_terms.astype(jnp.bfloat16), 'prow').astype(jnp.float32)  134 us
    all_to_all x1, blocking collectives, body(): lax.all_to_all(panel_full, 'pcol', split_axis=1, concat_axis=0, tiled=True)  101 us
    unnamed x1, other arithmetic  84.6 us
    unnamed x13, local copies, waits for them, and re-layouts  40.9 us
    all_gather x1, local copies, waits for them, and re-layouts, body(): panel_full = lax.all_gather(masked_local, 'prow', axis=1, tiled=True)  34.5 us
  transfers between devices with their start and end apart: 3, of which 3 were waited for; matrix products, arithmetic and copies ran while one was open for 0% of the time, Pallas kernels for 0%

commit v1 on v0

v1 whole, which is shorter than its diff:
```python
import functools

import jax
import jax.numpy as jnp
from jax import lax
from jax.experimental import pallas as pl
from jax.experimental.pallas import tpu as pltpu
from jax.sharding import PartitionSpec as P

BS = 128
NZ, NY_LO, NX, NY_HI, NCORE = 8, 2, 4, 2, 2
F32, BF16 = jnp.float32, jnp.bfloat16
AXES = ("prow", "pcol")


def device_index(z, ylo, x, yhi, core):
    return (2 * z + ylo) * 16 + 4 * x + 2 * yhi + core


def permutation(target):
    pairs = []
    for z in range(NZ):
        for ylo in range(NY_LO):
            for x in range(NX):
                for yhi in range(NY_HI):
                    for core in range(NCORE):
                        to = target(z, ylo, x, yhi, core)
                        if to is not None:
                            pairs.append((device_index(z, ylo, x, yhi, core), device_index(*to)))
    return pairs


L_TURN = permutation(lambda z, l, x, q, c: (2 * x + z % 2, c, z // 2, q, l))
Z_UP = permutation(lambda z, l, x, q, c: ((z + 1) % 8, l, x, q, c))
Z_DOWN = permutation(lambda z, l, x, q, c: ((z - 1) % 8, l, x, q, c))
Y_NEAR = permutation(lambda z, l, x, q, c: (z, 1 - l, x, q, c))
Y_FAR = permutation(lambda z, l, x, q, c: (z, 1 - l, x, 1 - q, c))
CORE = permutation(lambda z, l, x, q, c: (z, l, x, q, 1 - c))
X_UP = permutation(lambda z, l, x, q, c: (z, l, (x + 1) % 4, q, c))
X_DOWN = permutation(lambda z, l, x, q, c: (z, l, (x - 1) % 4, q, c))
HOME = permutation(lambda z, l, x, q, c: (z, c, x, q, l))


def z_swap(bit):
    return permutation(lambda z, l, x, q, c: (z ^ bit, l, x, q, c))


def move(value, pairs):
    return lax.ppermute(value, AXES, pairs)


def local_flags(ancestors, block_slot, row, column):
    own = lax.dynamic_index_in_dim(ancestors, column, 0, keepdims=False)
    numbers = jnp.arange(block_slot.shape[0], dtype=jnp.int32)
    used = jnp.any(own[:, None] == numbers[None, :], axis=0)
    slots = row * 8 + jnp.arange(8, dtype=jnp.int32)
    return jnp.any(used[None, :] & (block_slot[None, :] == slots[:, None]), axis=1)


def product_kernel(scalars, a0, a1, l0, l1, out):
    total = jnp.dot(a0[0], l0[0], preferred_element_type=F32)
    total += jnp.dot(a1[0], l1[0], preferred_element_type=F32)
    out[0] = total.astype(out.dtype)


def products(scalars, a_blocks, l_blocks, dtype):
    def l_map(flip):
        return lambda j, s: (2 * ((s[2] + j) % 4) + (s[1] ^ flip), 0, 0)

    return pl.pallas_call(
        product_kernel,
        grid_spec=pltpu.PrefetchScalarGridSpec(
            num_scalar_prefetch=1,
            grid=(4,),
            in_specs=[
                pl.BlockSpec((1, 1024, 1024), lambda j, s: (s[0], 0, 0)),
                pl.BlockSpec((1, 1024, 1024), lambda j, s: (s[0] + 1, 0, 0)),
                pl.BlockSpec((1, 1024, 256), l_map(0)),
                pl.BlockSpec((1, 1024, 256), l_map(1)),
            ],
            out_specs=pl.BlockSpec((1, 1024, 256), lambda j, s: (j, 0, 0)),
        ),
        out_shape=jax.ShapeDtypeStruct((4, 1024, 256), dtype),
        compiler_params=pltpu.CompilerParams(vmem_limit_bytes=40 * 2**20),
        cost_estimate=pl.CostEstimate(flops=2 * 1024 * 2048 * 1024, bytes_accessed=12 * 2**20, transcendentals=0),
    )(scalars, a_blocks, a_blocks, l_blocks, l_blocks)


def body(ainv, l_panels, dinv, ancestors, block_slot):
    row = lax.axis_index("prow")
    column = lax.axis_index("pcol")
    z, ylo = row // 2, row % 2
    x, yhi, core = column // 4, (column // 2) % 2, column % 2

    flags = jnp.repeat(local_flags(ancestors, block_slot, row, column), BS)[:, None]
    masked = jnp.where(flags, l_panels[0], jnp.zeros((), BF16))

    here = move(masked, L_TURN)
    near = move(ainv, Y_NEAR)
    far = move(ainv, Y_FAR)

    l_all = jnp.zeros((8, 1024, 256), BF16)
    put = lambda buffer, block, at, start=0: lax.dynamic_update_slice(buffer, block[None], (at, start, 0))
    l_all = put(l_all, here, z)
    up = down = here
    for step in range(1, 4):
        up, down = move(up, Z_UP), move(down, Z_DOWN)
        l_all = put(l_all, up, (z - step) % 8)
        l_all = put(l_all, down, (z + step) % 8)
    l_all = put(l_all, move(up[:512], Z_UP), (z + 4) % 8)
    l_all = put(l_all, move(down[512:], Z_DOWN), (z + 4) % 8, 512)

    across = jnp.concatenate([move(far[:512], Y_NEAR), move(near[512:], Y_FAR)], axis=0)
    a_all = jnp.stack([ainv, across, near, far])

    mine = (ylo != core).astype(jnp.int32)
    scalars = lambda which: jnp.stack([2 * which, yhi, x]).astype(jnp.int32)
    given = products(scalars(1 - mine), a_all, l_all, BF16)
    taken = move(given, CORE)
    kept = products(scalars(mine), a_all, l_all, F32)
    sums = [kept[j] + taken[j].astype(F32) for j in range(4)]

    first_up = move(sums[2][:512].astype(BF16), X_UP)
    first_down = move(sums[2][512:].astype(BF16), X_DOWN)
    one_up = jnp.concatenate([sums[1][:512] + first_up.astype(F32), sums[1][512:]], axis=0).astype(BF16)
    one_down = jnp.concatenate([sums[3][:512], sums[3][512:] + first_down.astype(F32)], axis=0).astype(BF16)
    total = sums[0] + move(one_up, X_UP).astype(F32) + move(one_down, X_DOWN).astype(F32)
    total = (-total).astype(BF16)
    total = jnp.where(ylo != core, move(total, HOME), total)
    inverse_column = jnp.where(flags, total, jnp.zeros((), BF16))

    terms = lax.dot_general(masked, inverse_column, (((0,), (0,)), ((), ())), preferred_element_type=F32)
    for pairs in (Y_NEAR, z_swap(1), z_swap(2), z_swap(4)):
        terms = terms.astype(BF16)
        terms = terms.astype(F32) + move(terms, pairs).astype(F32)
    return inverse_column[None], dinv - terms[None]


def solution(mesh):
    return jax.shard_map(
        body,
        mesh=mesh,
        in_specs=(P("prow", "pcol"), P("pcol", "prow", None), P("pcol", None, None), P(), P()),
        out_specs=(P("pcol", "prow", None), P("pcol", None, None)),
        check_vma=False,
    )
```

time: 769 us -> 205 us (0.27)
  waiting for transfers between devices: 473 us -> 115 us
  blocking collectives: 101 us -> 0 us
  other arithmetic: 90 us -> 13.4 us
  local copies, waits for them, and re-layouts: 75.8 us -> 8.75 us
  starting transfers between devices: 0.12 us -> 46.1 us
  Pallas kernels: 0 us -> 15.8 us
  between operations: 13.8 us -> 1.09 us
  matrix products: 12.7 us -> 0.7 us
    all_gather x1 -> x0, waiting for transfers between devices: 186 us -> none  [body(): panel_full = lax.all_gather(masked_local, 'prow', axis=1, tiled=True)]
    reduce_scatter x1 -> x0, waiting for transfers between devices: 154 us -> none  [body(): lax.psum_scatter(partial_terms, 'pcol', scatter_dimension=0, tiled=True)]
    psum x1 -> x0, waiting for transfers between devices: 134 us -> none  [body(): lax.psum(local_terms.astype(jnp.bfloat16), 'prow').astype(jnp.float32)]
    ppermute x0 -> x23, waiting for transfers between devices: none -> 115 us  [move(): return lax.ppermute(value, AXES, pairs)]
    all_to_all x1 -> x0, blocking collectives: 101 us -> none  [body(): lax.all_to_all(panel_full, 'pcol', split_axis=1, concat_axis=0, tiled=True)]
    unnamed x1 -> x0, other arithmetic: 84.6 us -> none
    ppermute x0 -> x23, starting transfers between devices: none -> 46.1 us  [move(): return lax.ppermute(value, AXES, pairs)]
    unnamed x13 -> x16, local copies, waits for them, and re-layouts: 40.9 us -> 2.9 us
  transfers between devices with their start and end apart: 3 -> 23, of which waited for: 3 -> 14; matrix products, arithmetic and copies ran while one was open for 0% -> 4% of each run, Pallas kernels for 0% -> 4%
where the time goes in v1:
time: 205 us; the launch traced here: 201 us
  waiting for transfers between devices  115 us (56%)
  starting transfers between devices  46.1 us (22%)
  Pallas kernels  15.8 us (8%)
  other arithmetic  13.4 us (7%)
  local copies, waits for them, and re-layouts  8.75 us (4%)
    ppermute x23, waiting for transfers between devices, move(): return lax.ppermute(value, AXES, pairs)  115 us
    ppermute x23, starting transfers between devices, move(): return lax.ppermute(value, AXES, pairs)  46.1 us
    pallas_call x2, Pallas kernels, products(): pl.pallas_call(product_kernel, grid_spec=pltpu.PrefetchScalarGridSpec(num...  15.8 us
    another operation x2, other arithmetic, body(): a_all = jnp.stack([ainv, across, near, far])  5.92 us
  transfers between devices with their start and end apart: 23, of which 14 were waited for; matrix products, arithmetic and copies ran while one was open for 4% of the time, Pallas kernels for 4%

profile of v1, /device:TPU:2, one launch (start us, length us, event | category | flops | bytes accessed | tf_op | source)
XLA Modules:
  0.0 200.9 jit_solution(5303314352671196023)
XLA Ops:
  2.4 1.2 bitcast_select_fusion
  3.6 5.2 %collective-permute-start.4 = (bf16[1024,256]{1,0:T(8,128)(2,1)S(1)}, bf16[1024,256]{1,0:T(8,128)(2,1)S(1)}, u32[]{:S(2)}, u32[]{:S(2)}) collective-permute-start(bf16[1024,256]{1,0:T(8,128)(2,1)S(1)} %bitcast_select_fusion), channel_id=1, source_target_pairs={{0,0},{1,16},{2,2},{3,18},{4,64},{5,80},{6,66},{7,82},{8,128},{9,1... | collective-permute-start | bytes 1572872 | tf_op jit(solution)/shard_map/ppermute | solution.py:49
  9.8 2.9 %collective-permute-start = (bf16[1024,1024]{1,0:T(8,128)(2,1)}, bf16[1024,1024]{1,0:T(8,128)(2,1)}, u32[]{:S(2)}, u32[]{:S(2)}) collective-permute-start(bf16[1024,1024]{1,0:T(8,128)(2,1)} %param.5), channel_id=1, source_target_pairs={{0,18},{1,19},{2,16},{3,17},{4,22},{5,23},{6,20},{7,21},{8,26},{9,... | collective-permute-start | bytes 6291464 | tf_op jit(solution)/shard_map/ppermute | solution.py:49
  12.6 31.6 %collective-permute-done.4 = bf16[1024,256]{1,0:T(8,128)(2,1)S(1)} collective-permute-done((bf16[1024,256]{1,0:T(8,128)(2,1)S(1)}, bf16[1024,256]{1,0:T(8,128)(2,1)S(1)}, u32[]{:S(2)}, u32[]{:S(2)}) %collective-permute-start.4) | collective-permute-done | bytes 524320 | tf_op jit(solution)/shard_map/ppermute | solution.py:49
  45.0 2.5 %collective-permute-start.6 = (bf16[1024,256]{1,0:T(8,128)(2,1)S(1)}, bf16[1024,256]{1,0:T(8,128)(2,1)S(1)}, u32[]{:S(2)}, u32[]{:S(2)}) collective-permute-start(bf16[1024,256]{1,0:T(8,128)(2,1)S(1)} %collective-permute-done.4), channel_id=1, source_target_pairs={{0,224},{1,225},{2,226},{3,227},{4,228},{5,229},{6,230},{7,231},{8... | collective-permute-start | bytes 1572872 | tf_op jit(solution)/shard_map/ppermute | solution.py:49
  47.4 12.1 %collective-permute-done.5 = bf16[1024,256]{1,0:T(8,128)(2,1)} collective-permute-done((bf16[1024,256]{1,0:T(8,128)(2,1)S(1)}, bf16[1024,256]{1,0:T(8,128)(2,1)}, u32[]{:S(2)}, u32[]{:S(2)}) %collective-permute-start.5) | collective-permute-done | bytes 524320 | tf_op jit(solution)/shard_map/ppermute | solution.py:49
  59.5 3.2 %collective-permute-start.8 = (bf16[1024,256]{1,0:T(8,128)(2,1)S(1)}, bf16[1024,256]{1,0:T(8,128)(2,1)}, u32[]{:S(2)}, u32[]{:S(2)}) collective-permute-start(bf16[1024,256]{1,0:T(8,128)(2,1)S(1)} %collective-permute-done.6), channel_id=1, source_target_pairs={{0,224},{1,225},{2,226},{3,227},{4,228},{5,229},{6,230},{7,231},{8... | collective-permute-start | bytes 1572872 | tf_op jit(solution)/shard_map/ppermute | solution.py:49
  64.3 9.9 %collective-permute-done.7 = bf16[1024,256]{1,0:T(8,128)(2,1)} collective-permute-done((bf16[1024,256]{1,0:T(8,128)(2,1)}, bf16[1024,256]{1,0:T(8,128)(2,1)}, u32[]{:S(2)}, u32[]{:S(2)}) %collective-permute-start.7) | collective-permute-done | bytes 524320 | tf_op jit(solution)/shard_map/ppermute | solution.py:49
  74.2 3.5 %collective-permute-start.10 = (bf16[1024,256]{1,0:T(8,128)(2,1)}, bf16[1024,256]{1,0:T(8,128)(2,1)S(1)}, u32[]{:S(2)}, u32[]{:S(2)}) collective-permute-start(bf16[1024,256]{1,0:T(8,128)(2,1)} %collective-permute-done.8), channel_id=1, source_target_pairs={{0,224},{1,225},{2,226},{3,227},{4,228},{5,229},{6,230},{7,231},{8... | collective-permute-start | bytes 1572872 | tf_op jit(solution)/shard_map/ppermute | solution.py:49
  79.1 1.9 slice.94
  80.9 1.7 collective-permute-start.1
  83.7 5.4 %collective-permute-done.9 = bf16[1024,256]{1,0:T(8,128)(2,1)S(1)} collective-permute-done((bf16[1024,256]{1,0:T(8,128)(2,1)}, bf16[1024,256]{1,0:T(8,128)(2,1)S(1)}, u32[]{:S(2)}, u32[]{:S(2)}) %collective-permute-start.9) | collective-permute-done | bytes 524320 | tf_op jit(solution)/shard_map/ppermute | solution.py:49
  89.2 3.3 %collective-permute-start.12 = (bf16[512,256]{1,0:T(8,128)(2,1)S(1)}, bf16[512,256]{1,0:T(8,128)(2,1)S(1)}, u32[]{:S(2)}, u32[]{:S(2)}) collective-permute-start(bf16[512,256]{1,0:T(8,128)(2,1)S(1)} %slice.97), channel_id=1, source_target_pairs={{0,224},{1,225},{2,226},{3,227},{4,228},{5,229},{6,230},{7,231},{8... | collective-permute-start | bytes 786440 | tf_op jit(solution)/shard_map/ppermute | solution.py:49
  92.6 4.4 %collective-permute-done.11 = bf16[512,256]{1,0:T(8,128)(2,1)S(1)} collective-permute-done((bf16[512,256]{1,0:T(8,128)(2,1)S(1)}, bf16[512,256]{1,0:T(8,128)(2,1)S(1)}, u32[]{:S(2)}, u32[]{:S(2)}) %collective-permute-start.11) | collective-permute-done | bytes 262176 | tf_op jit(solution)/shard_map/ppermute | solution.py:49
  97.1 7.0 %collective-permute-done.3 = bf16[512,1024]{1,0:T(8,128)(2,1)S(1)} collective-permute-done((bf16[512,1024]{1,0:T(8,128)(2,1)S(1)}, bf16[512,1024]{1,0:T(8,128)(2,1)S(1)}, u32[]{:S(2)}, u32[]{:S(2)}) %collective-permute-start.3) | collective-permute-done | bytes 1048608 | tf_op jit(solution)/shard_map/ppermute | solution.py:49
  105.1 5.7 %pad_maximum_fusion.a0.a1 = bf16[4,1024,1024]{2,1,0:T(8,128)(2,1)} fusion(bf16[1,1024,1024]{2,1,0:T(8,128)(2,1)} %bitcast.8, bf16[1,1024,1024]{2,1,0:T(8,128)(2,1)S(1)} %bitcast.68, bf16[1,1024,1024]{2,1,0:T(8,128)(2,1)S(1)} %maximum_bitcast_fusion, bf16[1,1024,1024]{2,1,0:T(8,128)(2,1)S(1)} %bitcast.69), kind=kLoop, calls=%fused_computation | loop fusion | flops 12582912 | bytes 16777216 | tf_op jit(solution)/shard_map/stack | solution.py:114
  110.8 7.9 %shard_map.69 = bf16[4,1024,256]{2,1,0:T(8,128)(2,1)S(1)} custom-call(s32[3]{0:T(128)S(1)} %add_add_fusion.1.scalars, bf16[4,1024,1024]{2,1,0:T(8,128)(2,1)} %pad_maximum_fusion.a0.a1, bf16[4,1024,1024]{2,1,0:T(8,128)(2,1)} %pad_maximum_fusion.a0.a1, bf16[8,1024,256]{2,1,0:T(8,128)(2,1)S(1)} %bitcast_dynamic-update-slice_fusion.7.l0.l1, ...), custom_call_target="tpu_custom_call" | custom-call | flops 4294967296 | bytes 12582912 | tf_op jit(solution)/shard_map/pallas_call | solution.py:70
  119.1 2.2 %copy-done.2 = bf16[8,1024,256]{2,1,0:T(8,128)(2,1)S(1)} copy-done((bf16[8,1024,256]{2,1,0:T(8,128)(2,1)S(1)}, bf16[8,1024,256]{2,1,0:T(8,128)(2,1)}, u32[]{:S(2)}) %copy-start.2) | copy-done | bytes 4194328
  121.3 7.9 %shard_map.68 = f32[4,1024,256]{2,1,0:T(8,128)S(1)} custom-call(s32[3]{0:T(128)S(1)} %add_add_fusion.scalars, bf16[4,1024,1024]{2,1,0:T(8,128)(2,1)} %pad_maximum_fusion.a0.a1, bf16[4,1024,1024]{2,1,0:T(8,128)(2,1)} %pad_maximum_fusion.a0.a1, bf16[8,1024,256]{2,1,0:T(8,128)(2,1)S(1)} %copy-done.2, bf16[8,1024,256]{2,1,0:T(8,128)(2,1)S(1)} %copy-done.2), custom_call_target="tpu_custom_call" | custom-call | flops 4294967296 | bytes 12582912 | tf_op jit(solution)/shard_map/pallas_call | solution.py:70
  129.2 1.8 slice_add_fusion.2
  131.0 3.8 %collective-permute-start.16 = (bf16[512,256]{1,0:T(8,128)(2,1)S(1)}, bf16[512,256]{1,0:T(8,128)(2,1)S(1)}, u32[]{:S(2)}, u32[]{:S(2)}) collective-permute-start(bf16[512,256]{1,0:T(8,128)(2,1)S(1)} %get-tuple-element.6), channel_id=1, source_target_pairs={{0,12},{1,13},{2,14},{3,15},{4,0},{5,1},{6,2},{7,3},{8,4},{9,5},{1... | collective-permute-start | bytes 786440 | tf_op jit(solution)/shard_map/ppermute | solution.py:49
  135.1 6.8 %collective-permute-done.16 = bf16[512,256]{1,0:T(8,128)(2,1)S(1)} collective-permute-done((bf16[512,256]{1,0:T(8,128)(2,1)S(1)}, bf16[512,256]{1,0:T(8,128)(2,1)S(1)}, u32[]{:S(2)}, u32[]{:S(2)}) %collective-permute-start.16) | collective-permute-done | bytes 262176 | tf_op jit(solution)/shard_map/ppermute | solution.py:49
  142.0 1.7 collective-permute-start.17
  144.3 11.5 %collective-permute-done.17 = bf16[1024,256]{1,0:T(8,128)(2,1)S(1)} collective-permute-done((bf16[1024,256]{1,0:T(8,128)(2,1)S(1)}, bf16[1024,256]{1,0:T(8,128)(2,1)S(1)}, u32[]{:S(2)}, u32[]{:S(2)}) %collective-permute-start.17) | collective-permute-done | bytes 524320 | tf_op jit(solution)/shard_map/ppermute | solution.py:49
  155.8 2.4 %collective-permute-done.15 = bf16[1024,256]{1,0:T(8,128)(2,1)S(1)} collective-permute-done((bf16[1024,256]{1,0:T(8,128)(2,1)S(1)}, bf16[1024,256]{1,0:T(8,128)(2,1)S(1)}, u32[]{:S(2)}, u32[]{:S(2)}) %collective-permute-start.15) | collective-permute-done | bytes 524320 | tf_op jit(solution)/shard_map/ppermute | solution.py:49
  158.3 1.4 fusion.5
  161.0 11.6 %collective-permute-start.19 = (bf16[256,256]{1,0:T(8,128)(2,1)S(1)}, bf16[256,256]{1,0:T(8,128)(2,1)S(1)}, u32[]{:S(2)}, u32[]{:S(2)}) collective-permute-start(bf16[256,256]{1,0:T(8,128)(2,1)S(1)} %convolution_convert_fusion), channel_id=1, source_target_pairs={{0,16},{1,17},{2,18},{3,19},{4,20},{5,21},{6,22},{7,23},{8,24},{9,... | collective-permute-start | bytes 393224 | tf_op jit(solution)/shard_map/ppermute | solution.py:49
  172.6 3.8 %collective-permute-done.19 = bf16[256,256]{1,0:T(8,128)(2,1)S(1)} collective-permute-done((bf16[256,256]{1,0:T(8,128)(2,1)S(1)}, bf16[256,256]{1,0:T(8,128)(2,1)S(1)}, u32[]{:S(2)}, u32[]{:S(2)}) %collective-permute-start.19) | collective-permute-done | bytes 131104 | tf_op jit(solution)/shard_map/ppermute | solution.py:49
  176.6 5.0 %collective-permute-done.20 = bf16[256,256]{1,0:T(8,128)(2,1)S(1)} collective-permute-done((bf16[256,256]{1,0:T(8,128)(2,1)S(1)}, bf16[256,256]{1,0:T(8,128)(2,1)S(1)}, u32[]{:S(2)}, u32[]{:S(2)}) %collective-permute-start.20) | collective-permute-done | bytes 131104 | tf_op jit(solution)/shard_map/ppermute | solution.py:49
  181.7 7.5 %collective-permute-done.21 = bf16[256,256]{1,0:T(8,128)(2,1)S(1)} collective-permute-done((bf16[256,256]{1,0:T(8,128)(2,1)S(1)}, bf16[256,256]{1,0:T(8,128)(2,1)S(1)}, u32[]{:S(2)}, u32[]{:S(2)}) %collective-permute-start.21) | collective-permute-done | bytes 131104 | tf_op jit(solution)/shard_map/ppermute | solution.py:49
  189.2 3.0 %collective-permute-start.22 = (bf16[256,256]{1,0:T(8,128)(2,1)S(1)}, bf16[256,256]{1,0:T(8,128)(2,1)S(1)}, u32[]{:S(2)}, u32[]{:S(2)}) collective-permute-start(bf16[256,256]{1,0:T(8,128)(2,1)S(1)} %add_convert_fusion), channel_id=1, source_target_pairs={{0,128},{1,129},{2,130},{3,131},{4,132},{5,133},{6,134},{7,135},{8... | collective-permute-start | bytes 393224 | tf_op jit(solution)/shard_map/ppermute | solution.py:49
  193.2 6.9 %collective-permute-done.22 = bf16[256,256]{1,0:T(8,128)(2,1)S(1)} collective-permute-done((bf16[256,256]{1,0:T(8,128)(2,1)S(1)}, bf16[256,256]{1,0:T(8,128)(2,1)S(1)}, u32[]{:S(2)}, u32[]{:S(2)}) %collective-permute-start.22) | collective-permute-done | bytes 131104 | tf_op jit(solution)/shard_map/ppermute | solution.py:49
  (71 shorter events, 13.3 us)
Async XLA Ops:
  0.6 0.7 copy-start
  3.6 40.6 %collective-permute-start.4 = (bf16[1024,256]{1,0:T(8,128)(2,1)S(1)}, bf16[1024,256]{1,0:T(8,128)(2,1)S(1)}, u32[]{:S(2)}, u32[]{:S(2)}) collective-permute-start(bf16[1024,256]{1,0:T(8,128)(2,1)S(1)} %bitcast_select_fusion), channel_id=1, source_target_pairs={{0,0},{1,16},{2,2},{3,18},{4,64},{5,80},{6,66},{7,82},{8,128},{9,1... | collective-permute-start | bytes 1572872 | tf_op jit(solution)/shard_map/ppermute | solution.py:49
  8.8 70.1 %collective-permute-start.2 = (bf16[1024,1024]{1,0:T(8,128)(2,1)}, bf16[1024,1024]{1,0:T(8,128)(2,1)S(1)}, u32[]{:S(2)}, u32[]{:S(2)}) collective-permute-start(bf16[1024,1024]{1,0:T(8,128)(2,1)} %param.5), channel_id=1, source_target_pairs={{0,16},{1,17},{2,18},{3,19},{4,20},{5,21},{6,22},{7,23},{8,24},{9,... | collective-permute-start | bytes 6291464 | tf_op jit(solution)/shard_map/ppermute | solution.py:49
  9.8 69.3 %collective-permute-start = (bf16[1024,1024]{1,0:T(8,128)(2,1)}, bf16[1024,1024]{1,0:T(8,128)(2,1)}, u32[]{:S(2)}, u32[]{:S(2)}) collective-permute-start(bf16[1024,1024]{1,0:T(8,128)(2,1)} %param.5), channel_id=1, source_target_pairs={{0,18},{1,19},{2,16},{3,17},{4,22},{5,23},{6,20},{7,21},{8,26},{9,... | collective-permute-start | bytes 6291464 | tf_op jit(solution)/shard_map/ppermute | solution.py:49
  44.2 15.3 %collective-permute-start.5 = (bf16[1024,256]{1,0:T(8,128)(2,1)S(1)}, bf16[1024,256]{1,0:T(8,128)(2,1)}, u32[]{:S(2)}, u32[]{:S(2)}) collective-permute-start(bf16[1024,256]{1,0:T(8,128)(2,1)S(1)} %collective-permute-done.4), channel_id=1, source_target_pairs={{0,32},{1,33},{2,34},{3,35},{4,36},{5,37},{6,38},{7,39},{8,40},{9,... | collective-permute-start | bytes 1572872 | tf_op jit(solution)/shard_map/ppermute | solution.py:49
  45.0 14.6 %collective-permute-start.6 = (bf16[1024,256]{1,0:T(8,128)(2,1)S(1)}, bf16[1024,256]{1,0:T(8,128)(2,1)S(1)}, u32[]{:S(2)}, u32[]{:S(2)}) collective-permute-start(bf16[1024,256]{1,0:T(8,128)(2,1)S(1)} %collective-permute-done.4), channel_id=1, source_target_pairs={{0,224},{1,225},{2,226},{3,227},{4,228},{5,229},{6,230},{7,231},{8... | collective-permute-start | bytes 1572872 | tf_op jit(solution)/shard_map/ppermute | solution.py:49
  59.5 14.7 %collective-permute-start.7 = (bf16[1024,256]{1,0:T(8,128)(2,1)}, bf16[1024,256]{1,0:T(8,128)(2,1)}, u32[]{:S(2)}, u32[]{:S(2)}) collective-permute-start(bf16[1024,256]{1,0:T(8,128)(2,1)} %collective-permute-done.5), channel_id=1, source_target_pairs={{0,32},{1,33},{2,34},{3,35},{4,36},{5,37},{6,38},{7,39},{8,40},{9,... | collective-permute-start | bytes 1572872 | tf_op jit(solution)/shard_map/ppermute | solution.py:49
  59.5 14.7 %collective-permute-start.8 = (bf16[1024,256]{1,0:T(8,128)(2,1)S(1)}, bf16[1024,256]{1,0:T(8,128)(2,1)}, u32[]{:S(2)}, u32[]{:S(2)}) collective-permute-start(bf16[1024,256]{1,0:T(8,128)(2,1)S(1)} %collective-permute-done.6), channel_id=1, source_target_pairs={{0,224},{1,225},{2,226},{3,227},{4,228},{5,229},{6,230},{7,231},{8... | collective-permute-start | bytes 1572872 | tf_op jit(solution)/shard_map/ppermute | solution.py:49
  74.2 14.9 %collective-permute-start.9 = (bf16[1024,256]{1,0:T(8,128)(2,1)}, bf16[1024,256]{1,0:T(8,128)(2,1)S(1)}, u32[]{:S(2)}, u32[]{:S(2)}) collective-permute-start(bf16[1024,256]{1,0:T(8,128)(2,1)} %collective-permute-done.7), channel_id=1, source_target_pairs={{0,32},{1,33},{2,34},{3,35},{4,36},{5,37},{6,38},{7,39},{8,40},{9,... | collective-permute-start | bytes 1572872 | tf_op jit(solution)/shard_map/ppermute | solution.py:49
  74.2 15.0 %collective-permute-start.10 = (bf16[1024,256]{1,0:T(8,128)(2,1)}, bf16[1024,256]{1,0:T(8,128)(2,1)S(1)}, u32[]{:S(2)}, u32[]{:S(2)}) collective-permute-start(bf16[1024,256]{1,0:T(8,128)(2,1)} %collective-permute-done.8), channel_id=1, source_target_pairs={{0,224},{1,225},{2,226},{3,227},{4,228},{5,229},{6,230},{7,231},{8... | collective-permute-start | bytes 1572872 | tf_op jit(solution)/shard_map/ppermute | solution.py:49
  78.9 13.8 %copy-start.3 = (bf16[1024,1024]{1,0:T(8,128)(2,1)}, bf16[1024,1024]{1,0:T(8,128)(2,1)S(1)}, u32[]{:S(2)}) copy-start(bf16[1024,1024]{1,0:T(8,128)(2,1)S(1)} %collective-permute-done.2) | copy-start | bytes 6291460
  78.9 25.2 %collective-permute-start.3 = (bf16[512,1024]{1,0:T(8,128)(2,1)S(1)}, bf16[512,1024]{1,0:T(8,128)(2,1)S(1)}, u32[]{:S(2)}, u32[]{:S(2)}) collective-permute-start(bf16[512,1024]{1,0:T(8,128)(2,1)S(1)} %slice.95), channel_id=1, source_target_pairs={{0,18},{1,19},{2,16},{3,17},{4,22},{5,23},{6,20},{7,21},{8,26},{9,... | collective-permute-start | bytes 3145736 | tf_op jit(solution)/shard_map/ppermute | solution.py:49
  80.9 24.0 %collective-permute-start.1 = (bf16[512,1024]{1,0:T(8,128)(2,1)S(1)}, bf16[512,1024]{1,0:T(8,128)(2,1)S(1)}, u32[]{:S(2)}, u32[]{:S(2)}) collective-permute-start(bf16[512,1024]{1,0:T(8,128)(2,1)S(1)} %slice.94), channel_id=1, source_target_pairs={{0,16},{1,17},{2,18},{3,19},{4,20},{5,21},{6,22},{7,23},{8,24},{9,... | collective-permute-start | bytes 3145736 | tf_op jit(solution)/shard_map/ppermute | solution.py:49
  83.7 21.4 %copy-start.5 = (bf16[1024,1024]{1,0:T(8,128)(2,1)S(1)}, bf16[1024,1024]{1,0:T(8,128)(2,1)}, u32[]{:S(2)}) copy-start(bf16[1024,1024]{1,0:T(8,128)(2,1)} %param.5) | copy-start | bytes 6291460
  89.1 7.9 %collective-permute-start.11 = (bf16[512,256]{1,0:T(8,128)(2,1)S(1)}, bf16[512,256]{1,0:T(8,128)(2,1)S(1)}, u32[]{:S(2)}, u32[]{:S(2)}) collective-permute-start(bf16[512,256]{1,0:T(8,128)(2,1)S(1)} %slice.96), channel_id=1, source_target_pairs={{0,32},{1,33},{2,34},{3,35},{4,36},{5,37},{6,38},{7,39},{8,40},{9,... | collective-permute-start | bytes 786440 | tf_op jit(solution)/shard_map/ppermute | solution.py:49
  89.2 7.8 %collective-permute-start.12 = (bf16[512,256]{1,0:T(8,128)(2,1)S(1)}, bf16[512,256]{1,0:T(8,128)(2,1)S(1)}, u32[]{:S(2)}, u32[]{:S(2)}) collective-permute-start(bf16[512,256]{1,0:T(8,128)(2,1)S(1)} %slice.97), channel_id=1, source_target_pairs={{0,224},{1,225},{2,226},{3,227},{4,228},{5,229},{6,230},{7,231},{8... | collective-permute-start | bytes 786440 | tf_op jit(solution)/shard_map/ppermute | solution.py:49
  97.1 8.0 %copy-start.4 = (bf16[1024,1024]{1,0:T(8,128)(2,1)S(1)}, bf16[1024,1024]{1,0:T(8,128)(2,1)}, u32[]{:S(2)}) copy-start(bf16[1024,1024]{1,0:T(8,128)(2,1)} %copy-done.3) | copy-start | bytes 6291460
  97.1 13.7 %copy-start.1 = (bf16[8,1024,256]{2,1,0:T(8,128)(2,1)}, bf16[8,1024,256]{2,1,0:T(8,128)(2,1)S(1)}, u32[]{:S(2)}) copy-start(bf16[8,1024,256]{2,1,0:T(8,128)(2,1)S(1)} %bitcast_dynamic-update-slice_fusion.7.l0.l1) | copy-start | bytes 12582916
  118.7 10.5 %collective-permute-start.13 = (bf16[4,1024,256]{2,1,0:T(8,128)(2,1)S(1)}, bf16[4,1024,256]{2,1,0:T(8,128)(2,1)}, u32[]{:S(2)}, u32[]{:S(2)}) collective-permute-start(bf16[4,1024,256]{2,1,0:T(8,128)(2,1)S(1)} %shard_map.69), channel_id=1, source_target_pairs={{0,1},{1,0},{2,3},{3,2},{4,5},{5,4},{6,7},{7,6},{8,9},{9,8},{10,11... | collective-permute-start | bytes 6291464 | tf_op jit(solution)/shard_map/ppermute | solution.py:49
  119.1 2.2 %copy-start.2 = (bf16[8,1024,256]{2,1,0:T(8,128)(2,1)S(1)}, bf16[8,1024,256]{2,1,0:T(8,128)(2,1)}, u32[]{:S(2)}) copy-start(bf16[8,1024,256]{2,1,0:T(8,128)(2,1)} %copy-done.1) | copy-start | bytes 12582916
  131.0 10.9 %collective-permute-start.16 = (bf16[512,256]{1,0:T(8,128)(2,1)S(1)}, bf16[512,256]{1,0:T(8,128)(2,1)S(1)}, u32[]{:S(2)}, u32[]{:S(2)}) collective-permute-start(bf16[512,256]{1,0:T(8,128)(2,1)S(1)} %get-tuple-element.6), channel_id=1, source_target_pairs={{0,12},{1,13},{2,14},{3,15},{4,0},{5,1},{6,2},{7,3},{8,4},{9,5},{1... | collective-permute-start | bytes 786440 | tf_op jit(solution)/shard_map/ppermute | solution.py:49
  134.8 25.5 %copy-start.6 = (bf16[1,1024,256]{2,1,0:T(8,128)(2,1)S(1)}, bf16[1,1024,256]{2,1,0:T(8,128)(2,1)}, u32[]{:S(2)}) copy-start(bf16[1,1024,256]{2,1,0:T(8,128)(2,1)} %param.6) | copy-start | bytes 1572868
  134.8 8.9 %collective-permute-start.14 = (bf16[512,256]{1,0:T(8,128)(2,1)S(1)}, bf16[512,256]{1,0:T(8,128)(2,1)S(1)}, u32[]{:S(2)}, u32[]{:S(2)}) collective-permute-start(bf16[512,256]{1,0:T(8,128)(2,1)S(1)} %get-tuple-element.5), channel_id=1, source_target_pairs={{0,4},{1,5},{2,6},{3,7},{4,8},{5,9},{6,10},{7,11},{8,12},{9,13},{1... | collective-permute-start | bytes 786440 | tf_op jit(solution)/shard_map/ppermute | solution.py:49
  142.0 13.8 %collective-permute-start.17 = (bf16[1024,256]{1,0:T(8,128)(2,1)S(1)}, bf16[1024,256]{1,0:T(8,128)(2,1)S(1)}, u32[]{:S(2)}, u32[]{:S(2)}) collective-permute-start(bf16[1024,256]{1,0:T(8,128)(2,1)S(1)} %pad_maximum_fusion.2), channel_id=1, source_target_pairs={{0,12},{1,13},{2,14},{3,15},{4,0},{5,1},{6,2},{7,3},{8,4},{9,5},{1... | collective-permute-start | bytes 1572872 | tf_op jit(solution)/shard_map/ppermute | solution.py:49
  143.8 56.3 %copy-start.7 = (f32[1,256,256]{2,1,0:T(8,128)S(1)}, f32[1,256,256]{2,1,0:T(8,128)}, u32[]{:S(2)}) copy-start(f32[1,256,256]{2,1,0:T(8,128)} %param.7) | copy-start | bytes 786436
  143.8 14.4 %collective-permute-start.15 = (bf16[1024,256]{1,0:T(8,128)(2,1)S(1)}, bf16[1024,256]{1,0:T(8,128)(2,1)S(1)}, u32[]{:S(2)}, u32[]{:S(2)}) collective-permute-start(bf16[1024,256]{1,0:T(8,128)(2,1)S(1)} %pad_maximum_fusion.1), channel_id=1, source_target_pairs={{0,4},{1,5},{2,6},{3,7},{4,8},{5,9},{6,10},{7,11},{8,12},{9,13},{1... | collective-permute-start | bytes 1572872 | tf_op jit(solution)/shard_map/ppermute | solution.py:49
  159.6 0.7 collective-permute-start.18
  161.0 15.4 %collective-permute-start.19 = (bf16[256,256]{1,0:T(8,128)(2,1)S(1)}, bf16[256,256]{1,0:T(8,128)(2,1)S(1)}, u32[]{:S(2)}, u32[]{:S(2)}) collective-permute-start(bf16[256,256]{1,0:T(8,128)(2,1)S(1)} %convolution_convert_fusion), channel_id=1, source_target_pairs={{0,16},{1,17},{2,18},{3,19},{4,20},{5,21},{6,22},{7,23},{8,24},{9,... | collective-permute-start | bytes 393224 | tf_op jit(solution)/shard_map/ppermute | solution.py:49
  176.5 5.1 %collective-permute-start.20 = (bf16[256,256]{1,0:T(8,128)(2,1)S(1)}, bf16[256,256]{1,0:T(8,128)(2,1)S(1)}, u32[]{:S(2)}, u32[]{:S(2)}) collective-permute-start(bf16[256,256]{1,0:T(8,128)(2,1)S(1)} %add_convert_fusion.2), channel_id=1, source_target_pairs={{0,32},{1,33},{2,34},{3,35},{4,36},{5,37},{6,38},{7,39},{8,40},{9,... | collective-permute-start | bytes 393224 | tf_op jit(solution)/shard_map/ppermute | solution.py:49
  181.6 7.6 %collective-permute-start.21 = (bf16[256,256]{1,0:T(8,128)(2,1)S(1)}, bf16[256,256]{1,0:T(8,128)(2,1)S(1)}, u32[]{:S(2)}, u32[]{:S(2)}) collective-permute-start(bf16[256,256]{1,0:T(8,128)(2,1)S(1)} %add_convert_fusion.1), channel_id=1, source_target_pairs={{0,64},{1,65},{2,66},{3,67},{4,68},{5,69},{6,70},{7,71},{8,72},{9,... | collective-permute-start | bytes 393224 | tf_op jit(solution)/shard_map/ppermute | solution.py:49
  189.2 10.9 %collective-permute-start.22 = (bf16[256,256]{1,0:T(8,128)(2,1)S(1)}, bf16[256,256]{1,0:T(8,128)(2,1)S(1)}, u32[]{:S(2)}, u32[]{:S(2)}) collective-permute-start(bf16[256,256]{1,0:T(8,128)(2,1)S(1)} %add_convert_fusion), channel_id=1, source_target_pairs={{0,128},{1,129},{2,130},{3,131},{4,132},{5,133},{6,134},{7,135},{8... | collective-permute-start | bytes 393224 | tf_op jit(solution)/shard_map/ppermute | solution.py:49

commit v2 on v1

v2 whole, which is shorter than its diff:
```python
import jax
import jax.numpy as jnp
from jax import lax
from jax.experimental import pallas as pl
from jax.experimental.pallas import tpu as pltpu
from jax.sharding import PartitionSpec as P

BS = 128
VMEM_MIB = 56
NZ, NY_LO, NX, NY_HI, NCORE = 8, 2, 4, 2, 2
F32, BF16 = jnp.float32, jnp.bfloat16
AXES = ("prow", "pcol")


def device_index(z, ylo, x, yhi, core):
    return (2 * z + ylo) * 16 + 4 * x + 2 * yhi + core


def permutation(target):
    pairs = []
    for z in range(NZ):
        for ylo in range(NY_LO):
            for x in range(NX):
                for yhi in range(NY_HI):
                    for core in range(NCORE):
                        to = target(z, ylo, x, yhi, core)
                        if to is not None:
                            pairs.append((device_index(z, ylo, x, yhi, core), device_index(*to)))
    return pairs


L_TURN = permutation(lambda z, l, x, q, c: (2 * ((x - z // 2) % 4) + z % 2, l, z // 2, q, c))
Z_UP = permutation(lambda z, l, x, q, c: ((z + 1) % 8, l, x, q, c))
Z_DOWN = permutation(lambda z, l, x, q, c: ((z - 1) % 8, l, x, q, c))
Y_NEAR = permutation(lambda z, l, x, q, c: (z, 1 - l, x, q, c))
Y_FAR = permutation(lambda z, l, x, q, c: (z, 1 - l, x, 1 - q, c))
CORE = permutation(lambda z, l, x, q, c: (z, l, x, q, 1 - c))
X_HOME = [permutation(lambda z, l, x, q, c, j=j: (z, c, (x + j) % 4, q, l)) for j in range(4)]


def swap(z_bits, ylo_bit):
    return permutation(lambda z, l, x, q, c: (z ^ z_bits, l ^ ylo_bit, x, q, c))


def move(value, pairs):
    return lax.ppermute(value, AXES, pairs)


def local_flags(ancestors, block_slot, row, column):
    own = lax.dynamic_index_in_dim(ancestors, column, 0, keepdims=False)
    numbers = jnp.arange(block_slot.shape[0], dtype=jnp.int32)
    used = jnp.any(own[:, None] == numbers[None, :], axis=0)
    slots = row * 8 + jnp.arange(8, dtype=jnp.int32)
    return jnp.any(used[None, :] & (block_slot[None, :] == slots[:, None]), axis=1)


L_STEPS = (0, -1, 1, -2, 2, -3, 3, 4, 4)


def product_kernel(scalars, *refs):
    own, across, near, far, l_refs, out = refs[0], refs[1:3], refs[3], refs[4], refs[5:14], refs[14]
    a_vmem, l_vmem, out_vmem, a_sem, l_sem, out_sem = refs[15:]
    z, yhi, which = scalars[0], scalars[1], scalars[2]

    def a_start(tile):
        rows = pl.ds(256 * tile, 256)
        sources = (
            (own.at[rows], across[tile // 2].at[pl.ds(256 * (tile % 2), 256)]),
            (near.at[rows], far.at[rows]),
        )
        for choice in range(2):
            @pl.when(which == choice)
            def _():
                for at in range(2):
                    target = a_vmem.at[rows, pl.ds(1024 * at, 1024)]
                    pltpu.make_async_copy(sources[choice][at], target, a_sem.at[tile]).start()

    def l_start(slots):
        for parity, sign in ((0, 1), (1, -1)):
            pairs = ((0, sign), (2 * sign, 3 * sign), (-sign, -2 * sign), (-3 * sign, 4))

            @pl.when(lax.rem(z, 2) == parity)
            def _():
                for slot in slots:
                    for step in pairs[slot]:
                        first = ((parity + step) % 2 ^ yhi) * 1024
                        for at in range(9):
                            if L_STEPS[at] == step:
                                rows = 512 if at >= 7 else 1024
                                start = pl.multiple_of(first + (512 if at == 8 else 0), 512)
                                target = l_vmem.at[slot, pl.ds(start, rows)]
                                pltpu.make_async_copy(l_refs[at], target, l_sem.at[slot]).start()

    a_start(0)
    l_start((0,))
    for tile in range(1, 4):
        a_start(tile)
    l_start((1, 2, 3))

    sign = 1 - 2 * lax.rem(z, 2)

    def multiply(slot, wait):
        pltpu.make_async_copy(l_vmem.at[slot], l_vmem.at[slot], l_sem.at[slot]).wait()
        for tile in range(4):
            rows = pl.ds(256 * tile, 256)
            if wait:
                pltpu.make_async_copy(a_vmem.at[rows], a_vmem.at[rows], a_sem.at[tile]).wait()
            total = jnp.dot(a_vmem[rows], l_vmem[slot], preferred_element_type=F32)
            out_vmem[slot, rows] = total.astype(BF16)
        shift = jnp.where(slot == 1, sign, jnp.where(slot == 2, -sign, jnp.where(slot == 3, 2, 0)))
        j = lax.rem(z // 2 + shift + 4, 4)
        pltpu.make_async_copy(out_vmem.at[slot], out.at[j], out_sem.at[slot]).start()

    multiply(0, True)

    @pl.loop(1, 4)
    def _(slot):
        multiply(slot, False)

    for slot in range(4):
        pltpu.make_async_copy(out_vmem.at[slot], out.at[slot], out_sem.at[slot]).wait()


def products(scalars, a_pieces, l_pieces):
    anywhere = pl.BlockSpec(memory_space=pl.ANY)
    return pl.pallas_call(
        product_kernel,
        in_specs=[pl.BlockSpec(memory_space=pltpu.SMEM)] + [anywhere] * 14,
        out_specs=anywhere,
        out_shape=jax.ShapeDtypeStruct((4, 1024, 256), BF16),
        scratch_shapes=[
            pltpu.VMEM((1024, 2048), BF16),
            pltpu.VMEM((4, 2048, 256), BF16),
            pltpu.VMEM((4, 1024, 256), BF16),
            pltpu.SemaphoreType.DMA((4,)),
            pltpu.SemaphoreType.DMA((4,)),
            pltpu.SemaphoreType.DMA((4,)),
        ],
        compiler_params=pltpu.CompilerParams(vmem_limit_bytes=VMEM_MIB * 2**20),
        cost_estimate=pl.CostEstimate(flops=2 * 1024 * 2048 * 1024, bytes_accessed=12 * 2**20, transcendentals=0),
    )(scalars, *a_pieces, *l_pieces)


def body(ainv, l_panels, dinv, ancestors, block_slot):
    row = lax.axis_index("prow")
    column = lax.axis_index("pcol")
    z, ylo = row // 2, row % 2
    x, yhi, core = column // 4, (column // 2) % 2, column % 2

    flags = jnp.repeat(local_flags(ancestors, block_slot, row, column), BS)[:, None]
    masked = jnp.where(flags, l_panels[0], jnp.zeros((), BF16))

    here = move(move(masked, X_HOME[0]), L_TURN)
    near = move(ainv, Y_NEAR)
    far = move(ainv, Y_FAR)

    l_pieces = [here]
    up = down = here
    for _ in range(2):
        up, down = move(up, Z_UP), move(down, Z_DOWN)
        l_pieces += [up, down]
    up, down, near, far = lax.optimization_barrier((up, down, near, far))
    across_top, across_bottom = move(far[:512], Y_NEAR), move(near[512:], Y_FAR)
    up, down = move(up, Z_UP), move(down, Z_DOWN)
    l_pieces += [up, down, move(up[:512], Z_UP), move(down[512:], Z_DOWN)]
    a_pieces = (ainv, across_top, across_bottom, near, far)

    mine = (ylo != core).astype(jnp.int32)
    give = jnp.stack([z, yhi, 1 - mine]).astype(jnp.int32)
    keep = jnp.stack([z, yhi, mine]).astype(jnp.int32)
    given = products(give, a_pieces, l_pieces)
    taken = move(given, CORE)
    kept = products(keep, a_pieces, l_pieces)
    sums = [(kept[j].astype(F32) + taken[j].astype(F32)).astype(BF16) for j in range(4)]

    total = sum(move(sums[j], X_HOME[j]).astype(F32) for j in (2, 1, 3, 0))
    inverse_column = jnp.where(flags, -total, jnp.zeros((), F32)).astype(BF16)

    terms = lax.dot_general(masked, inverse_column, (((0,), (0,)), ((), ())), preferred_element_type=F32)
    for pairs in (swap(0, 1), swap(1, 0), swap(2, 0), swap(4, 0)):
        terms = terms.astype(BF16)
        terms = terms.astype(F32) + move(terms, pairs).astype(F32)
    return inverse_column[None], dinv - terms[None]


def solution(mesh):
    return jax.shard_map(
        body,
        mesh=mesh,
        in_specs=(P("prow", "pcol"), P("pcol", "prow", None), P("pcol", None, None), P(), P()),
        out_specs=(P("pcol", "prow", None), P("pcol", None, None)),
        check_vma=False,
    )
```

time: 205 us -> 183 us (0.89); the launches traced: 201 us -> 182 us
  starting transfers between devices: 46.1 us -> 38.9 us
  other arithmetic: 13.4 us -> 6.7 us
  local copies, waits for them, and re-layouts: 8.75 us -> 2.42 us
  Pallas kernels: 15.8 us -> 19.9 us
    ppermute x23, starting transfers between devices: 46.1 us -> 38.9 us  [move(): return lax.ppermute(value, AXES, pairs)]
    another operation x6 -> x2, other arithmetic: 6.21 us -> 1.26 us  [the longest x1 0.66 us: body(): keep = jnp.stack([z, yhi, mine]).astype(jnp.int32)]
    pallas_call x2, Pallas kernels: 15.8 us -> 19.9 us  [products(): pl.pallas_call(product_kernel, in_specs=[pl.BlockSpec(memory_space=pltpu....]
    dynamic_update_slice x9 -> x0, local copies, waits for them, and re-layouts: 3.44 us -> none  [body(): lax.dynamic_update_slice(buffer, block[None], (at, start, 0))]
  transfers between devices with their start and end apart: 23 -> 23, of which waited for: 14 -> 16; matrix products, arithmetic and copies ran while one was open for 4% -> 1% of each run, Pallas kernels for 4% -> 5%
where the time goes in v2:
time: 183 us; the launch traced here: 182 us
  waiting for transfers between devices  113 us (62%)
  starting transfers between devices  38.9 us (21%)
  Pallas kernels  19.9 us (11%)
  other arithmetic  6.7 us (4%)
  local copies, waits for them, and re-layouts  2.42 us (1%)
    ppermute x23, waiting for transfers between devices, move(): return lax.ppermute(value, AXES, pairs)  113 us
    ppermute x23, starting transfers between devices, move(): return lax.ppermute(value, AXES, pairs)  38.9 us
    pallas_call x2, Pallas kernels, products(): pl.pallas_call(product_kernel, in_specs=[pl.BlockSpec(memory_space=pltpu....  19.9 us
  transfers between devices with their start and end apart: 23, of which 16 were waited for; matrix products, arithmetic and copies ran while one was open for 1% of the time, Pallas kernels for 5%

profile of v2, /device:TPU:2, one launch (start us, length us, event | category | flops | bytes accessed | tf_op | source)
XLA Modules:
  0.0 182.4 jit_solution(11971298263528663130)
XLA Ops:
  1.4 0.8 and_reduce_fusion
  2.4 1.2 bitcast_select_fusion
  4.3 4.5 %collective-permute-start.7 = (bf16[1024,1024]{1,0:T(8,128)(2,1)}, bf16[1024,1024]{1,0:T(8,128)(2,1)S(1)}, u32[]{:S(2)}, u32[]{:S(2)}) collective-permute-start(bf16[1024,1024]{1,0:T(8,128)(2,1)} %refs_0_.3), channel_id=1, source_target_pairs={{0,18},{1,19},{2,16},{3,17},{4,22},{5,23},{6,20},{7,21},{8,26},{9,... | collective-permute-start | bytes 6291464 | tf_op jit(solution)/shard_map/ppermute | solution.py:46
  8.8 5.1 %collective-permute-start.1 = (bf16[1024,256]{1,0:T(8,128)(2,1)S(1)}, bf16[1024,256]{1,0:T(8,128)(2,1)S(1)}, u32[]{:S(2)}, u32[]{:S(2)}) collective-permute-start(bf16[1024,256]{1,0:T(8,128)(2,1)S(1)} %collective-permute-done), channel_id=1, source_target_pairs={{0,0},{1,1},{2,2},{3,3},{4,64},{5,65},{6,66},{7,67},{8,128},{9,129... | collective-permute-start | bytes 1572872 | tf_op jit(solution)/shard_map/ppermute | solution.py:46
  14.0 21.5 %collective-permute-done.1.refs_5_ = bf16[1024,256]{1,0:T(8,128)(2,1)S(1)} collective-permute-done((bf16[1024,256]{1,0:T(8,128)(2,1)S(1)}, bf16[1024,256]{1,0:T(8,128)(2,1)S(1)}, u32[]{:S(2)}, u32[]{:S(2)}) %collective-permute-start.1) | collective-permute-done | bytes 524320 | tf_op jit(solution)/shard_map/ppermute | solution.py:46
  35.5 2.0 %collective-permute-start.2 = (bf16[1024,256]{1,0:T(8,128)(2,1)S(1)}, bf16[1024,256]{1,0:T(8,128)(2,1)S(1)}, u32[]{:S(2)}, u32[]{:S(2)}) collective-permute-start(bf16[1024,256]{1,0:T(8,128)(2,1)S(1)} %collective-permute-done.1.refs_5_), channel_id=1, source_target_pairs={{0,32},{1,33},{2,34},{3,35},{4,36},{5,37},{6,38},{7,39},{8,40},{9,... | collective-permute-start | bytes 1572872 | tf_op jit(solution)/shard_map/ppermute | solution.py:46
  37.5 11.0 %collective-permute-done.4.refs_7_ = bf16[1024,256]{1,0:T(8,128)(2,1)S(1)} collective-permute-done((bf16[1024,256]{1,0:T(8,128)(2,1)S(1)}, bf16[1024,256]{1,0:T(8,128)(2,1)S(1)}, u32[]{:S(2)}, u32[]{:S(2)}) %collective-permute-start.4) | collective-permute-done | bytes 524320 | tf_op jit(solution)/shard_map/ppermute | solution.py:46
  48.6 4.2 %collective-permute-start.5 = (bf16[1024,256]{1,0:T(8,128)(2,1)S(1)}, bf16[1024,256]{1,0:T(8,128)(2,1)S(1)}, u32[]{:S(2)}, u32[]{:S(2)}) collective-permute-start(bf16[1024,256]{1,0:T(8,128)(2,1)S(1)} %collective-permute-done.4.refs_7_), channel_id=1, source_target_pairs={{0,224},{1,225},{2,226},{3,227},{4,228},{5,229},{6,230},{7,231},{8... | collective-permute-start | bytes 1572872 | tf_op jit(solution)/shard_map/ppermute | solution.py:46
  53.3 11.3 %collective-permute-done.5.refs_9_ = bf16[1024,256]{1,0:T(8,128)(2,1)S(1)} collective-permute-done((bf16[1024,256]{1,0:T(8,128)(2,1)S(1)}, bf16[1024,256]{1,0:T(8,128)(2,1)S(1)}, u32[]{:S(2)}, u32[]{:S(2)}) %collective-permute-start.5) | collective-permute-done | bytes 524320 | tf_op jit(solution)/shard_map/ppermute | solution.py:46
  64.6 6.3 %collective-permute-done.3.refs_8_ = bf16[1024,256]{1,0:T(8,128)(2,1)S(1)} collective-permute-done((bf16[1024,256]{1,0:T(8,128)(2,1)S(1)}, bf16[1024,256]{1,0:T(8,128)(2,1)S(1)}, u32[]{:S(2)}, u32[]{:S(2)}) %collective-permute-start.3) | collective-permute-done | bytes 524320 | tf_op jit(solution)/shard_map/ppermute | solution.py:46
  71.1 2.4 %collective-permute-start.9 = (bf16[512,1024]{1,0:T(8,128)(2,1)S(1)}, bf16[512,1024]{1,0:T(8,128)(2,1)}, u32[]{:S(2)}, u32[]{:S(2)}) collective-permute-start(bf16[512,1024]{1,0:T(8,128)(2,1)S(1)} %slice.37), channel_id=1, source_target_pairs={{0,18},{1,19},{2,16},{3,17},{4,22},{5,23},{6,20},{7,21},{8,26},{9,... | collective-permute-start | bytes 3145736 | tf_op jit(solution)/shard_map/ppermute | solution.py:46
  73.5 3.2 %collective-permute-start.11 = (bf16[1024,256]{1,0:T(8,128)(2,1)S(1)}, bf16[1024,256]{1,0:T(8,128)(2,1)S(1)}, u32[]{:S(2)}, u32[]{:S(2)}) collective-permute-start(bf16[1024,256]{1,0:T(8,128)(2,1)S(1)} %collective-permute-done.5.refs_9_), channel_id=1, source_target_pairs={{0,224},{1,225},{2,226},{3,227},{4,228},{5,229},{6,230},{7,231},{8... | collective-permute-start | bytes 1572872 | tf_op jit(solution)/shard_map/ppermute | solution.py:46
  76.8 9.9 %collective-permute-done.10.refs_10_ = bf16[1024,256]{1,0:T(8,128)(2,1)S(1)} collective-permute-done((bf16[1024,256]{1,0:T(8,128)(2,1)S(1)}, bf16[1024,256]{1,0:T(8,128)(2,1)S(1)}, u32[]{:S(2)}, u32[]{:S(2)}) %collective-permute-start.10) | collective-permute-done | bytes 524320 | tf_op jit(solution)/shard_map/ppermute | solution.py:46
  88.3 2.5 %collective-permute-start.13 = (bf16[512,256]{1,0:T(8,128)(2,1)S(1)}, bf16[512,256]{1,0:T(8,128)(2,1)}, u32[]{:S(2)}, u32[]{:S(2)}) collective-permute-start(bf16[512,256]{1,0:T(8,128)(2,1)S(1)} %slice.49), channel_id=1, source_target_pairs={{0,224},{1,225},{2,226},{3,227},{4,228},{5,229},{6,230},{7,231},{8... | collective-permute-start | bytes 786440 | tf_op jit(solution)/shard_map/ppermute | solution.py:46
  91.5 3.0 %collective-permute-done.12.refs_12_ = bf16[512,256]{1,0:T(8,128)(2,1)S(1)} collective-permute-done((bf16[512,256]{1,0:T(8,128)(2,1)S(1)}, bf16[512,256]{1,0:T(8,128)(2,1)S(1)}, u32[]{:S(2)}, u32[]{:S(2)}) %collective-permute-start.12) | collective-permute-done | bytes 262176 | tf_op jit(solution)/shard_map/ppermute | solution.py:46
  94.8 3.0 %collective-permute-done.9.refs_2_ = bf16[512,1024]{1,0:T(8,128)(2,1)} collective-permute-done((bf16[512,1024]{1,0:T(8,128)(2,1)S(1)}, bf16[512,1024]{1,0:T(8,128)(2,1)}, u32[]{:S(2)}, u32[]{:S(2)}) %collective-permute-start.9) | collective-permute-done | bytes 1048608 | tf_op jit(solution)/shard_map/ppermute | solution.py:46
  97.9 10.1 %shard_map.69 = bf16[4,1024,256]{2,1,0:T(8,128)(2,1)} custom-call(s32[3]{0:T(128)} %pad_add_fusion.2.scalars, bf16[1024,1024]{1,0:T(8,128)(2,1)} %refs_0_.3, bf16[512,1024]{1,0:T(8,128)(2,1)} %collective-permute-done.8.refs_1_, bf16[512,1024]{1,0:T(8,128)(2,1)} %collective-permute-done.9.refs_2_, bf16[1024,1024]{1,0:T(8,128)(2,1)} %copy-done.3, ...), custom_call_target="tpu_custom_call" | custom-call | flops 4294967296 | bytes 12582912 | tf_op jit(solution)/shard_map/pallas_call | solution.py:126
  108.9 9.9 %shard_map.68 = bf16[4,1024,256]{2,1,0:T(8,128)(2,1)} custom-call(s32[3]{0:T(128)} %pad_add_fusion.scalars, bf16[1024,1024]{1,0:T(8,128)(2,1)} %refs_0_.3, bf16[512,1024]{1,0:T(8,128)(2,1)} %collective-permute-done.8.refs_1_, bf16[512,1024]{1,0:T(8,128)(2,1)} %collective-permute-done.9.refs_2_, bf16[1024,1024]{1,0:T(8,128)(2,1)} %copy-done.3, ...), custom_call_target="tpu_custom_call" | custom-call | flops 4294967296 | bytes 12582912 | tf_op jit(solution)/shard_map/pallas_call | solution.py:126
  118.8 2.1 %fusion = (bf16[1024,256]{1,0:T(8,128)(2,1)S(1)}, bf16[1024,256]{1,0:T(8,128)(2,1)S(1)}, bf16[1024,256]{1,0:T(8,128)(2,1)S(1)}, bf16[1024,256]{1,0:T(8,128)(2,1)S(1)}) fusion(bf16[4,1024,256]{2,1,0:T(8,128)(2,1)S(1)} %collective-permute-done.14, bf16[4,1024,256]{2,1,0:T(8,128)(2,1)} %shard_map.68), kind=kLoop, calls=%fused_computation.6 | loop fusion | flops 4194304 | bytes 6291456 | tf_op jit(solution)/shard_map/convert_element_type | solution.py:174
  120.8 1.4 collective-permute-start.15
  122.9 4.0 %collective-permute-start.17 = (bf16[1024,256]{1,0:T(8,128)(2,1)S(1)}, bf16[1024,256]{1,0:T(8,128)(2,1)S(1)}, u32[]{:S(2)}, u32[]{:S(2)}) collective-permute-start(bf16[1024,256]{1,0:T(8,128)(2,1)S(1)} %get-tuple-element.12), channel_id=1, source_target_pairs={{0,12},{1,28},{2,14},{3,30},{4,0},{5,16},{6,2},{7,18},{8,4},{9,20}... | collective-permute-start | bytes 1572872 | tf_op jit(solution)/shard_map/ppermute | solution.py:46
  127.0 10.3 %collective-permute-done.15 = bf16[1024,256]{1,0:T(8,128)(2,1)S(1)} collective-permute-done((bf16[1024,256]{1,0:T(8,128)(2,1)S(1)}, bf16[1024,256]{1,0:T(8,128)(2,1)S(1)}, u32[]{:S(2)}, u32[]{:S(2)}) %collective-permute-start.15) | collective-permute-done | bytes 524320 | tf_op jit(solution)/shard_map/ppermute | solution.py:46
  137.3 9.1 %collective-permute-done.17 = bf16[1024,256]{1,0:T(8,128)(2,1)S(1)} collective-permute-done((bf16[1024,256]{1,0:T(8,128)(2,1)S(1)}, bf16[1024,256]{1,0:T(8,128)(2,1)S(1)}, u32[]{:S(2)}, u32[]{:S(2)}) %collective-permute-start.17) | collective-permute-done | bytes 524320 | tf_op jit(solution)/shard_map/ppermute | solution.py:46
  146.4 1.9 %collective-permute-done.16 = bf16[1024,256]{1,0:T(8,128)(2,1)S(1)} collective-permute-done((bf16[1024,256]{1,0:T(8,128)(2,1)S(1)}, bf16[1024,256]{1,0:T(8,128)(2,1)S(1)}, u32[]{:S(2)}, u32[]{:S(2)}) %collective-permute-start.16) | collective-permute-done | bytes 524320 | tf_op jit(solution)/shard_map/ppermute | solution.py:46
  149.0 1.2 collective-permute-start.19
  150.2 4.9 %collective-permute-done.19 = bf16[256,256]{1,0:T(8,128)(2,1)S(1)} collective-permute-done((bf16[256,256]{1,0:T(8,128)(2,1)S(1)}, bf16[256,256]{1,0:T(8,128)(2,1)S(1)}, u32[]{:S(2)}, u32[]{:S(2)}) %collective-permute-start.19) | collective-permute-done | bytes 131104 | tf_op jit(solution)/shard_map/ppermute | solution.py:46
  155.2 5.6 %collective-permute-done.20 = bf16[256,256]{1,0:T(8,128)(2,1)S(1)} collective-permute-done((bf16[256,256]{1,0:T(8,128)(2,1)S(1)}, bf16[256,256]{1,0:T(8,128)(2,1)S(1)}, u32[]{:S(2)}, u32[]{:S(2)}) %collective-permute-start.20) | collective-permute-done | bytes 131104 | tf_op jit(solution)/shard_map/ppermute | solution.py:46
  160.9 1.3 collective-permute-start.21
  162.2 7.3 %collective-permute-done.21 = bf16[256,256]{1,0:T(8,128)(2,1)S(1)} collective-permute-done((bf16[256,256]{1,0:T(8,128)(2,1)S(1)}, bf16[256,256]{1,0:T(8,128)(2,1)S(1)}, u32[]{:S(2)}, u32[]{:S(2)}) %collective-permute-start.21) | collective-permute-done | bytes 131104 | tf_op jit(solution)/shard_map/ppermute | solution.py:46
  169.5 5.0 %collective-permute-start.22 = (bf16[256,256]{1,0:T(8,128)(2,1)S(1)}, bf16[256,256]{1,0:T(8,128)(2,1)S(1)}, u32[]{:S(2)}, u32[]{:S(2)}) collective-permute-start(bf16[256,256]{1,0:T(8,128)(2,1)S(1)} %add_convert_fusion.4), channel_id=1, source_target_pairs={{0,128},{1,129},{2,130},{3,131},{4,132},{5,133},{6,134},{7,135},{8... | collective-permute-start | bytes 393224 | tf_op jit(solution)/shard_map/ppermute | solution.py:46
  174.4 7.2 %collective-permute-done.22 = bf16[256,256]{1,0:T(8,128)(2,1)S(1)} collective-permute-done((bf16[256,256]{1,0:T(8,128)(2,1)S(1)}, bf16[256,256]{1,0:T(8,128)(2,1)S(1)}, u32[]{:S(2)}, u32[]{:S(2)}) %collective-permute-start.22) | collective-permute-done | bytes 131104 | tf_op jit(solution)/shard_map/ppermute | solution.py:46
  181.6 0.7 bitcast_subtract_fusion
  (61 shorter events, 7.3 us)
Async XLA Ops:
  3.6 5.2 %collective-permute-start = (bf16[1024,256]{1,0:T(8,128)(2,1)S(1)}, bf16[1024,256]{1,0:T(8,128)(2,1)S(1)}, u32[]{:S(2)}, u32[]{:S(2)}) collective-permute-start(bf16[1024,256]{1,0:T(8,128)(2,1)S(1)} %bitcast_select_fusion), channel_id=1, source_target_pairs={{0,0},{1,16},{2,2},{3,18},{4,4},{5,20},{6,6},{7,22},{8,8},{9,24},{... | collective-permute-start | bytes 1572872 | tf_op jit(solution)/shard_map/ppermute | solution.py:46
  4.3 66.6 %collective-permute-start.7 = (bf16[1024,1024]{1,0:T(8,128)(2,1)}, bf16[1024,1024]{1,0:T(8,128)(2,1)S(1)}, u32[]{:S(2)}, u32[]{:S(2)}) collective-permute-start(bf16[1024,1024]{1,0:T(8,128)(2,1)} %refs_0_.3), channel_id=1, source_target_pairs={{0,18},{1,19},{2,16},{3,17},{4,22},{5,23},{6,20},{7,21},{8,26},{9,... | collective-permute-start | bytes 6291464 | tf_op jit(solution)/shard_map/ppermute | solution.py:46
  8.8 62.1 %collective-permute-start.6 = (bf16[1024,1024]{1,0:T(8,128)(2,1)}, bf16[1024,1024]{1,0:T(8,128)(2,1)S(1)}, u32[]{:S(2)}, u32[]{:S(2)}) collective-permute-start(bf16[1024,1024]{1,0:T(8,128)(2,1)} %refs_0_.3), channel_id=1, source_target_pairs={{0,16},{1,17},{2,18},{3,19},{4,20},{5,21},{6,22},{7,23},{8,24},{9,... | collective-permute-start | bytes 6291464 | tf_op jit(solution)/shard_map/ppermute | solution.py:46
  8.8 26.7 %collective-permute-start.1 = (bf16[1024,256]{1,0:T(8,128)(2,1)S(1)}, bf16[1024,256]{1,0:T(8,128)(2,1)S(1)}, u32[]{:S(2)}, u32[]{:S(2)}) collective-permute-start(bf16[1024,256]{1,0:T(8,128)(2,1)S(1)} %collective-permute-done), channel_id=1, source_target_pairs={{0,0},{1,1},{2,2},{3,3},{4,64},{5,65},{6,66},{7,67},{8,128},{9,129... | collective-permute-start | bytes 1572872 | tf_op jit(solution)/shard_map/ppermute | solution.py:46
  35.5 35.4 %copy-start.7 = (bf16[1024,256]{1,0:T(8,128)(2,1)}, bf16[1024,256]{1,0:T(8,128)(2,1)S(1)}, u32[]{:S(2)}) copy-start(bf16[1024,256]{1,0:T(8,128)(2,1)S(1)} %collective-permute-done.1.refs_5_) | copy-start | bytes 1572868
  35.5 13.1 %collective-permute-start.4 = (bf16[1024,256]{1,0:T(8,128)(2,1)S(1)}, bf16[1024,256]{1,0:T(8,128)(2,1)S(1)}, u32[]{:S(2)}, u32[]{:S(2)}) collective-permute-start(bf16[1024,256]{1,0:T(8,128)(2,1)S(1)} %collective-permute-done.1.refs_5_), channel_id=1, source_target_pairs={{0,224},{1,225},{2,226},{3,227},{4,228},{5,229},{6,230},{7,231},{8... | collective-permute-start | bytes 1572872 | tf_op jit(solution)/shard_map/ppermute | solution.py:46
  35.5 17.8 %collective-permute-start.2 = (bf16[1024,256]{1,0:T(8,128)(2,1)S(1)}, bf16[1024,256]{1,0:T(8,128)(2,1)S(1)}, u32[]{:S(2)}, u32[]{:S(2)}) collective-permute-start(bf16[1024,256]{1,0:T(8,128)(2,1)S(1)} %collective-permute-done.1.refs_5_), channel_id=1, source_target_pairs={{0,32},{1,33},{2,34},{3,35},{4,36},{5,37},{6,38},{7,39},{8,40},{9,... | collective-permute-start | bytes 1572872 | tf_op jit(solution)/shard_map/ppermute | solution.py:46
  48.6 22.4 %copy-start.8 = (bf16[1024,256]{1,0:T(8,128)(2,1)}, bf16[1024,256]{1,0:T(8,128)(2,1)S(1)}, u32[]{:S(2)}) copy-start(bf16[1024,256]{1,0:T(8,128)(2,1)S(1)} %collective-permute-done.4.refs_7_) | copy-start | bytes 1572868
  48.6 16.1 %collective-permute-start.5 = (bf16[1024,256]{1,0:T(8,128)(2,1)S(1)}, bf16[1024,256]{1,0:T(8,128)(2,1)S(1)}, u32[]{:S(2)}, u32[]{:S(2)}) collective-permute-start(bf16[1024,256]{1,0:T(8,128)(2,1)S(1)} %collective-permute-done.4.refs_7_), channel_id=1, source_target_pairs={{0,224},{1,225},{2,226},{3,227},{4,228},{5,229},{6,230},{7,231},{8... | collective-permute-start | bytes 1572872 | tf_op jit(solution)/shard_map/ppermute | solution.py:46
  53.3 17.7 %copy-start.9 = (bf16[1024,256]{1,0:T(8,128)(2,1)}, bf16[1024,256]{1,0:T(8,128)(2,1)S(1)}, u32[]{:S(2)}) copy-start(bf16[1024,256]{1,0:T(8,128)(2,1)S(1)} %collective-permute-done.2.refs_6_) | copy-start | bytes 1572868
  53.3 17.6 %collective-permute-start.3 = (bf16[1024,256]{1,0:T(8,128)(2,1)S(1)}, bf16[1024,256]{1,0:T(8,128)(2,1)S(1)}, u32[]{:S(2)}, u32[]{:S(2)}) collective-permute-start(bf16[1024,256]{1,0:T(8,128)(2,1)S(1)} %collective-permute-done.2.refs_6_), channel_id=1, source_target_pairs={{0,32},{1,33},{2,34},{3,35},{4,36},{5,37},{6,38},{7,39},{8,40},{9,... | collective-permute-start | bytes 1572872 | tf_op jit(solution)/shard_map/ppermute | solution.py:46
  64.6 23.0 %copy-start.10 = (bf16[1024,256]{1,0:T(8,128)(2,1)}, bf16[1024,256]{1,0:T(8,128)(2,1)S(1)}, u32[]{:S(2)}) copy-start(bf16[1024,256]{1,0:T(8,128)(2,1)S(1)} %collective-permute-done.5.refs_9_) | copy-start | bytes 1572868
  70.9 16.7 %copy-start.11 = (bf16[1024,256]{1,0:T(8,128)(2,1)}, bf16[1024,256]{1,0:T(8,128)(2,1)S(1)}, u32[]{:S(2)}) copy-start(bf16[1024,256]{1,0:T(8,128)(2,1)S(1)} %collective-permute-done.3.refs_8_) | copy-start | bytes 1572868
  70.9 15.8 %copy-start.2 = (bf16[1024,1024]{1,0:T(8,128)(2,1)}, bf16[1024,1024]{1,0:T(8,128)(2,1)S(1)}, u32[]{:S(2)}) copy-start(bf16[1024,1024]{1,0:T(8,128)(2,1)S(1)} %collective-permute-done.7.refs_4_) | copy-start | bytes 6291460
  71.0 15.8 %copy-start.3 = (bf16[1024,1024]{1,0:T(8,128)(2,1)}, bf16[1024,1024]{1,0:T(8,128)(2,1)S(1)}, u32[]{:S(2)}) copy-start(bf16[1024,1024]{1,0:T(8,128)(2,1)S(1)} %collective-permute-done.6.refs_3_) | copy-start | bytes 6291460
  71.1 26.7 %collective-permute-start.9 = (bf16[512,1024]{1,0:T(8,128)(2,1)S(1)}, bf16[512,1024]{1,0:T(8,128)(2,1)}, u32[]{:S(2)}, u32[]{:S(2)}) collective-permute-start(bf16[512,1024]{1,0:T(8,128)(2,1)S(1)} %slice.37), channel_id=1, source_target_pairs={{0,18},{1,19},{2,16},{3,17},{4,22},{5,23},{6,20},{7,21},{8,26},{9,... | collective-permute-start | bytes 3145736 | tf_op jit(solution)/shard_map/ppermute | solution.py:46
  73.5 24.3 %collective-permute-start.8 = (bf16[512,1024]{1,0:T(8,128)(2,1)S(1)}, bf16[512,1024]{1,0:T(8,128)(2,1)}, u32[]{:S(2)}, u32[]{:S(2)}) collective-permute-start(bf16[512,1024]{1,0:T(8,128)(2,1)S(1)} %slice.36), channel_id=1, source_target_pairs={{0,16},{1,17},{2,18},{3,19},{4,20},{5,21},{6,22},{7,23},{8,24},{9,... | collective-permute-start | bytes 3145736 | tf_op jit(solution)/shard_map/ppermute | solution.py:46
  73.5 13.2 %collective-permute-start.10 = (bf16[1024,256]{1,0:T(8,128)(2,1)S(1)}, bf16[1024,256]{1,0:T(8,128)(2,1)S(1)}, u32[]{:S(2)}, u32[]{:S(2)}) collective-permute-start(bf16[1024,256]{1,0:T(8,128)(2,1)S(1)} %collective-permute-done.3.refs_8_), channel_id=1, source_target_pairs={{0,32},{1,33},{2,34},{3,35},{4,36},{5,37},{6,38},{7,39},{8,40},{9,... | collective-permute-start | bytes 1572872 | tf_op jit(solution)/shard_map/ppermute | solution.py:46
  73.5 13.3 %collective-permute-start.11 = (bf16[1024,256]{1,0:T(8,128)(2,1)S(1)}, bf16[1024,256]{1,0:T(8,128)(2,1)S(1)}, u32[]{:S(2)}, u32[]{:S(2)}) collective-permute-start(bf16[1024,256]{1,0:T(8,128)(2,1)S(1)} %collective-permute-done.5.refs_9_), channel_id=1, source_target_pairs={{0,224},{1,225},{2,226},{3,227},{4,228},{5,229},{6,230},{7,231},{8... | collective-permute-start | bytes 1572872 | tf_op jit(solution)/shard_map/ppermute | solution.py:46
  86.8 7.7 %collective-permute-start.12 = (bf16[512,256]{1,0:T(8,128)(2,1)S(1)}, bf16[512,256]{1,0:T(8,128)(2,1)S(1)}, u32[]{:S(2)}, u32[]{:S(2)}) collective-permute-start(bf16[512,256]{1,0:T(8,128)(2,1)S(1)} %slice.48), channel_id=1, source_target_pairs={{0,32},{1,33},{2,34},{3,35},{4,36},{5,37},{6,38},{7,39},{8,40},{9,... | collective-permute-start | bytes 786440 | tf_op jit(solution)/shard_map/ppermute | solution.py:46
  88.3 6.5 %collective-permute-start.13 = (bf16[512,256]{1,0:T(8,128)(2,1)S(1)}, bf16[512,256]{1,0:T(8,128)(2,1)}, u32[]{:S(2)}, u32[]{:S(2)}) collective-permute-start(bf16[512,256]{1,0:T(8,128)(2,1)S(1)} %slice.49), channel_id=1, source_target_pairs={{0,224},{1,225},{2,226},{3,227},{4,228},{5,229},{6,230},{7,231},{8... | collective-permute-start | bytes 786440 | tf_op jit(solution)/shard_map/ppermute | solution.py:46
  108.0 10.8 %collective-permute-start.14 = (bf16[4,1024,256]{2,1,0:T(8,128)(2,1)}, bf16[4,1024,256]{2,1,0:T(8,128)(2,1)S(1)}, u32[]{:S(2)}, u32[]{:S(2)}) collective-permute-start(bf16[4,1024,256]{2,1,0:T(8,128)(2,1)} %shard_map.69), channel_id=1, source_target_pairs={{0,1},{1,0},{2,3},{3,2},{4,5},{5,4},{6,7},{7,6},{8,9},{9,8},{10,11... | collective-permute-start | bytes 6291464 | tf_op jit(solution)/shard_map/ppermute | solution.py:46
  120.8 16.5 %collective-permute-start.15 = (bf16[1024,256]{1,0:T(8,128)(2,1)S(1)}, bf16[1024,256]{1,0:T(8,128)(2,1)S(1)}, u32[]{:S(2)}, u32[]{:S(2)}) collective-permute-start(bf16[1024,256]{1,0:T(8,128)(2,1)S(1)} %get-tuple-element.10), channel_id=1, source_target_pairs={{0,8},{1,24},{2,10},{3,26},{4,12},{5,28},{6,14},{7,30},{8,0},{9,16... | collective-permute-start | bytes 1572872 | tf_op jit(solution)/shard_map/ppermute | solution.py:46
  122.3 15.1 %collective-permute-start.18 = (bf16[1024,256]{1,0:T(8,128)(2,1)S(1)}, bf16[1024,256]{1,0:T(8,128)(2,1)S(1)}, u32[]{:S(2)}, u32[]{:S(2)}) collective-permute-start(bf16[1024,256]{1,0:T(8,128)(2,1)S(1)} %get-tuple-element.11), channel_id=1, source_target_pairs={{0,0},{1,16},{2,2},{3,18},{4,4},{5,20},{6,6},{7,22},{8,8},{9,24},{... | collective-permute-start | bytes 1572872 | tf_op jit(solution)/shard_map/ppermute | solution.py:46
  122.9 23.5 %collective-permute-start.17 = (bf16[1024,256]{1,0:T(8,128)(2,1)S(1)}, bf16[1024,256]{1,0:T(8,128)(2,1)S(1)}, u32[]{:S(2)}, u32[]{:S(2)}) collective-permute-start(bf16[1024,256]{1,0:T(8,128)(2,1)S(1)} %get-tuple-element.12), channel_id=1, source_target_pairs={{0,12},{1,28},{2,14},{3,30},{4,0},{5,16},{6,2},{7,18},{8,4},{9,20}... | collective-permute-start | bytes 1572872 | tf_op jit(solution)/shard_map/ppermute | solution.py:46
  127.0 54.7 %copy-start.4 = (f32[1,256,256]{2,1,0:T(8,128)S(1)}, f32[1,256,256]{2,1,0:T(8,128)}, u32[]{:S(2)}) copy-start(f32[1,256,256]{2,1,0:T(8,128)} %param.7) | copy-start | bytes 786436
  127.0 21.3 %collective-permute-start.16 = (bf16[1024,256]{1,0:T(8,128)(2,1)S(1)}, bf16[1024,256]{1,0:T(8,128)(2,1)S(1)}, u32[]{:S(2)}, u32[]{:S(2)}) collective-permute-start(bf16[1024,256]{1,0:T(8,128)(2,1)S(1)} %get-tuple-element.13), channel_id=1, source_target_pairs={{0,4},{1,20},{2,6},{3,22},{4,8},{5,24},{6,10},{7,26},{8,12},{9,28}... | collective-permute-start | bytes 1572872 | tf_op jit(solution)/shard_map/ppermute | solution.py:46
  148.6 33.7 %copy-start.1 = (bf16[1024,256]{1,0:T(8,128)(2,1)}, bf16[1024,256]{1,0:T(8,128)(2,1)S(1)}, u32[]{:S(2)}) copy-start(bf16[1024,256]{1,0:T(8,128)(2,1)S(1)} %select_convert_fusion) | copy-start | bytes 1572868
  149.0 6.1 %collective-permute-start.19 = (bf16[256,256]{1,0:T(8,128)(2,1)S(1)}, bf16[256,256]{1,0:T(8,128)(2,1)S(1)}, u32[]{:S(2)}, u32[]{:S(2)}) collective-permute-start(bf16[256,256]{1,0:T(8,128)(2,1)S(1)} %convolution_convert_fusion), channel_id=1, source_target_pairs={{0,16},{1,17},{2,18},{3,19},{4,20},{5,21},{6,22},{7,23},{8,24},{9,... | collective-permute-start | bytes 393224 | tf_op jit(solution)/shard_map/ppermute | solution.py:46
  155.1 5.7 %collective-permute-start.20 = (bf16[256,256]{1,0:T(8,128)(2,1)S(1)}, bf16[256,256]{1,0:T(8,128)(2,1)S(1)}, u32[]{:S(2)}, u32[]{:S(2)}) collective-permute-start(bf16[256,256]{1,0:T(8,128)(2,1)S(1)} %add_convert_fusion.6), channel_id=1, source_target_pairs={{0,32},{1,33},{2,34},{3,35},{4,36},{5,37},{6,38},{7,39},{8,40},{9,... | collective-permute-start | bytes 393224 | tf_op jit(solution)/shard_map/ppermute | solution.py:46
  160.9 8.6 %collective-permute-start.21 = (bf16[256,256]{1,0:T(8,128)(2,1)S(1)}, bf16[256,256]{1,0:T(8,128)(2,1)S(1)}, u32[]{:S(2)}, u32[]{:S(2)}) collective-permute-start(bf16[256,256]{1,0:T(8,128)(2,1)S(1)} %add_convert_fusion.5), channel_id=1, source_target_pairs={{0,64},{1,65},{2,66},{3,67},{4,68},{5,69},{6,70},{7,71},{8,72},{9,... | collective-permute-start | bytes 393224 | tf_op jit(solution)/shard_map/ppermute | solution.py:46
  169.5 12.2 %collective-permute-start.22 = (bf16[256,256]{1,0:T(8,128)(2,1)S(1)}, bf16[256,256]{1,0:T(8,128)(2,1)S(1)}, u32[]{:S(2)}, u32[]{:S(2)}) collective-permute-start(bf16[256,256]{1,0:T(8,128)(2,1)S(1)} %add_convert_fusion.4), channel_id=1, source_target_pairs={{0,128},{1,129},{2,130},{3,131},{4,132},{5,133},{6,134},{7,135},{8... | collective-permute-start | bytes 393224 | tf_op jit(solution)/shard_map/ppermute | solution.py:46
  (4 other events, 5.8 us)

commit v3 on v2

v3 whole, which is shorter than its diff:
```python
import jax
import jax.numpy as jnp
from jax import lax
from jax.experimental import pallas as pl
from jax.experimental.pallas import tpu as pltpu
from jax.sharding import PartitionSpec as P

BS = 128
VMEM_MIB = 56
NZ, NY_LO, NX, NY_HI, NCORE = 8, 2, 4, 2, 2
F32, BF16 = jnp.float32, jnp.bfloat16
AXES = ("prow", "pcol")


def device_index(z, ylo, x, yhi, core):
    return (2 * z + ylo) * 16 + 4 * x + 2 * yhi + core


def permutation(target):
    pairs = []
    for z in range(NZ):
        for ylo in range(NY_LO):
            for x in range(NX):
                for yhi in range(NY_HI):
                    for core in range(NCORE):
                        to = target(z, ylo, x, yhi, core)
                        if to is not None:
                            pairs.append((device_index(z, ylo, x, yhi, core), device_index(*to)))
    return pairs


L_TURN = permutation(lambda z, l, x, q, c: (2 * ((x - z // 2) % 4) + z % 2, l, z // 2, q, c))
CORE = permutation(lambda z, l, x, q, c: (z, l, x, q, 1 - c))
HOME = permutation(lambda z, l, x, q, c: (z, c, x, q, l))


def way(core):
    return 1 - 2 * core


Z_AHEAD = permutation(lambda z, l, x, q, c: ((z + way(c)) % 8, l, x, q, c))
Z_BACK = permutation(lambda z, l, x, q, c: ((z - way(c)) % 8, l, x, q, c))
Y_FIRST = permutation(lambda z, l, x, q, c: (z, 1 - l, x, q ^ c, c))
Y_SECOND = permutation(lambda z, l, x, q, c: (z, 1 - l, x, 1 - (q ^ c), c))
X_AHEAD = permutation(lambda z, l, x, q, c: (z, l, (x + way(c)) % 4, q, c))
X_AHEAD_HOME = permutation(lambda z, l, x, q, c: (z, c, (x + way(c)) % 4, q, l))
X_BACK_HOME = permutation(lambda z, l, x, q, c: (z, c, (x - way(c)) % 4, q, l))


def swap(z_bits, ylo_bit):
    return permutation(lambda z, l, x, q, c: (z ^ z_bits, l ^ ylo_bit, x, q, c))


def move(value, pairs):
    return lax.ppermute(value, AXES, pairs)


def local_flags(ancestors, block_slot, row, column):
    own = lax.dynamic_index_in_dim(ancestors, column, 0, keepdims=False)
    numbers = jnp.arange(block_slot.shape[0], dtype=jnp.int32)
    used = jnp.any(own[:, None] == numbers[None, :], axis=0)
    slots = row * 8 + jnp.arange(8, dtype=jnp.int32)
    return jnp.any(used[None, :] & (block_slot[None, :] == slots[:, None]), axis=1)


L_STEPS = (0, 1, -1, 2, -2, 3, -3, 4)


def product_kernel(scalars, *refs):
    own, across, first_y, second_y, l_refs, out = refs[0], refs[1], refs[2], refs[3], refs[4:12], refs[12]
    a_vmem, l_vmem, out_vmem, a_sem, l_sem, out_sem = refs[13:]
    z, half, which, side, order = scalars[0], scalars[1], scalars[2], scalars[3], scalars[4]

    def a_start(tile):
        rows = pl.ds(256 * tile, 256)
        for choice, sources in enumerate(((own, across), (first_y, second_y))):
            @pl.when(which == choice)
            def _():
                for at in range(2):
                    target = a_vmem.at[rows, pl.ds(1024 * at, 1024)]
                    pltpu.make_async_copy(sources[at].at[rows], target, a_sem.at[tile]).start()

    def l_start(slots):
        for parity, sign in ((0, -1), (1, 1)):
            pairs = ((0, sign), (2 * sign, 3 * sign), (-sign, -2 * sign), (-3 * sign, 4))

            @pl.when(side == parity)
            def _():
                for slot in slots:
                    for step in pairs[slot]:
                        start = pl.multiple_of((half ^ (step % 2)) * 1024, 1024)
                        target = l_vmem.at[slot, pl.ds(start, 1024)]
                        pltpu.make_async_copy(l_refs[L_STEPS.index(step)], target, l_sem.at[slot]).start()

    a_start(0)
    l_start((0,))
    for tile in range(1, 4):
        a_start(tile)
    l_start((1, 2, 3))

    sign = 1 - 2 * lax.rem(z, 2)

    def multiply(slot, wait):
        pltpu.make_async_copy(l_vmem.at[slot], l_vmem.at[slot], l_sem.at[slot]).wait()
        for tile in range(4):
            rows = pl.ds(256 * tile, 256)
            if wait:
                pltpu.make_async_copy(a_vmem.at[rows], a_vmem.at[rows], a_sem.at[tile]).wait()
            total = jnp.dot(a_vmem[rows], l_vmem[slot], preferred_element_type=F32)
            out_vmem[slot, rows] = total.astype(BF16)
        shift = jnp.where(slot == 1, sign, jnp.where(slot == 2, -sign, jnp.where(slot == 3, 2, 0)))
        j = lax.rem((z // 2 + shift + 4) * order, 4)
        pltpu.make_async_copy(out_vmem.at[slot], out.at[j], out_sem.at[slot]).start()

    multiply(0, True)

    @pl.loop(1, 4)
    def _(slot):
        multiply(slot, False)

    for slot in range(4):
        pltpu.make_async_copy(out_vmem.at[slot], out.at[slot], out_sem.at[slot]).wait()


def products(scalars, a_pieces, l_pieces):
    anywhere = pl.BlockSpec(memory_space=pl.ANY)
    return pl.pallas_call(
        product_kernel,
        in_specs=[pl.BlockSpec(memory_space=pltpu.SMEM)] + [anywhere] * 12,
        out_specs=anywhere,
        out_shape=jax.ShapeDtypeStruct((4, 1024, 256), BF16),
        scratch_shapes=[
            pltpu.VMEM((1024, 2048), BF16),
            pltpu.VMEM((4, 2048, 256), BF16),
            pltpu.VMEM((4, 1024, 256), BF16),
            pltpu.SemaphoreType.DMA((4,)),
            pltpu.SemaphoreType.DMA((4,)),
            pltpu.SemaphoreType.DMA((4,)),
        ],
        compiler_params=pltpu.CompilerParams(vmem_limit_bytes=VMEM_MIB * 2**20),
        cost_estimate=pl.CostEstimate(flops=2 * 1024 * 2048 * 1024, bytes_accessed=12 * 2**20, transcendentals=0),
    )(scalars, *a_pieces, *l_pieces)


def body(ainv, l_panels, dinv, ancestors, block_slot):
    row = lax.axis_index("prow")
    column = lax.axis_index("pcol")
    z, ylo = row // 2, row % 2
    x, yhi, core = column // 4, (column // 2) % 2, column % 2

    flags = jnp.repeat(local_flags(ancestors, block_slot, row, column), BS)[:, None]
    masked = jnp.where(flags, l_panels[0], jnp.zeros((), BF16))

    here = move(move(masked, HOME), L_TURN)
    first_y = move(ainv, Y_FIRST)
    second_y = move(ainv, Y_SECOND)

    l_pieces = [here]
    ahead = back = here
    for _ in range(2):
        ahead, back = move(ahead, Z_AHEAD), move(back, Z_BACK)
        l_pieces += [ahead, back]
    ahead, back, first_y, second_y = lax.optimization_barrier((ahead, back, first_y, second_y))
    across = move(second_y, Y_FIRST)
    ahead, back = move(ahead, Z_AHEAD), move(back, Z_BACK)
    l_pieces += [ahead, back, move(ahead, Z_AHEAD)]
    a_pieces = (ainv, across, first_y, second_y)

    mine = (ylo != core).astype(jnp.int32)

    def scalars(which, for_core):
        return jnp.stack([z, (z % 2) ^ yhi ^ (which & core), which, (z % 2) ^ core, 1 + 2 * for_core]).astype(jnp.int32)

    given = products(scalars(1 - mine, 1 - core), a_pieces, l_pieces)
    taken = move(given, CORE)
    kept = products(scalars(mine, core), a_pieces, l_pieces)
    sums = [kept[j].astype(F32) + taken[j].astype(F32) for j in range(4)]

    relayed = move(sums[2].astype(BF16), X_AHEAD)
    total = move(sums[3].astype(BF16), X_BACK_HOME).astype(F32) + move(sums[0].astype(BF16), HOME).astype(F32)
    total += move((sums[1] + relayed.astype(F32)).astype(BF16), X_AHEAD_HOME).astype(F32)
    inverse_column = jnp.where(flags, -total, jnp.zeros((), F32)).astype(BF16)

    terms = lax.dot_general(masked, inverse_column, (((0,), (0,)), ((), ())), preferred_element_type=F32)
    other = jnp.where(ylo == 0, terms[128:], terms[:128]).astype(BF16)
    half = jnp.where(ylo == 0, terms[:128], terms[128:]) + move(other, swap(0, 1)).astype(F32)
    for bit in (1, 2, 4):
        half = half.astype(BF16)
        half = half.astype(F32) + move(half, swap(bit, 0)).astype(F32)
    half = half.astype(BF16)
    other = move(half, swap(0, 1))
    terms = jnp.concatenate([jnp.where(ylo == 0, half, other), jnp.where(ylo == 0, other, half)], axis=0)
    return inverse_column[None], dinv - terms.astype(F32)[None]


def solution(mesh):
    return jax.shard_map(
        body,
        mesh=mesh,
        in_specs=(P("prow", "pcol"), P("pcol", "prow", None), P("pcol", None, None), P(), P()),
        out_specs=(P("pcol", "prow", None), P("pcol", None, None)),
        check_vma=False,
    )
```

time: 183 us -> 177 us (0.967)
  waiting for transfers between devices: 113 us -> 103 us
  other arithmetic: 6.7 us -> 9.15 us
    ppermute x23 -> x22, waiting for transfers between devices: 113 us -> 103 us  [move(): return lax.ppermute(value, AXES, pairs)]
    convert_element_type x4 -> x7, other arithmetic: 2.17 us -> 4.71 us  [the longest x1 2.54 us: body(): sums[3].astype(BF16)]
    ppermute x23 -> x22, starting transfers between devices: 38.9 us -> 39.8 us  [move(): return lax.ppermute(value, AXES, pairs)]
  transfers between devices with their start and end apart: 23 -> 22, of which waited for: 16 -> 14; matrix products, arithmetic and copies ran while one was open for 1% -> 2% of each run, Pallas kernels for 5% -> 6%
where the time goes in v3:
time: 177 us; the launch traced here: 176 us
  waiting for transfers between devices  103 us (58%)
  starting transfers between devices  39.8 us (22%)
  Pallas kernels  19.6 us (11%)
  other arithmetic  9.15 us (5%)
  local copies, waits for them, and re-layouts  2.72 us (2%)
    ppermute x22, waiting for transfers between devices, move(): return lax.ppermute(value, AXES, pairs)  103 us
    ppermute x22, starting transfers between devices, move(): return lax.ppermute(value, AXES, pairs)  39.8 us
    pallas_call x2, Pallas kernels, products(): pl.pallas_call(product_kernel, in_specs=[pl.BlockSpec(memory_space=pltpu....  19.6 us
  transfers between devices with their start and end apart: 22, of which 14 were waited for; matrix products, arithmetic and copies ran while one was open for 2% of the time, Pallas kernels for 6%

profile of v3, /device:TPU:2, one launch (start us, length us, event | category | flops | bytes accessed | tf_op | source)
XLA Modules:
  0.0 175.6 jit_solution(10764995721792625669)
XLA Ops:
  1.4 0.8 and_reduce_fusion
  2.4 1.2 bitcast_select_fusion
  4.3 4.5 %collective-permute-start.7 = (bf16[1024,1024]{1,0:T(8,128)(2,1)}, bf16[1024,1024]{1,0:T(8,128)(2,1)S(1)}, u32[]{:S(2)}, u32[]{:S(2)}) collective-permute-start(bf16[1024,1024]{1,0:T(8,128)(2,1)} %refs_0_.3), channel_id=1, source_target_pairs={{0,18},{1,17},{2,16},{3,19},{4,22},{5,21},{6,20},{7,23},{8,26},{9,... | collective-permute-start | bytes 6291464 | tf_op jit(solution)/shard_map/ppermute | solution.py:55
  8.8 5.1 %collective-permute-start.1 = (bf16[1024,256]{1,0:T(8,128)(2,1)S(1)}, bf16[1024,256]{1,0:T(8,128)(2,1)S(1)}, u32[]{:S(2)}, u32[]{:S(2)}) collective-permute-start(bf16[1024,256]{1,0:T(8,128)(2,1)S(1)} %collective-permute-done), channel_id=1, source_target_pairs={{0,0},{1,1},{2,2},{3,3},{4,64},{5,65},{6,66},{7,67},{8,128},{9,129... | collective-permute-start | bytes 1572872 | tf_op jit(solution)/shard_map/ppermute | solution.py:55
  14.0 20.6 %collective-permute-done.1.refs_4_ = bf16[1024,256]{1,0:T(8,128)(2,1)S(1)} collective-permute-done((bf16[1024,256]{1,0:T(8,128)(2,1)S(1)}, bf16[1024,256]{1,0:T(8,128)(2,1)S(1)}, u32[]{:S(2)}, u32[]{:S(2)}) %collective-permute-start.1) | collective-permute-done | bytes 524320 | tf_op jit(solution)/shard_map/ppermute | solution.py:55
  34.6 2.0 %collective-permute-start.2 = (bf16[1024,256]{1,0:T(8,128)(2,1)S(1)}, bf16[1024,256]{1,0:T(8,128)(2,1)S(1)}, u32[]{:S(2)}, u32[]{:S(2)}) collective-permute-start(bf16[1024,256]{1,0:T(8,128)(2,1)S(1)} %collective-permute-done.1.refs_4_), channel_id=1, source_target_pairs={{0,32},{1,225},{2,34},{3,227},{4,36},{5,229},{6,38},{7,231},{8,40}... | collective-permute-start | bytes 1572872 | tf_op jit(solution)/shard_map/ppermute | solution.py:55
  36.6 9.5 %collective-permute-done.4.refs_6_ = bf16[1024,256]{1,0:T(8,128)(2,1)S(1)} collective-permute-done((bf16[1024,256]{1,0:T(8,128)(2,1)S(1)}, bf16[1024,256]{1,0:T(8,128)(2,1)S(1)}, u32[]{:S(2)}, u32[]{:S(2)}) %collective-permute-start.4) | collective-permute-done | bytes 524320 | tf_op jit(solution)/shard_map/ppermute | solution.py:55
  46.1 4.9 %collective-permute-start.5 = (bf16[1024,256]{1,0:T(8,128)(2,1)S(1)}, bf16[1024,256]{1,0:T(8,128)(2,1)}, u32[]{:S(2)}, u32[]{:S(2)}) collective-permute-start(bf16[1024,256]{1,0:T(8,128)(2,1)S(1)} %collective-permute-done.4.refs_6_), channel_id=1, source_target_pairs={{0,224},{1,33},{2,226},{3,35},{4,228},{5,37},{6,230},{7,39},{8,232... | collective-permute-start | bytes 1572872 | tf_op jit(solution)/shard_map/ppermute | solution.py:55
  51.0 2.1 %collective-permute-done.2.refs_5_ = bf16[1024,256]{1,0:T(8,128)(2,1)S(1)} collective-permute-done((bf16[1024,256]{1,0:T(8,128)(2,1)S(1)}, bf16[1024,256]{1,0:T(8,128)(2,1)S(1)}, u32[]{:S(2)}, u32[]{:S(2)}) %collective-permute-start.2) | collective-permute-done | bytes 524320 | tf_op jit(solution)/shard_map/ppermute | solution.py:55
  53.1 6.6 %collective-permute-done.5.refs_8_ = bf16[1024,256]{1,0:T(8,128)(2,1)} collective-permute-done((bf16[1024,256]{1,0:T(8,128)(2,1)S(1)}, bf16[1024,256]{1,0:T(8,128)(2,1)}, u32[]{:S(2)}, u32[]{:S(2)}) %collective-permute-start.5) | collective-permute-done | bytes 524320 | tf_op jit(solution)/shard_map/ppermute | solution.py:55
  59.7 8.0 %collective-permute-done.3.refs_7_ = bf16[1024,256]{1,0:T(8,128)(2,1)S(1)} collective-permute-done((bf16[1024,256]{1,0:T(8,128)(2,1)S(1)}, bf16[1024,256]{1,0:T(8,128)(2,1)S(1)}, u32[]{:S(2)}, u32[]{:S(2)}) %collective-permute-start.3) | collective-permute-done | bytes 524320 | tf_op jit(solution)/shard_map/ppermute | solution.py:55
  68.5 5.4 %collective-permute-start.10 = (bf16[1024,256]{1,0:T(8,128)(2,1)}, bf16[1024,256]{1,0:T(8,128)(2,1)}, u32[]{:S(2)}, u32[]{:S(2)}) collective-permute-start(bf16[1024,256]{1,0:T(8,128)(2,1)} %collective-permute-done.5.refs_8_), channel_id=1, source_target_pairs={{0,224},{1,33},{2,226},{3,35},{4,228},{5,37},{6,230},{7,39},{8,232... | collective-permute-start | bytes 1572872 | tf_op jit(solution)/shard_map/ppermute | solution.py:55
  73.9 10.8 %collective-permute-done.9.refs_9_ = bf16[1024,256]{1,0:T(8,128)(2,1)} collective-permute-done((bf16[1024,256]{1,0:T(8,128)(2,1)S(1)}, bf16[1024,256]{1,0:T(8,128)(2,1)}, u32[]{:S(2)}, u32[]{:S(2)}) %collective-permute-start.9) | collective-permute-done | bytes 524320 | tf_op jit(solution)/shard_map/ppermute | solution.py:55
  85.4 10.6 %collective-permute-done.11.refs_11_ = bf16[1024,256]{1,0:T(8,128)(2,1)} collective-permute-done((bf16[1024,256]{1,0:T(8,128)(2,1)}, bf16[1024,256]{1,0:T(8,128)(2,1)}, u32[]{:S(2)}, u32[]{:S(2)}) %collective-permute-start.11) | collective-permute-done | bytes 524320 | tf_op jit(solution)/shard_map/ppermute | solution.py:55
  96.0 9.8 %shard_map.69 = bf16[4,1024,256]{2,1,0:T(8,128)(2,1)} custom-call(s32[5]{0:T(128)} %stack.41.scalars, bf16[1024,1024]{1,0:T(8,128)(2,1)} %refs_0_.3, bf16[1024,1024]{1,0:T(8,128)(2,1)} %collective-permute-done.8.refs_1_, bf16[1024,1024]{1,0:T(8,128)(2,1)} %collective-permute-done.6.refs_2_, bf16[1024,1024]{1,0:T(8,128)(2,1)} %copy-done.3, ...), custom_call_target="tpu_custom_call" | custom-call | flops 4294967296 | bytes 12582912 | tf_op jit(solution)/shard_map/pallas_call | solution.py:127
  106.7 9.8 %shard_map.68 = bf16[4,1024,256]{2,1,0:T(8,128)(2,1)} custom-call(s32[5]{0:T(128)} %stack.37.scalars, bf16[1024,1024]{1,0:T(8,128)(2,1)} %refs_0_.3, bf16[1024,1024]{1,0:T(8,128)(2,1)} %collective-permute-done.8.refs_1_, bf16[1024,1024]{1,0:T(8,128)(2,1)} %collective-permute-done.6.refs_2_, bf16[1024,1024]{1,0:T(8,128)(2,1)} %copy-done.3, ...), custom_call_target="tpu_custom_call" | custom-call | flops 4294967296 | bytes 12582912 | tf_op jit(solution)/shard_map/pallas_call | solution.py:127
  116.5 2.5 %fusion.1 = (bf16[1024,256]{1,0:T(8,128)(2,1)}, bf16[1024,256]{1,0:T(8,128)(2,1)S(1)}, bf16[1024,256]{1,0:T(8,128)(2,1)S(1)}) fusion(bf16[4,1024,256]{2,1,0:T(8,128)(2,1)S(1)} %collective-permute-done.12, bf16[4,1024,256]{2,1,0:T(8,128)(2,1)} %shard_map.68), kind=kLoop, calls=%fused_computation.6 | loop fusion | flops 3145728 | bytes 4718592 | tf_op jit(solution)/shard_map/convert_element_type | solution.py:180
  119.0 3.2 %collective-permute-start.15 = (bf16[1024,256]{1,0:T(8,128)(2,1)S(1)}, bf16[1024,256]{1,0:T(8,128)(2,1)S(1)}, u32[]{:S(2)}, u32[]{:S(2)}) collective-permute-start(bf16[1024,256]{1,0:T(8,128)(2,1)S(1)} %get-tuple-element.11), channel_id=1, source_target_pairs={{0,4},{1,13},{2,6},{3,15},{4,8},{5,1},{6,10},{7,3},{8,12},{9,5},{1... | collective-permute-start | bytes 1572872 | tf_op jit(solution)/shard_map/ppermute | solution.py:55
  122.2 1.4 collective-permute-start.14
  123.7 9.9 %collective-permute-done.15 = bf16[1024,256]{1,0:T(8,128)(2,1)S(1)} collective-permute-done((bf16[1024,256]{1,0:T(8,128)(2,1)S(1)}, bf16[1024,256]{1,0:T(8,128)(2,1)S(1)}, u32[]{:S(2)}, u32[]{:S(2)}) %collective-permute-start.15) | collective-permute-done | bytes 524320 | tf_op jit(solution)/shard_map/ppermute | solution.py:55
  133.5 2.1 %fusion = bf16[1024,256]{1,0:T(8,128)(2,1)} fusion(bf16[1024,256]{1,0:T(8,128)(2,1)S(1)} %collective-permute-done.15, bf16[4,1024,256]{2,1,0:T(8,128)(2,1)S(1)} %collective-permute-done.12, bf16[4,1024,256]{2,1,0:T(8,128)(2,1)} %shard_map.68), kind=kLoop, calls=%fused_computation.1 | loop fusion | flops 1572864 | bytes 2097152 | tf_op jit(solution)/shard_map/convert_element_type | solution.py:181
  135.6 2.5 %collective-permute-start.16 = (bf16[1024,256]{1,0:T(8,128)(2,1)}, bf16[1024,256]{1,0:T(8,128)(2,1)S(1)}, u32[]{:S(2)}, u32[]{:S(2)}) collective-permute-start(bf16[1024,256]{1,0:T(8,128)(2,1)} %fusion), channel_id=1, source_target_pairs={{0,4},{1,28},{2,6},{3,30},{4,8},{5,16},{6,10},{7,18},{8,12},{9,20}... | collective-permute-start | bytes 1572872 | tf_op jit(solution)/shard_map/ppermute | solution.py:55
  138.1 7.0 %collective-permute-done.16 = bf16[1024,256]{1,0:T(8,128)(2,1)S(1)} collective-permute-done((bf16[1024,256]{1,0:T(8,128)(2,1)}, bf16[1024,256]{1,0:T(8,128)(2,1)S(1)}, u32[]{:S(2)}, u32[]{:S(2)}) %collective-permute-start.16) | collective-permute-done | bytes 524320 | tf_op jit(solution)/shard_map/ppermute | solution.py:55
  145.1 1.5 select_convert_fusion
  147.0 2.5 %collective-permute-start.17 = (bf16[128,256]{1,0:T(8,128)(2,1)S(1)}, bf16[128,256]{1,0:T(8,128)(2,1)S(1)}, u32[]{:S(2)}, u32[]{:S(2)}) collective-permute-start(bf16[128,256]{1,0:T(8,128)(2,1)S(1)} %select_convert_fusion.1), channel_id=1, source_target_pairs={{0,16},{1,17},{2,18},{3,19},{4,20},{5,21},{6,22},{7,23},{8,24},{9,... | collective-permute-start | bytes 196616 | tf_op jit(solution)/shard_map/ppermute | solution.py:55
  149.5 2.4 %collective-permute-done.17 = bf16[128,256]{1,0:T(8,128)(2,1)S(1)} collective-permute-done((bf16[128,256]{1,0:T(8,128)(2,1)S(1)}, bf16[128,256]{1,0:T(8,128)(2,1)S(1)}, u32[]{:S(2)}, u32[]{:S(2)}) %collective-permute-start.17) | collective-permute-done | bytes 65568 | tf_op jit(solution)/shard_map/ppermute | solution.py:55
  151.9 4.3 %collective-permute-done.18 = bf16[128,256]{1,0:T(8,128)(2,1)S(1)} collective-permute-done((bf16[128,256]{1,0:T(8,128)(2,1)S(1)}, bf16[128,256]{1,0:T(8,128)(2,1)S(1)}, u32[]{:S(2)}, u32[]{:S(2)}) %collective-permute-start.18) | collective-permute-done | bytes 65568 | tf_op jit(solution)/shard_map/ppermute | solution.py:55
  156.3 5.3 %collective-permute-done.19 = bf16[128,256]{1,0:T(8,128)(2,1)S(1)} collective-permute-done((bf16[128,256]{1,0:T(8,128)(2,1)S(1)}, bf16[128,256]{1,0:T(8,128)(2,1)S(1)}, u32[]{:S(2)}, u32[]{:S(2)}) %collective-permute-start.19) | collective-permute-done | bytes 65568 | tf_op jit(solution)/shard_map/ppermute | solution.py:55
  161.6 4.3 %collective-permute-start.20 = (bf16[128,256]{1,0:T(8,128)(2,1)S(1)}, bf16[128,256]{1,0:T(8,128)(2,1)S(1)}, u32[]{:S(2)}, u32[]{:S(2)}) collective-permute-start(bf16[128,256]{1,0:T(8,128)(2,1)S(1)} %add_convert_fusion.4), channel_id=1, source_target_pairs={{0,128},{1,129},{2,130},{3,131},{4,132},{5,133},{6,134},{7,135},{8... | collective-permute-start | bytes 196616 | tf_op jit(solution)/shard_map/ppermute | solution.py:55
  165.9 4.0 %collective-permute-done.20 = bf16[128,256]{1,0:T(8,128)(2,1)S(1)} collective-permute-done((bf16[128,256]{1,0:T(8,128)(2,1)S(1)}, bf16[128,256]{1,0:T(8,128)(2,1)S(1)}, u32[]{:S(2)}, u32[]{:S(2)}) %collective-permute-start.20) | collective-permute-done | bytes 65568 | tf_op jit(solution)/shard_map/ppermute | solution.py:55
  169.9 2.7 %collective-permute-start.21 = (bf16[128,256]{1,0:T(8,128)(2,1)S(1)}, bf16[128,256]{1,0:T(8,128)(2,1)S(1)}, u32[]{:S(2)}, u32[]{:S(2)}) collective-permute-start(bf16[128,256]{1,0:T(8,128)(2,1)S(1)} %add_convert_fusion.3), channel_id=1, source_target_pairs={{0,16},{1,17},{2,18},{3,19},{4,20},{5,21},{6,22},{7,23},{8,24},{9,... | collective-permute-start | bytes 196616 | tf_op jit(solution)/shard_map/ppermute | solution.py:55
  172.6 2.2 %collective-permute-done.21 = bf16[128,256]{1,0:T(8,128)(2,1)S(1)} collective-permute-done((bf16[128,256]{1,0:T(8,128)(2,1)S(1)}, bf16[128,256]{1,0:T(8,128)(2,1)S(1)}, u32[]{:S(2)}, u32[]{:S(2)}) %collective-permute-start.21) | collective-permute-done | bytes 65568 | tf_op jit(solution)/shard_map/ppermute | solution.py:55
  (49 shorter events, 5.3 us)
Async XLA Ops:
  0.6 0.7 copy-start
  3.6 5.2 %collective-permute-start = (bf16[1024,256]{1,0:T(8,128)(2,1)S(1)}, bf16[1024,256]{1,0:T(8,128)(2,1)S(1)}, u32[]{:S(2)}, u32[]{:S(2)}) collective-permute-start(bf16[1024,256]{1,0:T(8,128)(2,1)S(1)} %bitcast_select_fusion), channel_id=1, source_target_pairs={{0,0},{1,16},{2,2},{3,18},{4,4},{5,20},{6,6},{7,22},{8,8},{9,24},{... | collective-permute-start | bytes 1572872 | tf_op jit(solution)/shard_map/ppermute | solution.py:55
  4.3 63.4 %collective-permute-start.7 = (bf16[1024,1024]{1,0:T(8,128)(2,1)}, bf16[1024,1024]{1,0:T(8,128)(2,1)S(1)}, u32[]{:S(2)}, u32[]{:S(2)}) collective-permute-start(bf16[1024,1024]{1,0:T(8,128)(2,1)} %refs_0_.3), channel_id=1, source_target_pairs={{0,18},{1,17},{2,16},{3,19},{4,22},{5,21},{6,20},{7,23},{8,26},{9,... | collective-permute-start | bytes 6291464 | tf_op jit(solution)/shard_map/ppermute | solution.py:55
  8.8 58.9 %collective-permute-start.6 = (bf16[1024,1024]{1,0:T(8,128)(2,1)}, bf16[1024,1024]{1,0:T(8,128)(2,1)}, u32[]{:S(2)}, u32[]{:S(2)}) collective-permute-start(bf16[1024,1024]{1,0:T(8,128)(2,1)} %refs_0_.3), channel_id=1, source_target_pairs={{0,16},{1,19},{2,18},{3,17},{4,20},{5,23},{6,22},{7,21},{8,24},{9,... | collective-permute-start | bytes 6291464 | tf_op jit(solution)/shard_map/ppermute | solution.py:55
  8.8 25.8 %collective-permute-start.1 = (bf16[1024,256]{1,0:T(8,128)(2,1)S(1)}, bf16[1024,256]{1,0:T(8,128)(2,1)S(1)}, u32[]{:S(2)}, u32[]{:S(2)}) collective-permute-start(bf16[1024,256]{1,0:T(8,128)(2,1)S(1)} %collective-permute-done), channel_id=1, source_target_pairs={{0,0},{1,1},{2,2},{3,3},{4,64},{5,65},{6,66},{7,67},{8,128},{9,129... | collective-permute-start | bytes 1572872 | tf_op jit(solution)/shard_map/ppermute | solution.py:55
  34.6 61.4 %copy-start.4 = (bf16[1024,256]{1,0:T(8,128)(2,1)}, bf16[1024,256]{1,0:T(8,128)(2,1)S(1)}, u32[]{:S(2)}) copy-start(bf16[1024,256]{1,0:T(8,128)(2,1)S(1)} %collective-permute-done.1.refs_4_) | copy-start | bytes 1572868
  34.6 11.5 %collective-permute-start.4 = (bf16[1024,256]{1,0:T(8,128)(2,1)S(1)}, bf16[1024,256]{1,0:T(8,128)(2,1)S(1)}, u32[]{:S(2)}, u32[]{:S(2)}) collective-permute-start(bf16[1024,256]{1,0:T(8,128)(2,1)S(1)} %collective-permute-done.1.refs_4_), channel_id=1, source_target_pairs={{0,224},{1,33},{2,226},{3,35},{4,228},{5,37},{6,230},{7,39},{8,232... | collective-permute-start | bytes 1572872 | tf_op jit(solution)/shard_map/ppermute | solution.py:55
  34.6 18.5 %collective-permute-start.2 = (bf16[1024,256]{1,0:T(8,128)(2,1)S(1)}, bf16[1024,256]{1,0:T(8,128)(2,1)S(1)}, u32[]{:S(2)}, u32[]{:S(2)}) collective-permute-start(bf16[1024,256]{1,0:T(8,128)(2,1)S(1)} %collective-permute-done.1.refs_4_), channel_id=1, source_target_pairs={{0,32},{1,225},{2,34},{3,227},{4,36},{5,229},{6,38},{7,231},{8,40}... | collective-permute-start | bytes 1572872 | tf_op jit(solution)/shard_map/ppermute | solution.py:55
  46.1 21.6 %copy-start.5 = (bf16[1024,256]{1,0:T(8,128)(2,1)}, bf16[1024,256]{1,0:T(8,128)(2,1)S(1)}, u32[]{:S(2)}) copy-start(bf16[1024,256]{1,0:T(8,128)(2,1)S(1)} %collective-permute-done.4.refs_6_) | copy-start | bytes 1572868
  46.1 13.6 %collective-permute-start.5 = (bf16[1024,256]{1,0:T(8,128)(2,1)S(1)}, bf16[1024,256]{1,0:T(8,128)(2,1)}, u32[]{:S(2)}, u32[]{:S(2)}) collective-permute-start(bf16[1024,256]{1,0:T(8,128)(2,1)S(1)} %collective-permute-done.4.refs_6_), channel_id=1, source_target_pairs={{0,224},{1,33},{2,226},{3,35},{4,228},{5,37},{6,230},{7,39},{8,232... | collective-permute-start | bytes 1572872 | tf_op jit(solution)/shard_map/ppermute | solution.py:55
  53.1 14.6 %copy-start.6 = (bf16[1024,256]{1,0:T(8,128)(2,1)}, bf16[1024,256]{1,0:T(8,128)(2,1)S(1)}, u32[]{:S(2)}) copy-start(bf16[1024,256]{1,0:T(8,128)(2,1)S(1)} %collective-permute-done.2.refs_5_) | copy-start | bytes 1572868
  53.1 14.5 %collective-permute-start.3 = (bf16[1024,256]{1,0:T(8,128)(2,1)S(1)}, bf16[1024,256]{1,0:T(8,128)(2,1)S(1)}, u32[]{:S(2)}, u32[]{:S(2)}) collective-permute-start(bf16[1024,256]{1,0:T(8,128)(2,1)S(1)} %collective-permute-done.2.refs_5_), channel_id=1, source_target_pairs={{0,32},{1,225},{2,34},{3,227},{4,36},{5,229},{6,38},{7,231},{8,40}... | collective-permute-start | bytes 1572872 | tf_op jit(solution)/shard_map/ppermute | solution.py:55
  67.7 0.8 copy-start.7
  67.7 28.3 %copy-start.3 = (bf16[1024,1024]{1,0:T(8,128)(2,1)}, bf16[1024,1024]{1,0:T(8,128)(2,1)S(1)}, u32[]{:S(2)}) copy-start(bf16[1024,1024]{1,0:T(8,128)(2,1)S(1)} %collective-permute-done.7.refs_3_) | copy-start | bytes 6291460
  67.7 28.3 %collective-permute-start.8 = (bf16[1024,1024]{1,0:T(8,128)(2,1)S(1)}, bf16[1024,1024]{1,0:T(8,128)(2,1)}, u32[]{:S(2)}, u32[]{:S(2)}) collective-permute-start(bf16[1024,1024]{1,0:T(8,128)(2,1)S(1)} %collective-permute-done.7.refs_3_), channel_id=1, source_target_pairs={{0,16},{1,19},{2,18},{3,17},{4,20},{5,23},{6,22},{7,21},{8,24},{9,... | collective-permute-start | bytes 6291464 | tf_op jit(solution)/shard_map/ppermute | solution.py:55
  68.5 16.2 %collective-permute-start.9 = (bf16[1024,256]{1,0:T(8,128)(2,1)S(1)}, bf16[1024,256]{1,0:T(8,128)(2,1)}, u32[]{:S(2)}, u32[]{:S(2)}) collective-permute-start(bf16[1024,256]{1,0:T(8,128)(2,1)S(1)} %collective-permute-done.3.refs_7_), channel_id=1, source_target_pairs={{0,32},{1,225},{2,34},{3,227},{4,36},{5,229},{6,38},{7,231},{8,40}... | collective-permute-start | bytes 1572872 | tf_op jit(solution)/shard_map/ppermute | solution.py:55
  68.5 16.9 %collective-permute-start.10 = (bf16[1024,256]{1,0:T(8,128)(2,1)}, bf16[1024,256]{1,0:T(8,128)(2,1)}, u32[]{:S(2)}, u32[]{:S(2)}) collective-permute-start(bf16[1024,256]{1,0:T(8,128)(2,1)} %collective-permute-done.5.refs_8_), channel_id=1, source_target_pairs={{0,224},{1,33},{2,226},{3,35},{4,228},{5,37},{6,230},{7,39},{8,232... | collective-permute-start | bytes 1572872 | tf_op jit(solution)/shard_map/ppermute | solution.py:55
  84.7 11.3 %collective-permute-start.11 = (bf16[1024,256]{1,0:T(8,128)(2,1)}, bf16[1024,256]{1,0:T(8,128)(2,1)}, u32[]{:S(2)}, u32[]{:S(2)}) collective-permute-start(bf16[1024,256]{1,0:T(8,128)(2,1)} %collective-permute-done.9.refs_9_), channel_id=1, source_target_pairs={{0,32},{1,225},{2,34},{3,227},{4,36},{5,229},{6,38},{7,231},{8,40}... | collective-permute-start | bytes 1572872 | tf_op jit(solution)/shard_map/ppermute | solution.py:55
  105.8 10.7 %collective-permute-start.12 = (bf16[4,1024,256]{2,1,0:T(8,128)(2,1)}, bf16[4,1024,256]{2,1,0:T(8,128)(2,1)S(1)}, u32[]{:S(2)}, u32[]{:S(2)}) collective-permute-start(bf16[4,1024,256]{2,1,0:T(8,128)(2,1)} %shard_map.69), channel_id=1, source_target_pairs={{0,1},{1,0},{2,3},{3,2},{4,5},{5,4},{6,7},{7,6},{8,9},{9,8},{10,11... | collective-permute-start | bytes 6291464 | tf_op jit(solution)/shard_map/ppermute | solution.py:55
  119.0 14.5 %collective-permute-start.15 = (bf16[1024,256]{1,0:T(8,128)(2,1)S(1)}, bf16[1024,256]{1,0:T(8,128)(2,1)S(1)}, u32[]{:S(2)}, u32[]{:S(2)}) collective-permute-start(bf16[1024,256]{1,0:T(8,128)(2,1)S(1)} %get-tuple-element.11), channel_id=1, source_target_pairs={{0,4},{1,13},{2,6},{3,15},{4,8},{5,1},{6,10},{7,3},{8,12},{9,5},{1... | collective-permute-start | bytes 1572872 | tf_op jit(solution)/shard_map/ppermute | solution.py:55
  122.2 15.9 %collective-permute-start.13 = (bf16[1024,256]{1,0:T(8,128)(2,1)}, bf16[1024,256]{1,0:T(8,128)(2,1)}, u32[]{:S(2)}, u32[]{:S(2)}) collective-permute-start(bf16[1024,256]{1,0:T(8,128)(2,1)} %get-tuple-element.10), channel_id=1, source_target_pairs={{0,12},{1,20},{2,14},{3,22},{4,0},{5,24},{6,2},{7,26},{8,4},{9,28}... | collective-permute-start | bytes 1572872 | tf_op jit(solution)/shard_map/ppermute | solution.py:55
  122.2 15.9 %collective-permute-start.14 = (bf16[1024,256]{1,0:T(8,128)(2,1)S(1)}, bf16[1024,256]{1,0:T(8,128)(2,1)}, u32[]{:S(2)}, u32[]{:S(2)}) collective-permute-start(bf16[1024,256]{1,0:T(8,128)(2,1)S(1)} %get-tuple-element.12), channel_id=1, source_target_pairs={{0,0},{1,16},{2,2},{3,18},{4,4},{5,20},{6,6},{7,22},{8,8},{9,24},{... | collective-permute-start | bytes 1572872 | tf_op jit(solution)/shard_map/ppermute | solution.py:55
  135.6 9.5 %collective-permute-start.16 = (bf16[1024,256]{1,0:T(8,128)(2,1)}, bf16[1024,256]{1,0:T(8,128)(2,1)S(1)}, u32[]{:S(2)}, u32[]{:S(2)}) collective-permute-start(bf16[1024,256]{1,0:T(8,128)(2,1)} %fusion), channel_id=1, source_target_pairs={{0,4},{1,28},{2,6},{3,30},{4,8},{5,16},{6,10},{7,18},{8,12},{9,20}... | collective-permute-start | bytes 1572872 | tf_op jit(solution)/shard_map/ppermute | solution.py:55
  138.1 36.8 %copy-start.2 = (f32[1,256,256]{2,1,0:T(8,128)S(1)}, f32[1,256,256]{2,1,0:T(8,128)}, u32[]{:S(2)}) copy-start(f32[1,256,256]{2,1,0:T(8,128)} %param.7) | copy-start | bytes 786436
  146.6 29.0 %copy-start.1 = (bf16[1024,256]{1,0:T(8,128)(2,1)}, bf16[1024,256]{1,0:T(8,128)(2,1)S(1)}, u32[]{:S(2)}) copy-start(bf16[1024,256]{1,0:T(8,128)(2,1)S(1)} %select_convert_fusion) | copy-start | bytes 1572868
  147.0 4.8 %collective-permute-start.17 = (bf16[128,256]{1,0:T(8,128)(2,1)S(1)}, bf16[128,256]{1,0:T(8,128)(2,1)S(1)}, u32[]{:S(2)}, u32[]{:S(2)}) collective-permute-start(bf16[128,256]{1,0:T(8,128)(2,1)S(1)} %select_convert_fusion.1), channel_id=1, source_target_pairs={{0,16},{1,17},{2,18},{3,19},{4,20},{5,21},{6,22},{7,23},{8,24},{9,... | collective-permute-start | bytes 196616 | tf_op jit(solution)/shard_map/ppermute | solution.py:55
  151.8 4.4 %collective-permute-start.18 = (bf16[128,256]{1,0:T(8,128)(2,1)S(1)}, bf16[128,256]{1,0:T(8,128)(2,1)S(1)}, u32[]{:S(2)}, u32[]{:S(2)}) collective-permute-start(bf16[128,256]{1,0:T(8,128)(2,1)S(1)} %add_convert_fusion.6), channel_id=1, source_target_pairs={{0,32},{1,33},{2,34},{3,35},{4,36},{5,37},{6,38},{7,39},{8,40},{9,... | collective-permute-start | bytes 196616 | tf_op jit(solution)/shard_map/ppermute | solution.py:55
  156.2 5.4 %collective-permute-start.19 = (bf16[128,256]{1,0:T(8,128)(2,1)S(1)}, bf16[128,256]{1,0:T(8,128)(2,1)S(1)}, u32[]{:S(2)}, u32[]{:S(2)}) collective-permute-start(bf16[128,256]{1,0:T(8,128)(2,1)S(1)} %add_convert_fusion.5), channel_id=1, source_target_pairs={{0,64},{1,65},{2,66},{3,67},{4,68},{5,69},{6,70},{7,71},{8,72},{9,... | collective-permute-start | bytes 196616 | tf_op jit(solution)/shard_map/ppermute | solution.py:55
  161.6 8.3 %collective-permute-start.20 = (bf16[128,256]{1,0:T(8,128)(2,1)S(1)}, bf16[128,256]{1,0:T(8,128)(2,1)S(1)}, u32[]{:S(2)}, u32[]{:S(2)}) collective-permute-start(bf16[128,256]{1,0:T(8,128)(2,1)S(1)} %add_convert_fusion.4), channel_id=1, source_target_pairs={{0,128},{1,129},{2,130},{3,131},{4,132},{5,133},{6,134},{7,135},{8... | collective-permute-start | bytes 196616 | tf_op jit(solution)/shard_map/ppermute | solution.py:55
  169.9 4.9 %collective-permute-start.21 = (bf16[128,256]{1,0:T(8,128)(2,1)S(1)}, bf16[128,256]{1,0:T(8,128)(2,1)S(1)}, u32[]{:S(2)}, u32[]{:S(2)}) collective-permute-start(bf16[128,256]{1,0:T(8,128)(2,1)S(1)} %add_convert_fusion.3), channel_id=1, source_target_pairs={{0,16},{1,17},{2,18},{3,19},{4,20},{5,21},{6,22},{7,23},{8,24},{9,... | collective-permute-start | bytes 196616 | tf_op jit(solution)/shard_map/ppermute | solution.py:55

commit v4 on v3

--- a/solution.py
+++ b/solution.py
@@ -1,3 +1,5 @@
+import functools
+
 import jax
 import jax.numpy as jnp
 from jax import lax
@@ -66,69 +68,111 @@
 L_STEPS = (0, 1, -1, 2, -2, 3, -3, 4)
 
 
-def product_kernel(scalars, *refs):
-    own, across, first_y, second_y, l_refs, out = refs[0], refs[1], refs[2], refs[3], refs[4:12], refs[12]
-    a_vmem, l_vmem, out_vmem, a_sem, l_sem, out_sem = refs[13:]
-    z, half, which, side, order = scalars[0], scalars[1], scalars[2], scalars[3], scalars[4]
+A_ROWS = 256
+
+
+def product_kernel(early, scalars, *refs):
+    if early:
+        a_sets, l_refs, refs = (None, refs[0:2]), refs[2:9], refs[9:]
+        outs, refs = refs[:2], refs[2:]
+    else:
+        a_sets, l_refs, refs = (refs[0:2], refs[2:4]), refs[4:12], refs[13:]
+        outs, refs = refs[:1], refs[1:]
+    a_vmem, l_vmem, out_vmem, a_sem, l_sem, out_sem = refs
+    z, half, side, order, which = (scalars[at] for at in range(5))
+    first_slot = 0 if early else 3 * which
+    slots = 3 if early else 4
 
     def a_start(tile):
-        rows = pl.ds(256 * tile, 256)
-        for choice, sources in enumerate(((own, across), (first_y, second_y))):
-            @pl.when(which == choice)
-            def _():
+        rows = pl.ds(A_ROWS * tile, A_ROWS)
+        for choice, sources in enumerate(a_sets):
+            if sources is None:
+                continue
+
+            def start():
                 for at in range(2):
                     target = a_vmem.at[rows, pl.ds(1024 * at, 1024)]
                     pltpu.make_async_copy(sources[at].at[rows], target, a_sem.at[tile]).start()
 
-    def l_start(slots):
+            if early:
+                start()
+            else:
+                pl.when(which == choice)(start)
+
+    def l_start(these):
         for parity, sign in ((0, -1), (1, 1)):
             pairs = ((0, sign), (2 * sign, 3 * sign), (-sign, -2 * sign), (-3 * sign, 4))
 
             @pl.when(side == parity)
             def _():
-                for slot in slots:
+                for slot in these:
                     for step in pairs[slot]:
                         start = pl.multiple_of((half ^ (step % 2)) * 1024, 1024)
                         target = l_vmem.at[slot, pl.ds(start, 1024)]
                         pltpu.make_async_copy(l_refs[L_STEPS.index(step)], target, l_sem.at[slot]).start()
 
     a_start(0)
-    l_start((0,))
+    if early:
+        l_start((0,))
+    else:
+        pl.when(first_slot == 0)(lambda: l_start((0,)))
+        pl.when(first_slot == 3)(lambda: l_start((3,)))
     for tile in range(1, 4):
         a_start(tile)
-    l_start((1, 2, 3))
+    if early:
+        l_start((1, 2))
+    else:
+        pl.when(first_slot == 0)(lambda: l_start((1, 2, 3)))
 
     sign = 1 - 2 * lax.rem(z, 2)
 
     def multiply(slot, wait):
         pltpu.make_async_copy(l_vmem.at[slot], l_vmem.at[slot], l_sem.at[slot]).wait()
         for tile in range(4):
-            rows = pl.ds(256 * tile, 256)
+            rows = pl.ds(A_ROWS * tile, A_ROWS)
             if wait:
                 pltpu.make_async_copy(a_vmem.at[rows], a_vmem.at[rows], a_sem.at[tile]).wait()
             total = jnp.dot(a_vmem[rows], l_vmem[slot], preferred_element_type=F32)
             out_vmem[slot, rows] = total.astype(BF16)
         shift = jnp.where(slot == 1, sign, jnp.where(slot == 2, -sign, jnp.where(slot == 3, 2, 0)))
         j = lax.rem((z // 2 + shift + 4) * order, 4)
-        pltpu.make_async_copy(out_vmem.at[slot], out.at[j], out_sem.at[slot]).start()
-
-    multiply(0, True)
-
-    @pl.loop(1, 4)
-    def _(slot):
-        multiply(slot, False)
-
-    for slot in range(4):
-        pltpu.make_async_copy(out_vmem.at[slot], out.at[slot], out_sem.at[slot]).wait()
-
-
-def products(scalars, a_pieces, l_pieces):
+        if early:
+            for choice, out in enumerate(outs):
+                @pl.when(which == choice)
+                def _():
+                    pltpu.make_async_copy(out_vmem.at[slot], out.at[j], out_sem.at[slot]).start()
+        else:
+            pltpu.make_async_copy(out_vmem.at[slot], outs[0].at[j], out_sem.at[slot]).start()
+
+    def finish(slot):
+        pltpu.make_async_copy(out_vmem.at[slot], outs[0].at[slot], out_sem.at[slot]).wait()
+
+    def several():
+        multiply(0, True)
+        pl.loop(1, slots)(lambda slot: multiply(slot, False))
+        for slot in range(slots):
+            finish(slot)
+
+    def last():
+        multiply(3, True)
+        finish(3)
+
+    if early:
+        several()
+    else:
+        pl.when(first_slot == 0)(several)
+        pl.when(first_slot == 3)(last)
+
+
+def product_call(early, scalars, *arrays):
     anywhere = pl.BlockSpec(memory_space=pl.ANY)
+    block = jax.ShapeDtypeStruct((4, 1024, 256), BF16)
+    slots = 3 if early else 2.5
     return pl.pallas_call(
-        product_kernel,
-        in_specs=[pl.BlockSpec(memory_space=pltpu.SMEM)] + [anywhere] * 12,
-        out_specs=anywhere,
-        out_shape=jax.ShapeDtypeStruct((4, 1024, 256), BF16),
+        functools.partial(product_kernel, early),
+        in_specs=[pl.BlockSpec(memory_space=pltpu.SMEM)] + [anywhere] * len(arrays),
+        out_specs=(anywhere, anywhere) if early else anywhere,
+        out_shape=(block, block) if early else block,
         scratch_shapes=[
             pltpu.VMEM((1024, 2048), BF16),
             pltpu.VMEM((4, 2048, 256), BF16),
@@ -137,9 +181,20 @@
             pltpu.SemaphoreType.DMA((4,)),
             pltpu.SemaphoreType.DMA((4,)),
         ],
+        input_output_aliases={} if early else {len(arrays): 0},
         compiler_params=pltpu.CompilerParams(vmem_limit_bytes=VMEM_MIB * 2**20),
-        cost_estimate=pl.CostEstimate(flops=2 * 1024 * 2048 * 1024, bytes_accessed=12 * 2**20, transcendentals=0),
-    )(scalars, *a_pieces, *l_pieces)
+        cost_estimate=pl.CostEstimate(
+            flops=int(slots * 2 * 1024 * 2048 * 256), bytes_accessed=10 * 2**20, transcendentals=0
+        ),
+    )(scalars, *arrays)
+
+
+def products_early(scalars, a_pieces, l_pieces):
+    return product_call(True, scalars, *a_pieces, *l_pieces)
+
+
+def products(scalars, a_pieces, l_pieces, out):
+    return product_call(False, scalars, *a_pieces, *l_pieces, out)
 
 
 def body(ainv, l_panels, dinv, ancestors, block_slot):
@@ -163,30 +218,34 @@
     ahead, back, first_y, second_y = lax.optimization_barrier((ahead, back, first_y, second_y))
     across = move(second_y, Y_FIRST)
     ahead, back = move(ahead, Z_AHEAD), move(back, Z_BACK)
-    l_pieces += [ahead, back, move(ahead, Z_AHEAD)]
+    l_pieces += [ahead, back]
+
+    given_is_other = (ylo == core).astype(jnp.int32)
+
+    def scalars(other, for_core, last):
+        half = (z % 2) ^ yhi ^ (other & core)
+        return jnp.stack([z, half, (z % 2) ^ core, 1 + 2 * for_core, last]).astype(jnp.int32)
+
+    for_core = jnp.where(given_is_other == 1, 1 - core, core)
+    kept, given = products_early(scalars(1, for_core, given_is_other), (first_y, second_y), l_pieces)
+    l_pieces.append(move(ahead, Z_AHEAD))
     a_pieces = (ainv, across, first_y, second_y)
-
-    mine = (ylo != core).astype(jnp.int32)
-
-    def scalars(which, for_core):
-        return jnp.stack([z, (z % 2) ^ yhi ^ (which & core), which, (z % 2) ^ core, 1 + 2 * for_core]).astype(jnp.int32)
-
-    given = products(scalars(1 - mine, 1 - core), a_pieces, l_pieces)
+    given = products(scalars(given_is_other, 1 - core, given_is_other), a_pieces, l_pieces, given)
     taken = move(given, CORE)
-    kept = products(scalars(mine, core), a_pieces, l_pieces)
-    sums = [kept[j].astype(F32) + taken[j].astype(F32) for j in range(4)]
-
-    relayed = move(sums[2].astype(BF16), X_AHEAD)
-    total = move(sums[3].astype(BF16), X_BACK_HOME).astype(F32) + move(sums[0].astype(BF16), HOME).astype(F32)
-    total += move((sums[1] + relayed.astype(F32)).astype(BF16), X_AHEAD_HOME).astype(F32)
+    kept = products(scalars(1 - given_is_other, core, 1 - given_is_other), a_pieces, l_pieces, kept)
+    sums = [lax.optimization_barrier((kept[j].astype(F32) + taken[j].astype(F32)).astype(BF16)) for j in range(4)]
+
+    relayed = move(sums[2], X_AHEAD)
+    total = move(sums[3], X_BACK_HOME).astype(F32) + move(sums[0], HOME).astype(F32)
+    total += move((sums[1].astype(F32) + relayed.astype(F32)).astype(BF16), X_AHEAD_HOME).astype(F32)
     inverse_column = jnp.where(flags, -total, jnp.zeros((), F32)).astype(BF16)
 
     terms = lax.dot_general(masked, inverse_column, (((0,), (0,)), ((), ())), preferred_element_type=F32)
     other = jnp.where(ylo == 0, terms[128:], terms[:128]).astype(BF16)
     half = jnp.where(ylo == 0, terms[:128], terms[128:]) + move(other, swap(0, 1)).astype(F32)
-    for bit in (1, 2, 4):
+    for bits in (1, 2, 7):
         half = half.astype(BF16)
-        half = half.astype(F32) + move(half, swap(bit, 0)).astype(F32)
+        half = half.astype(F32) + move(half, swap(bits, 0)).astype(F32)
     half = half.astype(BF16)
     other = move(half, swap(0, 1))
     terms = jnp.concatenate([jnp.where(ylo == 0, half, other), jnp.where(ylo == 0, other, half)], axis=0)

time: 177 us -> 171 us (0.966)
  starting transfers between devices: 39.8 us -> 34.5 us
  Pallas kernels: 19.6 us -> 24.1 us
  waiting for transfers between devices: 103 us -> 98.9 us
  other arithmetic: 9.15 us -> 6.76 us
    ppermute x22, starting transfers between devices: 39.8 us -> 34.5 us  [move(): return lax.ppermute(value, AXES, pairs)]
    pallas_call x2 -> x3, Pallas kernels: 19.6 us -> 24.1 us  [product_call(): pl.pallas_call(functools.partial(product_kernel, early), in_specs=[pl.Blo...]
    ppermute x22, waiting for transfers between devices: 103 us -> 98.9 us  [move(): return lax.ppermute(value, AXES, pairs)]
    convert_element_type x2, other arithmetic: 4.61 us -> 2.39 us  [the longest x1 2.23 us: body(): (kept[j].astype(F32) + taken[j].astype(F32)).astype(BF16)]
  transfers between devices with their start and end apart: 22 -> 22, of which waited for: 14 -> 14; matrix products, arithmetic and copies ran while one was open for 2% -> 1% of each run, Pallas kernels for 6% -> 11%
where the time goes in v4:
time: 171 us; the launch traced here: 169 us
  waiting for transfers between devices  98.9 us (58%)
  starting transfers between devices  34.5 us (20%)
  Pallas kernels  24.1 us (14%)
  other arithmetic  6.76 us (4%)
  local copies, waits for them, and re-layouts  3.49 us (2%)
    ppermute x22, waiting for transfers between devices, move(): return lax.ppermute(value, AXES, pairs)  98.9 us
    ppermute x22, starting transfers between devices, move(): return lax.ppermute(value, AXES, pairs)  34.5 us
    pallas_call x3, Pallas kernels, product_call(): pl.pallas_call(functools.partial(product_kernel, early), in_specs=[pl.Blo...  24.1 us
  transfers between devices with their start and end apart: 22, of which 14 were waited for; matrix products, arithmetic and copies ran while one was open for 1% of the time, Pallas kernels for 11%

profile of v4, /device:TPU:2, one launch (start us, length us, event | category | flops | bytes accessed | tf_op | source)
XLA Modules:
  0.0 169.0 jit_solution(4486130159611453962)
XLA Ops:
  1.4 0.8 and_reduce_fusion
  2.4 1.2 bitcast_select_fusion
  4.3 4.5 %collective-permute-start.7 = (bf16[1024,1024]{1,0:T(8,128)(2,1)}, bf16[1024,1024]{1,0:T(8,128)(2,1)S(1)}, u32[]{:S(2)}, u32[]{:S(2)}) collective-permute-start(bf16[1024,1024]{1,0:T(8,128)(2,1)} %refs_0_.3), channel_id=1, source_target_pairs={{0,18},{1,17},{2,16},{3,19},{4,22},{5,21},{6,20},{7,23},{8,26},{9,... | collective-permute-start | bytes 6291464 | tf_op jit(solution)/shard_map/ppermute | solution.py:57
  8.8 5.1 %collective-permute-start.1 = (bf16[1024,256]{1,0:T(8,128)(2,1)S(1)}, bf16[1024,256]{1,0:T(8,128)(2,1)S(1)}, u32[]{:S(2)}, u32[]{:S(2)}) collective-permute-start(bf16[1024,256]{1,0:T(8,128)(2,1)S(1)} %collective-permute-done), channel_id=1, source_target_pairs={{0,0},{1,1},{2,2},{3,3},{4,64},{5,65},{6,66},{7,67},{8,128},{9,129... | collective-permute-start | bytes 1572872 | tf_op jit(solution)/shard_map/ppermute | solution.py:57
  14.0 20.6 %collective-permute-done.1.refs_2_.refs_4_ = bf16[1024,256]{1,0:T(8,128)(2,1)S(1)} collective-permute-done((bf16[1024,256]{1,0:T(8,128)(2,1)S(1)}, bf16[1024,256]{1,0:T(8,128)(2,1)S(1)}, u32[]{:S(2)}, u32[]{:S(2)}) %collective-permute-start.1) | collective-permute-done | bytes 524320 | tf_op jit(solution)/shard_map/ppermute | solution.py:57
  34.6 2.0 %collective-permute-start.2 = (bf16[1024,256]{1,0:T(8,128)(2,1)S(1)}, bf16[1024,256]{1,0:T(8,128)(2,1)S(1)}, u32[]{:S(2)}, u32[]{:S(2)}) collective-permute-start(bf16[1024,256]{1,0:T(8,128)(2,1)S(1)} %collective-permute-done.1.refs_2_.refs_4_), channel_id=1, source_target_pairs={{0,32},{1,225},{2,34},{3,227},{4,36},{5,229},{6,38},{7,231},{8,40}... | collective-permute-start | bytes 1572872 | tf_op jit(solution)/shard_map/ppermute | solution.py:57
  36.6 9.5 %collective-permute-done.4.refs_4_.refs_6_ = bf16[1024,256]{1,0:T(8,128)(2,1)S(1)} collective-permute-done((bf16[1024,256]{1,0:T(8,128)(2,1)S(1)}, bf16[1024,256]{1,0:T(8,128)(2,1)S(1)}, u32[]{:S(2)}, u32[]{:S(2)}) %collective-permute-start.4) | collective-permute-done | bytes 524320 | tf_op jit(solution)/shard_map/ppermute | solution.py:57
  46.1 4.9 %collective-permute-start.5 = (bf16[1024,256]{1,0:T(8,128)(2,1)S(1)}, bf16[1024,256]{1,0:T(8,128)(2,1)}, u32[]{:S(2)}, u32[]{:S(2)}) collective-permute-start(bf16[1024,256]{1,0:T(8,128)(2,1)S(1)} %collective-permute-done.4.refs_4_.refs_6_), channel_id=1, source_target_pairs={{0,224},{1,33},{2,226},{3,35},{4,228},{5,37},{6,230},{7,39},{8,232... | collective-permute-start | bytes 1572872 | tf_op jit(solution)/shard_map/ppermute | solution.py:57
  51.1 2.1 %collective-permute-done.2.refs_3_.refs_5_ = bf16[1024,256]{1,0:T(8,128)(2,1)S(1)} collective-permute-done((bf16[1024,256]{1,0:T(8,128)(2,1)S(1)}, bf16[1024,256]{1,0:T(8,128)(2,1)S(1)}, u32[]{:S(2)}, u32[]{:S(2)}) %collective-permute-start.2) | collective-permute-done | bytes 524320 | tf_op jit(solution)/shard_map/ppermute | solution.py:57
  53.2 6.6 %collective-permute-done.5.refs_6_.refs_8_ = bf16[1024,256]{1,0:T(8,128)(2,1)} collective-permute-done((bf16[1024,256]{1,0:T(8,128)(2,1)S(1)}, bf16[1024,256]{1,0:T(8,128)(2,1)}, u32[]{:S(2)}, u32[]{:S(2)}) %collective-permute-start.5) | collective-permute-done | bytes 524320 | tf_op jit(solution)/shard_map/ppermute | solution.py:57
  59.7 8.0 %collective-permute-done.3.refs_5_.refs_7_ = bf16[1024,256]{1,0:T(8,128)(2,1)S(1)} collective-permute-done((bf16[1024,256]{1,0:T(8,128)(2,1)S(1)}, bf16[1024,256]{1,0:T(8,128)(2,1)S(1)}, u32[]{:S(2)}, u32[]{:S(2)}) %collective-permute-start.3) | collective-permute-done | bytes 524320 | tf_op jit(solution)/shard_map/ppermute | solution.py:57
  67.8 0.7 copy-done.5
  68.5 5.4 %collective-permute-start.10 = (bf16[1024,256]{1,0:T(8,128)(2,1)}, bf16[1024,256]{1,0:T(8,128)(2,1)}, u32[]{:S(2)}, u32[]{:S(2)}) collective-permute-start(bf16[1024,256]{1,0:T(8,128)(2,1)} %collective-permute-done.5.refs_6_.refs_8_), channel_id=1, source_target_pairs={{0,224},{1,33},{2,226},{3,35},{4,228},{5,37},{6,230},{7,39},{8,232... | collective-permute-start | bytes 1572872 | tf_op jit(solution)/shard_map/ppermute | solution.py:57
  74.0 10.8 %collective-permute-done.9.refs_7_.refs_9_ = bf16[1024,256]{1,0:T(8,128)(2,1)} collective-permute-done((bf16[1024,256]{1,0:T(8,128)(2,1)S(1)}, bf16[1024,256]{1,0:T(8,128)(2,1)}, u32[]{:S(2)}, u32[]{:S(2)}) %collective-permute-start.9) | collective-permute-done | bytes 524320 | tf_op jit(solution)/shard_map/ppermute | solution.py:57
  86.1 8.6 %shard_map.68 = (bf16[4,1024,256]{2,1,0:T(8,128)(2,1)}, bf16[4,1024,256]{2,1,0:T(8,128)(2,1)}) custom-call(s32[5]{0:T(128)} %stack.53.scalars, bf16[1024,1024]{1,0:T(8,128)(2,1)} %collective-permute-done.6.refs_0_.refs_2_, bf16[1024,1024]{1,0:T(8,128)(2,1)} %copy-done.1, bf16[1024,256]{1,0:T(8,128)(2,1)} %copy-done.2, bf16[1024,256]{1,0:T(8,128)(2,1)} %copy-done.4, ...), custom_call_target="tpu_custom_call" | custom-call | flops 3221225472 | bytes 10485760 | tf_op jit(solution)/shard_map/pallas_call | solution.py:171
  94.7 1.4 collective-permute-done.11.refs_11_
  96.1 5.8 %shard_map.70 = bf16[4,1024,256]{2,1,0:T(8,128)(2,1)} custom-call(s32[5]{0:T(128)} %stack.56.scalars, bf16[1024,1024]{1,0:T(8,128)(2,1)} %refs_0_.3, bf16[1024,1024]{1,0:T(8,128)(2,1)} %collective-permute-done.8.refs_1_, bf16[1024,1024]{1,0:T(8,128)(2,1)} %collective-permute-done.6.refs_0_.refs_2_, ...), custom_call_target="tpu_custom_call", output_to_operand_aliasing={{}: (13, {})} | custom-call | flops 2684354560 | bytes 10485760 | tf_op jit(solution)/shard_map/pallas_call | solution.py:171
  101.9 5.1 %collective-permute-start.12 = (bf16[4,1024,256]{2,1,0:T(8,128)(2,1)}, bf16[4,1024,256]{2,1,0:T(8,128)(2,1)S(1)}, u32[]{:S(2)}, u32[]{:S(2)}) collective-permute-start(bf16[4,1024,256]{2,1,0:T(8,128)(2,1)} %shard_map.70), channel_id=1, source_target_pairs={{0,1},{1,0},{2,3},{3,2},{4,5},{5,4},{6,7},{7,6},{8,9},{9,8},{10,11... | collective-permute-start | bytes 6291464 | tf_op jit(solution)/shard_map/ppermute | solution.py:57
  107.7 9.7 %shard_map.69 = bf16[4,1024,256]{2,1,0:T(8,128)(2,1)} custom-call(s32[5]{0:T(128)} %stack.49.scalars, bf16[1024,1024]{1,0:T(8,128)(2,1)} %refs_0_.3, bf16[1024,1024]{1,0:T(8,128)(2,1)} %collective-permute-done.8.refs_1_, bf16[1024,1024]{1,0:T(8,128)(2,1)} %collective-permute-done.6.refs_0_.refs_2_, ...), custom_call_target="tpu_custom_call", output_to_operand_aliasing={{}: (13, {})} | custom-call | flops 2684354560 | bytes 10485760 | tf_op jit(solution)/shard_map/pallas_call | solution.py:171
  117.4 2.2 %fusion = (bf16[1024,256]{1,0:T(8,128)(2,1)S(1)}, bf16[1024,256]{1,0:T(8,128)(2,1)S(1)}, bf16[1024,256]{1,0:T(8,128)(2,1)S(1)}, bf16[1024,256]{1,0:T(8,128)(2,1)S(1)}) fusion(bf16[4,1024,256]{2,1,0:T(8,128)(2,1)S(1)} %collective-permute-done.12, bf16[4,1024,256]{2,1,0:T(8,128)(2,1)} %shard_map.69), kind=kLoop, calls=%fused_computation.6 | loop fusion | flops 4194304 | bytes 6291456 | tf_op jit(solution)/shard_map/convert_element_type | solution.py:236
  119.8 2.0 %collective-permute-start.13 = (bf16[1024,256]{1,0:T(8,128)(2,1)S(1)}, bf16[1024,256]{1,0:T(8,128)(2,1)S(1)}, u32[]{:S(2)}, u32[]{:S(2)}) collective-permute-start(bf16[1024,256]{1,0:T(8,128)(2,1)S(1)} %get-tuple-element.14), channel_id=1, source_target_pairs={{0,12},{1,20},{2,14},{3,22},{4,0},{5,24},{6,2},{7,26},{8,4},{9,28}... | collective-permute-start | bytes 1572872 | tf_op jit(solution)/shard_map/ppermute | solution.py:57
  121.8 1.5 collective-permute-start.14
  123.2 8.2 %collective-permute-done.15 = bf16[1024,256]{1,0:T(8,128)(2,1)S(1)} collective-permute-done((bf16[1024,256]{1,0:T(8,128)(2,1)S(1)}, bf16[1024,256]{1,0:T(8,128)(2,1)S(1)}, u32[]{:S(2)}, u32[]{:S(2)}) %collective-permute-start.15) | collective-permute-done | bytes 524320 | tf_op jit(solution)/shard_map/ppermute | solution.py:57
  131.8 9.4 %collective-permute-done.16 = bf16[1024,256]{1,0:T(8,128)(2,1)S(1)} collective-permute-done((bf16[1024,256]{1,0:T(8,128)(2,1)S(1)}, bf16[1024,256]{1,0:T(8,128)(2,1)S(1)}, u32[]{:S(2)}, u32[]{:S(2)}) %collective-permute-start.16) | collective-permute-done | bytes 524320 | tf_op jit(solution)/shard_map/ppermute | solution.py:57
  141.2 1.4 select_convert_fusion
  143.0 4.3 %collective-permute-done.17 = bf16[128,256]{1,0:T(8,128)(2,1)S(1)} collective-permute-done((bf16[128,256]{1,0:T(8,128)(2,1)S(1)}, bf16[128,256]{1,0:T(8,128)(2,1)S(1)}, u32[]{:S(2)}, u32[]{:S(2)}) %collective-permute-start.17) | collective-permute-done | bytes 65568 | tf_op jit(solution)/shard_map/ppermute | solution.py:57
  147.4 4.9 %collective-permute-done.18 = bf16[128,256]{1,0:T(8,128)(2,1)S(1)} collective-permute-done((bf16[128,256]{1,0:T(8,128)(2,1)S(1)}, bf16[128,256]{1,0:T(8,128)(2,1)S(1)}, u32[]{:S(2)}, u32[]{:S(2)}) %collective-permute-start.18) | collective-permute-done | bytes 65568 | tf_op jit(solution)/shard_map/ppermute | solution.py:57
  152.5 5.2 %collective-permute-done.19 = bf16[128,256]{1,0:T(8,128)(2,1)S(1)} collective-permute-done((bf16[128,256]{1,0:T(8,128)(2,1)S(1)}, bf16[128,256]{1,0:T(8,128)(2,1)S(1)}, u32[]{:S(2)}, u32[]{:S(2)}) %collective-permute-start.19) | collective-permute-done | bytes 65568 | tf_op jit(solution)/shard_map/ppermute | solution.py:57
  157.7 2.5 %collective-permute-start.20 = (bf16[128,256]{1,0:T(8,128)(2,1)S(1)}, bf16[128,256]{1,0:T(8,128)(2,1)S(1)}, u32[]{:S(2)}, u32[]{:S(2)}) collective-permute-start(bf16[128,256]{1,0:T(8,128)(2,1)S(1)} %add_convert_fusion.6), channel_id=1, source_target_pairs={{0,224},{1,225},{2,226},{3,227},{4,228},{5,229},{6,230},{7,231},{8... | collective-permute-start | bytes 196616 | tf_op jit(solution)/shard_map/ppermute | solution.py:57
  160.2 3.7 %collective-permute-done.20 = bf16[128,256]{1,0:T(8,128)(2,1)S(1)} collective-permute-done((bf16[128,256]{1,0:T(8,128)(2,1)S(1)}, bf16[128,256]{1,0:T(8,128)(2,1)S(1)}, u32[]{:S(2)}, u32[]{:S(2)}) %collective-permute-start.20) | collective-permute-done | bytes 65568 | tf_op jit(solution)/shard_map/ppermute | solution.py:57
  164.0 4.3 %collective-permute-done.21 = bf16[128,256]{1,0:T(8,128)(2,1)S(1)} collective-permute-done((bf16[128,256]{1,0:T(8,128)(2,1)S(1)}, bf16[128,256]{1,0:T(8,128)(2,1)S(1)}, u32[]{:S(2)}, u32[]{:S(2)}) %collective-permute-start.21) | collective-permute-done | bytes 65568 | tf_op jit(solution)/shard_map/ppermute | solution.py:57
  168.2 0.7 convert_subtract_fusion
  (55 shorter events, 4.9 us)
Async XLA Ops:
  0.6 0.7 copy-start
  3.6 81.1 %copy-start.6 = (bf16[1024,256]{1,0:T(8,128)(2,1)}, bf16[1024,256]{1,0:T(8,128)(2,1)S(1)}, u32[]{:S(2)}) copy-start(bf16[1024,256]{1,0:T(8,128)(2,1)S(1)} %bitcast_select_fusion) | copy-start | bytes 1572868
  3.6 5.2 %collective-permute-start = (bf16[1024,256]{1,0:T(8,128)(2,1)S(1)}, bf16[1024,256]{1,0:T(8,128)(2,1)S(1)}, u32[]{:S(2)}, u32[]{:S(2)}) collective-permute-start(bf16[1024,256]{1,0:T(8,128)(2,1)S(1)} %bitcast_select_fusion), channel_id=1, source_target_pairs={{0,0},{1,16},{2,2},{3,18},{4,4},{5,20},{6,6},{7,22},{8,8},{9,24},{... | collective-permute-start | bytes 1572872 | tf_op jit(solution)/shard_map/ppermute | solution.py:57
  4.3 63.4 %collective-permute-start.7 = (bf16[1024,1024]{1,0:T(8,128)(2,1)}, bf16[1024,1024]{1,0:T(8,128)(2,1)S(1)}, u32[]{:S(2)}, u32[]{:S(2)}) collective-permute-start(bf16[1024,1024]{1,0:T(8,128)(2,1)} %refs_0_.3), channel_id=1, source_target_pairs={{0,18},{1,17},{2,16},{3,19},{4,22},{5,21},{6,20},{7,23},{8,26},{9,... | collective-permute-start | bytes 6291464 | tf_op jit(solution)/shard_map/ppermute | solution.py:57
  8.8 58.9 %collective-permute-start.6 = (bf16[1024,1024]{1,0:T(8,128)(2,1)}, bf16[1024,1024]{1,0:T(8,128)(2,1)}, u32[]{:S(2)}, u32[]{:S(2)}) collective-permute-start(bf16[1024,1024]{1,0:T(8,128)(2,1)} %refs_0_.3), channel_id=1, source_target_pairs={{0,16},{1,19},{2,18},{3,17},{4,20},{5,23},{6,22},{7,21},{8,24},{9,... | collective-permute-start | bytes 6291464 | tf_op jit(solution)/shard_map/ppermute | solution.py:57
  8.8 25.8 %collective-permute-start.1 = (bf16[1024,256]{1,0:T(8,128)(2,1)S(1)}, bf16[1024,256]{1,0:T(8,128)(2,1)S(1)}, u32[]{:S(2)}, u32[]{:S(2)}) collective-permute-start(bf16[1024,256]{1,0:T(8,128)(2,1)S(1)} %collective-permute-done), channel_id=1, source_target_pairs={{0,0},{1,1},{2,2},{3,3},{4,64},{5,65},{6,66},{7,67},{8,128},{9,129... | collective-permute-start | bytes 1572872 | tf_op jit(solution)/shard_map/ppermute | solution.py:57
  34.6 51.5 %copy-start.2 = (bf16[1024,256]{1,0:T(8,128)(2,1)}, bf16[1024,256]{1,0:T(8,128)(2,1)S(1)}, u32[]{:S(2)}) copy-start(bf16[1024,256]{1,0:T(8,128)(2,1)S(1)} %collective-permute-done.1.refs_2_.refs_4_) | copy-start | bytes 1572868
  34.6 11.5 %collective-permute-start.4 = (bf16[1024,256]{1,0:T(8,128)(2,1)S(1)}, bf16[1024,256]{1,0:T(8,128)(2,1)S(1)}, u32[]{:S(2)}, u32[]{:S(2)}) collective-permute-start(bf16[1024,256]{1,0:T(8,128)(2,1)S(1)} %collective-permute-done.1.refs_2_.refs_4_), channel_id=1, source_target_pairs={{0,224},{1,33},{2,226},{3,35},{4,228},{5,37},{6,230},{7,39},{8,232... | collective-permute-start | bytes 1572872 | tf_op jit(solution)/shard_map/ppermute | solution.py:57
  34.6 18.5 %collective-permute-start.2 = (bf16[1024,256]{1,0:T(8,128)(2,1)S(1)}, bf16[1024,256]{1,0:T(8,128)(2,1)S(1)}, u32[]{:S(2)}, u32[]{:S(2)}) collective-permute-start(bf16[1024,256]{1,0:T(8,128)(2,1)S(1)} %collective-permute-done.1.refs_2_.refs_4_), channel_id=1, source_target_pairs={{0,32},{1,225},{2,34},{3,227},{4,36},{5,229},{6,38},{7,231},{8,40}... | collective-permute-start | bytes 1572872 | tf_op jit(solution)/shard_map/ppermute | solution.py:57
  46.1 40.0 %copy-start.3 = (bf16[1024,256]{1,0:T(8,128)(2,1)}, bf16[1024,256]{1,0:T(8,128)(2,1)S(1)}, u32[]{:S(2)}) copy-start(bf16[1024,256]{1,0:T(8,128)(2,1)S(1)} %collective-permute-done.4.refs_4_.refs_6_) | copy-start | bytes 1572868
  46.1 13.6 %collective-permute-start.5 = (bf16[1024,256]{1,0:T(8,128)(2,1)S(1)}, bf16[1024,256]{1,0:T(8,128)(2,1)}, u32[]{:S(2)}, u32[]{:S(2)}) collective-permute-start(bf16[1024,256]{1,0:T(8,128)(2,1)S(1)} %collective-permute-done.4.refs_4_.refs_6_), channel_id=1, source_target_pairs={{0,224},{1,33},{2,226},{3,35},{4,228},{5,37},{6,230},{7,39},{8,232... | collective-permute-start | bytes 1572872 | tf_op jit(solution)/shard_map/ppermute | solution.py:57
  53.2 14.5 %copy-start.4 = (bf16[1024,256]{1,0:T(8,128)(2,1)}, bf16[1024,256]{1,0:T(8,128)(2,1)S(1)}, u32[]{:S(2)}) copy-start(bf16[1024,256]{1,0:T(8,128)(2,1)S(1)} %collective-permute-done.2.refs_3_.refs_5_) | copy-start | bytes 1572868
  53.2 14.5 %collective-permute-start.3 = (bf16[1024,256]{1,0:T(8,128)(2,1)S(1)}, bf16[1024,256]{1,0:T(8,128)(2,1)S(1)}, u32[]{:S(2)}, u32[]{:S(2)}) collective-permute-start(bf16[1024,256]{1,0:T(8,128)(2,1)S(1)} %collective-permute-done.2.refs_3_.refs_5_), channel_id=1, source_target_pairs={{0,32},{1,225},{2,34},{3,227},{4,36},{5,229},{6,38},{7,231},{8,40}... | collective-permute-start | bytes 1572872 | tf_op jit(solution)/shard_map/ppermute | solution.py:57
  67.7 0.8 copy-start.5
  67.7 18.4 %copy-start.1 = (bf16[1024,1024]{1,0:T(8,128)(2,1)}, bf16[1024,1024]{1,0:T(8,128)(2,1)S(1)}, u32[]{:S(2)}) copy-start(bf16[1024,1024]{1,0:T(8,128)(2,1)S(1)} %collective-permute-done.7.refs_1_.refs_3_) | copy-start | bytes 6291460
  67.7 28.3 %collective-permute-start.8 = (bf16[1024,1024]{1,0:T(8,128)(2,1)S(1)}, bf16[1024,1024]{1,0:T(8,128)(2,1)}, u32[]{:S(2)}, u32[]{:S(2)}) collective-permute-start(bf16[1024,1024]{1,0:T(8,128)(2,1)S(1)} %collective-permute-done.7.refs_1_.refs_3_), channel_id=1, source_target_pairs={{0,16},{1,19},{2,18},{3,17},{4,20},{5,23},{6,22},{7,21},{8,24},{9,... | collective-permute-start | bytes 6291464 | tf_op jit(solution)/shard_map/ppermute | solution.py:57
  68.5 16.2 %collective-permute-start.9 = (bf16[1024,256]{1,0:T(8,128)(2,1)S(1)}, bf16[1024,256]{1,0:T(8,128)(2,1)}, u32[]{:S(2)}, u32[]{:S(2)}) collective-permute-start(bf16[1024,256]{1,0:T(8,128)(2,1)S(1)} %collective-permute-done.3.refs_5_.refs_7_), channel_id=1, source_target_pairs={{0,32},{1,225},{2,34},{3,227},{4,36},{5,229},{6,38},{7,231},{8,40}... | collective-permute-start | bytes 1572872 | tf_op jit(solution)/shard_map/ppermute | solution.py:57
  68.5 17.6 %collective-permute-start.10 = (bf16[1024,256]{1,0:T(8,128)(2,1)}, bf16[1024,256]{1,0:T(8,128)(2,1)}, u32[]{:S(2)}, u32[]{:S(2)}) collective-permute-start(bf16[1024,256]{1,0:T(8,128)(2,1)} %collective-permute-done.5.refs_6_.refs_8_), channel_id=1, source_target_pairs={{0,224},{1,33},{2,226},{3,35},{4,228},{5,37},{6,230},{7,39},{8,232... | collective-permute-start | bytes 1572872 | tf_op jit(solution)/shard_map/ppermute | solution.py:57
  84.7 11.3 %collective-permute-start.11 = (bf16[1024,256]{1,0:T(8,128)(2,1)}, bf16[1024,256]{1,0:T(8,128)(2,1)}, u32[]{:S(2)}, u32[]{:S(2)}) collective-permute-start(bf16[1024,256]{1,0:T(8,128)(2,1)} %collective-permute-done.9.refs_7_.refs_9_), channel_id=1, source_target_pairs={{0,32},{1,225},{2,34},{3,227},{4,36},{5,229},{6,38},{7,231},{8,40}... | collective-permute-start | bytes 1572872 | tf_op jit(solution)/shard_map/ppermute | solution.py:57
  101.9 15.5 %collective-permute-start.12 = (bf16[4,1024,256]{2,1,0:T(8,128)(2,1)}, bf16[4,1024,256]{2,1,0:T(8,128)(2,1)S(1)}, u32[]{:S(2)}, u32[]{:S(2)}) collective-permute-start(bf16[4,1024,256]{2,1,0:T(8,128)(2,1)} %shard_map.70), channel_id=1, source_target_pairs={{0,1},{1,0},{2,3},{3,2},{4,5},{5,4},{6,7},{7,6},{8,9},{9,8},{10,11... | collective-permute-start | bytes 6291464 | tf_op jit(solution)/shard_map/ppermute | solution.py:57
  119.7 22.9 %copy-start.7 = (bf16[1024,256]{1,0:T(8,128)(2,1)S(1)}, bf16[1024,256]{1,0:T(8,128)(2,1)}, u32[]{:S(2)}) copy-start(bf16[1024,256]{1,0:T(8,128)(2,1)} %copy-done.6) | copy-start | bytes 1572868
  119.7 11.8 %collective-permute-start.15 = (bf16[1024,256]{1,0:T(8,128)(2,1)S(1)}, bf16[1024,256]{1,0:T(8,128)(2,1)S(1)}, u32[]{:S(2)}, u32[]{:S(2)}) collective-permute-start(bf16[1024,256]{1,0:T(8,128)(2,1)S(1)} %get-tuple-element.15), channel_id=1, source_target_pairs={{0,4},{1,13},{2,6},{3,15},{4,8},{5,1},{6,10},{7,3},{8,12},{9,5},{1... | collective-permute-start | bytes 1572872 | tf_op jit(solution)/shard_map/ppermute | solution.py:57
  119.8 12.0 %collective-permute-start.13 = (bf16[1024,256]{1,0:T(8,128)(2,1)S(1)}, bf16[1024,256]{1,0:T(8,128)(2,1)S(1)}, u32[]{:S(2)}, u32[]{:S(2)}) collective-permute-start(bf16[1024,256]{1,0:T(8,128)(2,1)S(1)} %get-tuple-element.14), channel_id=1, source_target_pairs={{0,12},{1,20},{2,14},{3,22},{4,0},{5,24},{6,2},{7,26},{8,4},{9,28}... | collective-permute-start | bytes 1572872 | tf_op jit(solution)/shard_map/ppermute | solution.py:57
  121.8 10.0 %collective-permute-start.14 = (bf16[1024,256]{1,0:T(8,128)(2,1)S(1)}, bf16[1024,256]{1,0:T(8,128)(2,1)}, u32[]{:S(2)}, u32[]{:S(2)}) collective-permute-start(bf16[1024,256]{1,0:T(8,128)(2,1)S(1)} %get-tuple-element.17), channel_id=1, source_target_pairs={{0,0},{1,16},{2,2},{3,18},{4,4},{5,20},{6,6},{7,22},{8,8},{9,24},{... | collective-permute-start | bytes 1572872 | tf_op jit(solution)/shard_map/ppermute | solution.py:57
  131.6 9.6 %collective-permute-start.16 = (bf16[1024,256]{1,0:T(8,128)(2,1)S(1)}, bf16[1024,256]{1,0:T(8,128)(2,1)S(1)}, u32[]{:S(2)}, u32[]{:S(2)}) collective-permute-start(bf16[1024,256]{1,0:T(8,128)(2,1)S(1)} %add_convert_fusion), channel_id=1, source_target_pairs={{0,4},{1,28},{2,6},{3,30},{4,8},{5,16},{6,10},{7,18},{8,12},{9,20}... | collective-permute-start | bytes 1572872 | tf_op jit(solution)/shard_map/ppermute | solution.py:57
  131.8 36.5 %copy-start.9 = (f32[1,256,256]{2,1,0:T(8,128)S(1)}, f32[1,256,256]{2,1,0:T(8,128)}, u32[]{:S(2)}) copy-start(f32[1,256,256]{2,1,0:T(8,128)} %param.7) | copy-start | bytes 786436
  142.6 26.4 %copy-start.8 = (bf16[1024,256]{1,0:T(8,128)(2,1)}, bf16[1024,256]{1,0:T(8,128)(2,1)S(1)}, u32[]{:S(2)}) copy-start(bf16[1024,256]{1,0:T(8,128)(2,1)S(1)} %select_convert_fusion) | copy-start | bytes 1572868
  142.9 4.4 %collective-permute-start.17 = (bf16[128,256]{1,0:T(8,128)(2,1)S(1)}, bf16[128,256]{1,0:T(8,128)(2,1)S(1)}, u32[]{:S(2)}, u32[]{:S(2)}) collective-permute-start(bf16[128,256]{1,0:T(8,128)(2,1)S(1)} %select_convert_fusion.1), channel_id=1, source_target_pairs={{0,16},{1,17},{2,18},{3,19},{4,20},{5,21},{6,22},{7,23},{8,24},{9,... | collective-permute-start | bytes 196616 | tf_op jit(solution)/shard_map/ppermute | solution.py:57
  147.3 5.0 %collective-permute-start.18 = (bf16[128,256]{1,0:T(8,128)(2,1)S(1)}, bf16[128,256]{1,0:T(8,128)(2,1)S(1)}, u32[]{:S(2)}, u32[]{:S(2)}) collective-permute-start(bf16[128,256]{1,0:T(8,128)(2,1)S(1)} %add_convert_fusion.8), channel_id=1, source_target_pairs={{0,32},{1,33},{2,34},{3,35},{4,36},{5,37},{6,38},{7,39},{8,40},{9,... | collective-permute-start | bytes 196616 | tf_op jit(solution)/shard_map/ppermute | solution.py:57
  152.4 5.3 %collective-permute-start.19 = (bf16[128,256]{1,0:T(8,128)(2,1)S(1)}, bf16[128,256]{1,0:T(8,128)(2,1)S(1)}, u32[]{:S(2)}, u32[]{:S(2)}) collective-permute-start(bf16[128,256]{1,0:T(8,128)(2,1)S(1)} %add_convert_fusion.7), channel_id=1, source_target_pairs={{0,64},{1,65},{2,66},{3,67},{4,68},{5,69},{6,70},{7,71},{8,72},{9,... | collective-permute-start | bytes 196616 | tf_op jit(solution)/shard_map/ppermute | solution.py:57
  157.7 6.2 %collective-permute-start.20 = (bf16[128,256]{1,0:T(8,128)(2,1)S(1)}, bf16[128,256]{1,0:T(8,128)(2,1)S(1)}, u32[]{:S(2)}, u32[]{:S(2)}) collective-permute-start(bf16[128,256]{1,0:T(8,128)(2,1)S(1)} %add_convert_fusion.6), channel_id=1, source_target_pairs={{0,224},{1,225},{2,226},{3,227},{4,228},{5,229},{6,230},{7,231},{8... | collective-permute-start | bytes 196616 | tf_op jit(solution)/shard_map/ppermute | solution.py:57
  163.9 4.4 %collective-permute-start.21 = (bf16[128,256]{1,0:T(8,128)(2,1)S(1)}, bf16[128,256]{1,0:T(8,128)(2,1)S(1)}, u32[]{:S(2)}, u32[]{:S(2)}) collective-permute-start(bf16[128,256]{1,0:T(8,128)(2,1)S(1)} %add_convert_fusion.5), channel_id=1, source_target_pairs={{0,16},{1,17},{2,18},{3,19},{4,20},{5,21},{6,22},{7,23},{8,24},{9,... | collective-permute-start | bytes 196616 | tf_op jit(solution)/shard_map/ppermute | solution.py:57

commit v5 on v3

v5 whole, which is shorter than its diff:
```python
import functools

import jax
import jax.numpy as jnp
from jax import lax
from jax.experimental import pallas as pl
from jax.experimental.pallas import tpu as pltpu
from jax.sharding import PartitionSpec as P

BS = 128
VMEM_MIB = 32
NZ, NY_LO, NX, NY_HI, NCORE = 8, 2, 4, 2, 2
F32, BF16 = jnp.float32, jnp.bfloat16
AXES = ("prow", "pcol")


def device_index(z, ylo, x, yhi, core):
    return (2 * z + ylo) * 16 + 4 * x + 2 * yhi + core


def permutation(target):
    pairs = []
    for z in range(NZ):
        for ylo in range(NY_LO):
            for x in range(NX):
                for yhi in range(NY_HI):
                    for core in range(NCORE):
                        to = target(z, ylo, x, yhi, core)
                        if to is not None:
                            pairs.append((device_index(z, ylo, x, yhi, core), device_index(*to)))
    return pairs


L_TURN = permutation(lambda z, l, x, q, c: (2 * ((x - z // 2) % 4) + z % 2, l, z // 2, q, c))
CORE = permutation(lambda z, l, x, q, c: (z, l, x, q, 1 - c))
HOME = permutation(lambda z, l, x, q, c: (z, c, x, q, l))


def way(core):
    return 1 - 2 * core


Z_AHEAD = permutation(lambda z, l, x, q, c: ((z + way(c)) % 8, l, x, q, c))
Z_BACK = permutation(lambda z, l, x, q, c: ((z - way(c)) % 8, l, x, q, c))
Y_FIRST = permutation(lambda z, l, x, q, c: (z, 1 - l, x, q ^ c, c))
Y_SECOND = permutation(lambda z, l, x, q, c: (z, 1 - l, x, 1 - (q ^ c), c))
X_AHEAD = permutation(lambda z, l, x, q, c: (z, l, (x + way(c)) % 4, q, c))
X_AHEAD_HOME = permutation(lambda z, l, x, q, c: (z, c, (x + way(c)) % 4, q, l))
X_BACK_HOME = permutation(lambda z, l, x, q, c: (z, c, (x - way(c)) % 4, q, l))


def swap(z_bits, ylo_bit):
    return permutation(lambda z, l, x, q, c: (z ^ z_bits, l ^ ylo_bit, x, q, c))


def move(value, pairs):
    return lax.ppermute(value, AXES, pairs)


def local_flags(ancestors, block_slot, row, column):
    own = lax.dynamic_index_in_dim(ancestors, column, 0, keepdims=False)
    numbers = jnp.arange(block_slot.shape[0], dtype=jnp.int32)
    used = jnp.any(own[:, None] == numbers[None, :], axis=0)
    slots = row * 8 + jnp.arange(8, dtype=jnp.int32)
    return jnp.any(used[None, :] & (block_slot[None, :] == slots[:, None]), axis=1)


L_STEPS = (0, 1, -1, 2, -2, 3, -3, 4)


A_ROWS = 256


def product_kernel(early, scalars, *refs):
    if early:
        other_refs, l_refs, refs = refs[0:2], refs[2:9], refs[9:]
    else:
        own_refs, other_refs, l_refs, refs = refs[0:2], refs[2:4], refs[4:12], refs[14:]
    outs, (own_vmem, other_vmem, l_vmem, out_vmem, own_sem, other_sem, l_sem, out_sem) = refs[:2], refs[2:]
    z, half, side, own_order, other_order, other_out, core = (scalars[at] for at in range(7))

    def a_start(sources, target, sem, flip, tile):
        rows = pl.ds(A_ROWS * tile, A_ROWS)
        for at, source in enumerate(sources):
            columns = pl.ds(pl.multiple_of((at ^ flip) * 1024, 1024), 1024)
            pltpu.make_async_copy(source.at[rows], target.at[rows, columns], sem.at[tile]).start()

    def l_start(these):
        for parity, sign in ((0, -1), (1, 1)):
            pairs = ((0, sign), (2 * sign, 3 * sign), (-sign, -2 * sign), (-3 * sign, 4))

            @pl.when(side == parity)
            def _():
                for slot in these:
                    for step in pairs[slot]:
                        start = pl.multiple_of((half ^ (step % 2)) * 1024, 1024)
                        target = l_vmem.at[slot, pl.ds(start, 1024)]
                        pltpu.make_async_copy(l_refs[L_STEPS.index(step)], target, l_sem.at[slot]).start()

    def own_start(tile):
        a_start(own_refs, own_vmem, own_sem, 0, tile)

    def other_start(tile):
        a_start(other_refs, other_vmem, other_sem, core, tile)

    first_start = other_start if early else own_start
    first_start(0)
    l_start((0,))
    for tile in range(1, 4):
        first_start(tile)
    l_start((1, 2) if early else (1, 2, 3))
    if not early:
        for tile in range(4):
            other_start(tile)

    sign = 1 - 2 * lax.rem(z, 2)

    def multiply(a_vmem, a_sem, slot, result, order, which, wait_l=True):
        if wait_l:
            pltpu.make_async_copy(l_vmem.at[slot], l_vmem.at[slot], l_sem.at[slot]).wait()
        for tile in range(4):
            rows = pl.ds(A_ROWS * tile, A_ROWS)
            if a_sem is not None:
                pltpu.make_async_copy(a_vmem.at[rows], a_vmem.at[rows], a_sem.at[tile]).wait()
            total = jnp.dot(a_vmem[rows], l_vmem[slot], preferred_element_type=F32)
            out_vmem[result, rows] = total.astype(BF16)
        shift = jnp.where(slot == 1, sign, jnp.where(slot == 2, -sign, jnp.where(slot == 3, 2, 0)))
        j = lax.rem((z // 2 + shift + 4) * order, 4)
        for choice, out in enumerate(outs):
            @pl.when(which == choice)
            def _():
                pltpu.make_async_copy(out_vmem.at[result], out.at[j], out_sem.at[result]).start()

    if early:
        multiply(other_vmem, other_sem, 0, 0, other_order, other_out)
        pl.loop(1, 3)(lambda slot: multiply(other_vmem, None, slot, slot, other_order, other_out))
    else:
        multiply(own_vmem, own_sem, 0, 0, own_order, 1 - other_out)
        pl.loop(1, 4)(lambda slot: multiply(own_vmem, None, slot, slot, own_order, 1 - other_out))
        multiply(other_vmem, other_sem, 3, 4, other_order, other_out, wait_l=False)
    for result in range(3 if early else 5):
        pltpu.make_async_copy(out_vmem.at[result], outs[0].at[0], out_sem.at[result]).wait()


def product_call(early, scalars, *arrays):
    anywhere = pl.BlockSpec(memory_space=pl.ANY)
    block = jax.ShapeDtypeStruct((4, 1024, 256), BF16)
    slots = 3 if early else 5
    return pl.pallas_call(
        functools.partial(product_kernel, early),
        in_specs=[pl.BlockSpec(memory_space=pltpu.SMEM)] + [anywhere] * len(arrays),
        out_specs=(anywhere, anywhere),
        out_shape=(block, block),
        scratch_shapes=[
            pltpu.VMEM((1024, 2048), BF16),
            pltpu.VMEM((1024, 2048), BF16),
            pltpu.VMEM((4, 2048, 256), BF16),
            pltpu.VMEM((5, 1024, 256), BF16),
            pltpu.SemaphoreType.DMA((4,)),
            pltpu.SemaphoreType.DMA((4,)),
            pltpu.SemaphoreType.DMA((4,)),
            pltpu.SemaphoreType.DMA((5,)),
        ],
        input_output_aliases={} if early else {len(arrays) - 1: 0, len(arrays): 1},
        compiler_params=pltpu.CompilerParams(vmem_limit_bytes=VMEM_MIB * 2**20),
        cost_estimate=pl.CostEstimate(
            flops=slots * 2 * 1024 * 2048 * 256, bytes_accessed=10 * 2**20, transcendentals=0
        ),
    )(scalars, *arrays)


def products_early(scalars, a_pieces, l_pieces):
    return product_call(True, scalars, *a_pieces, *l_pieces)


def products(scalars, a_pieces, l_pieces, outs):
    return product_call(False, scalars, *a_pieces, *l_pieces, *outs)


def body(ainv, l_panels, dinv, ancestors, block_slot):
    row = lax.axis_index("prow")
    column = lax.axis_index("pcol")
    z, ylo = row // 2, row % 2
    x, yhi, core = column // 4, (column // 2) % 2, column % 2

    flags = jnp.repeat(local_flags(ancestors, block_slot, row, column), BS)[:, None]
    masked = jnp.where(flags, l_panels[0], jnp.zeros((), BF16))

    here = move(move(masked, HOME), L_TURN)
    first_y = move(ainv, Y_FIRST)
    second_y = move(ainv, Y_SECOND)

    l_pieces = [here]
    ahead = back = here
    for _ in range(2):
        ahead, back = move(ahead, Z_AHEAD), move(back, Z_BACK)
        l_pieces += [ahead, back]
    ahead, back, first_y, second_y = lax.optimization_barrier((ahead, back, first_y, second_y))
    across = move(second_y, Y_FIRST)
    ahead, back = move(ahead, Z_AHEAD), move(back, Z_BACK)
    l_pieces += [ahead, back]

    given_is_other = (ylo == core).astype(jnp.int32)
    own_core, other_core = jnp.where(given_is_other == 1, jnp.stack([core, 1 - core]), jnp.stack([1 - core, core]))
    scalars = [z, (z % 2) ^ yhi, (z % 2) ^ core, 1 + 2 * own_core, 1 + 2 * other_core, given_is_other, core]
    scalars = jnp.stack(scalars).astype(jnp.int32)
    outs = products_early(scalars, (first_y, second_y), l_pieces)
    l_pieces.append(move(ahead, Z_AHEAD))
    kept, given = products(scalars, (ainv, across, first_y, second_y), l_pieces, outs)
    taken = move(given, CORE)

    def block_sum(j):
        return (kept[j].astype(F32) + taken[j].astype(F32)).astype(BF16)

    sum_2, kept, taken = lax.optimization_barrier((block_sum(2), kept, taken))
    sum_3, sum_0, kept, taken = lax.optimization_barrier((block_sum(3), block_sum(0), kept, taken))
    sum_1 = lax.optimization_barrier(block_sum(1))

    relayed = move(sum_2, X_AHEAD)
    total = move(sum_3, X_BACK_HOME).astype(F32) + move(sum_0, HOME).astype(F32)
    total += move((sum_1.astype(F32) + relayed.astype(F32)).astype(BF16), X_AHEAD_HOME).astype(F32)
    inverse_column = jnp.where(flags, -total, jnp.zeros((), F32)).astype(BF16)

    terms = lax.dot_general(masked, inverse_column, (((0,), (0,)), ((), ())), preferred_element_type=F32)
    other = jnp.where(ylo == 0, terms[128:], terms[:128]).astype(BF16)
    half = jnp.where(ylo == 0, terms[:128], terms[128:]) + move(other, swap(0, 1)).astype(F32)
    for bits in (1, 2, 7):
        half = half.astype(BF16)
        half = half.astype(F32) + move(half, swap(bits, 0)).astype(F32)
    half = half.astype(BF16)
    other = move(half, swap(0, 1))
    terms = jnp.concatenate([jnp.where(ylo == 0, half, other), jnp.where(ylo == 0, other, half)], axis=0)
    return inverse_column[None], dinv - terms.astype(F32)[None]


def solution(mesh):
    return jax.shard_map(
        body,
        mesh=mesh,
        in_specs=(P("prow", "pcol"), P("pcol", "prow", None), P("pcol", None, None), P(), P()),
        out_specs=(P("pcol", "prow", None), P("pcol", None, None)),
        check_vma=False,
    )
```

time: 177 us -> 168 us (0.949)
  starting transfers between devices: 39.8 us -> 33.3 us
  other arithmetic: 9.15 us -> 5.12 us
    ppermute x22, starting transfers between devices: 39.8 us -> 33.3 us  [move(): return lax.ppermute(value, AXES, pairs)]
    convert_element_type x2 -> x4, other arithmetic: 4.61 us -> 0.69 us  [the longest x3 0.55 us: block_sum(): return (kept[j].astype(F32) + taken[j].astype(F32)).astype(BF16)]
  transfers between devices with their start and end apart: 22 -> 22, of which waited for: 14 -> 15; matrix products, arithmetic and copies ran while one was open for 2% -> 1% of each run, Pallas kernels for 6% -> 4%
where the time goes in v5:
time: 168 us; the launch traced here: 166 us
  waiting for transfers between devices  103 us (61%)
  starting transfers between devices  33.3 us (20%)
  Pallas kernels  18.6 us (11%)
  other arithmetic  5.12 us (3%)
  local copies, waits for them, and re-layouts  3.44 us (2%)
  between operations  2.09 us (1%)
    ppermute x22, waiting for transfers between devices, move(): return lax.ppermute(value, AXES, pairs)  103 us
    ppermute x22, starting transfers between devices, move(): return lax.ppermute(value, AXES, pairs)  33.3 us
    pallas_call x2, Pallas kernels, product_call(): pl.pallas_call(functools.partial(product_kernel, early), in_specs=[pl.Blo...  18.6 us
  transfers between devices with their start and end apart: 22, of which 15 were waited for; matrix products, arithmetic and copies ran while one was open for 1% of the time, Pallas kernels for 4%

profile of v5, /device:TPU:2, one launch (start us, length us, event | category | flops | bytes accessed | tf_op | source)
XLA Modules:
  0.0 165.8 jit_solution(4265075798674594598)
XLA Ops:
  1.4 0.8 and_reduce_fusion
  2.4 1.2 bitcast_select_fusion
  4.3 2.9 %collective-permute-start.6 = (bf16[1024,1024]{1,0:T(8,128)(2,1)}, bf16[1024,1024]{1,0:T(8,128)(2,1)S(1)}, u32[]{:S(2)}, u32[]{:S(2)}) collective-permute-start(bf16[1024,1024]{1,0:T(8,128)(2,1)} %refs_0_.1), channel_id=1, source_target_pairs={{0,16},{1,19},{2,18},{3,17},{4,20},{5,23},{6,22},{7,21},{8,24},{9,... | collective-permute-start | bytes 6291464 | tf_op jit(solution)/shard_map/ppermute | solution.py:57
  7.2 1.7 %collective-permute-start.7 = (bf16[1024,1024]{1,0:T(8,128)(2,1)}, bf16[1024,1024]{1,0:T(8,128)(2,1)}, u32[]{:S(2)}, u32[]{:S(2)}) collective-permute-start(bf16[1024,1024]{1,0:T(8,128)(2,1)} %refs_0_.1), channel_id=1, source_target_pairs={{0,18},{1,17},{2,16},{3,19},{4,22},{5,21},{6,20},{7,23},{8,26},{9,... | collective-permute-start | bytes 6291464 | tf_op jit(solution)/shard_map/ppermute | solution.py:57
  8.9 5.1 %collective-permute-start.1 = (bf16[1024,256]{1,0:T(8,128)(2,1)S(1)}, bf16[1024,256]{1,0:T(8,128)(2,1)S(1)}, u32[]{:S(2)}, u32[]{:S(2)}) collective-permute-start(bf16[1024,256]{1,0:T(8,128)(2,1)S(1)} %collective-permute-done), channel_id=1, source_target_pairs={{0,0},{1,1},{2,2},{3,3},{4,64},{5,65},{6,66},{7,67},{8,128},{9,129... | collective-permute-start | bytes 1572872 | tf_op jit(solution)/shard_map/ppermute | solution.py:57
  14.1 21.1 %collective-permute-done.1.refs_2_.refs_4_ = bf16[1024,256]{1,0:T(8,128)(2,1)S(1)} collective-permute-done((bf16[1024,256]{1,0:T(8,128)(2,1)S(1)}, bf16[1024,256]{1,0:T(8,128)(2,1)S(1)}, u32[]{:S(2)}, u32[]{:S(2)}) %collective-permute-start.1) | collective-permute-done | bytes 524320 | tf_op jit(solution)/shard_map/ppermute | solution.py:57
  35.2 2.0 %collective-permute-start.2 = (bf16[1024,256]{1,0:T(8,128)(2,1)S(1)}, bf16[1024,256]{1,0:T(8,128)(2,1)S(1)}, u32[]{:S(2)}, u32[]{:S(2)}) collective-permute-start(bf16[1024,256]{1,0:T(8,128)(2,1)S(1)} %collective-permute-done.1.refs_2_.refs_4_), channel_id=1, source_target_pairs={{0,32},{1,225},{2,34},{3,227},{4,36},{5,229},{6,38},{7,231},{8,40}... | collective-permute-start | bytes 1572872 | tf_op jit(solution)/shard_map/ppermute | solution.py:57
  37.2 10.0 %collective-permute-done.4.refs_4_.refs_6_ = bf16[1024,256]{1,0:T(8,128)(2,1)S(1)} collective-permute-done((bf16[1024,256]{1,0:T(8,128)(2,1)S(1)}, bf16[1024,256]{1,0:T(8,128)(2,1)S(1)}, u32[]{:S(2)}, u32[]{:S(2)}) %collective-permute-start.4) | collective-permute-done | bytes 524320 | tf_op jit(solution)/shard_map/ppermute | solution.py:57
  47.2 4.9 %collective-permute-start.5 = (bf16[1024,256]{1,0:T(8,128)(2,1)S(1)}, bf16[1024,256]{1,0:T(8,128)(2,1)}, u32[]{:S(2)}, u32[]{:S(2)}) collective-permute-start(bf16[1024,256]{1,0:T(8,128)(2,1)S(1)} %collective-permute-done.4.refs_4_.refs_6_), channel_id=1, source_target_pairs={{0,224},{1,33},{2,226},{3,35},{4,228},{5,37},{6,230},{7,39},{8,232... | collective-permute-start | bytes 1572872 | tf_op jit(solution)/shard_map/ppermute | solution.py:57
  52.1 1.2 collective-permute-done.2.refs_3_.refs_5_
  54.2 7.8 %collective-permute-done.5.refs_6_.refs_8_ = bf16[1024,256]{1,0:T(8,128)(2,1)} collective-permute-done((bf16[1024,256]{1,0:T(8,128)(2,1)S(1)}, bf16[1024,256]{1,0:T(8,128)(2,1)}, u32[]{:S(2)}, u32[]{:S(2)}) %collective-permute-start.5) | collective-permute-done | bytes 524320 | tf_op jit(solution)/shard_map/ppermute | solution.py:57
  62.0 5.7 %collective-permute-done.3.refs_5_.refs_7_ = bf16[1024,256]{1,0:T(8,128)(2,1)} collective-permute-done((bf16[1024,256]{1,0:T(8,128)(2,1)S(1)}, bf16[1024,256]{1,0:T(8,128)(2,1)}, u32[]{:S(2)}, u32[]{:S(2)}) %collective-permute-start.3) | collective-permute-done | bytes 524320 | tf_op jit(solution)/shard_map/ppermute | solution.py:57
  67.7 4.0 %collective-permute-start.8 = (bf16[1024,1024]{1,0:T(8,128)(2,1)}, bf16[1024,1024]{1,0:T(8,128)(2,1)}, u32[]{:S(2)}, u32[]{:S(2)}) collective-permute-start(bf16[1024,1024]{1,0:T(8,128)(2,1)} %collective-permute-done.7.refs_1_.refs_3_), channel_id=1, source_target_pairs={{0,16},{1,19},{2,18},{3,17},{4,20},{5,23},{6,22},{7,21},{8,24},{9,... | collective-permute-start | bytes 6291464 | tf_op jit(solution)/shard_map/ppermute | solution.py:57
  71.6 3.2 %collective-permute-start.10 = (bf16[1024,256]{1,0:T(8,128)(2,1)}, bf16[1024,256]{1,0:T(8,128)(2,1)}, u32[]{:S(2)}, u32[]{:S(2)}) collective-permute-start(bf16[1024,256]{1,0:T(8,128)(2,1)} %collective-permute-done.5.refs_6_.refs_8_), channel_id=1, source_target_pairs={{0,224},{1,33},{2,226},{3,35},{4,228},{5,37},{6,230},{7,39},{8,232... | collective-permute-start | bytes 1572872 | tf_op jit(solution)/shard_map/ppermute | solution.py:57
  74.9 13.0 %collective-permute-done.9.refs_7_.refs_9_ = bf16[1024,256]{1,0:T(8,128)(2,1)} collective-permute-done((bf16[1024,256]{1,0:T(8,128)(2,1)}, bf16[1024,256]{1,0:T(8,128)(2,1)}, u32[]{:S(2)}, u32[]{:S(2)}) %collective-permute-start.9) | collective-permute-done | bytes 524320 | tf_op jit(solution)/shard_map/ppermute | solution.py:57
  89.9 1.2 copy-done.3
  91.1 7.2 %shard_map.68 = (bf16[4,1024,256]{2,1,0:T(8,128)(2,1)S(1)}, bf16[4,1024,256]{2,1,0:T(8,128)(2,1)S(1)}) custom-call(s32[7]{0:T(128)S(1)} %stack.40.scalars, bf16[1024,1024]{1,0:T(8,128)(2,1)S(1)} %collective-permute-done.6.refs_0_.refs_2_, bf16[1024,1024]{1,0:T(8,128)(2,1)} %collective-permute-done.7.refs_1_.refs_3_, ...), custom_call_target="tpu_custom_call" | custom-call | flops 3221225472 | bytes 10485760 | tf_op jit(solution)/shard_map/pallas_call | solution.py:149
  98.6 11.5 %shard_map.69 = (bf16[4,1024,256]{2,1,0:T(8,128)(2,1)S(1)}, bf16[4,1024,256]{2,1,0:T(8,128)(2,1)S(1)}) custom-call(s32[7]{0:T(128)S(1)} %stack.40.scalars, bf16[1024,1024]{1,0:T(8,128)(2,1)S(1)} %copy-done.1, bf16[1024,1024]{1,0:T(8,128)(2,1)} %collective-permute-done.8.refs_1_, ...), custom_call_target="tpu_custom_call", output_to_operand_aliasing={{0}: (13, {}), {1}: (14, {})} | custom-call | flops 5368709120 | bytes 10485760 | tf_op jit(solution)/shard_map/pallas_call | solution.py:149
  110.2 4.1 %collective-permute-done.12 = bf16[4,1024,256]{2,1,0:T(8,128)(2,1)S(1)} collective-permute-done((bf16[4,1024,256]{2,1,0:T(8,128)(2,1)S(1)}, bf16[4,1024,256]{2,1,0:T(8,128)(2,1)S(1)}, u32[]{:S(2)}, u32[]{:S(2)}) %collective-permute-start.12) | collective-permute-done | bytes 2097184 | tf_op jit(solution)/shard_map/ppermute | solution.py:57
  114.5 1.1 collective-permute-start.15
  116.0 1.1 collective-permute-start.13
  117.8 10.9 %collective-permute-done.15 = bf16[1024,256]{1,0:T(8,128)(2,1)S(1)} collective-permute-done((bf16[1024,256]{1,0:T(8,128)(2,1)S(1)}, bf16[1024,256]{1,0:T(8,128)(2,1)S(1)}, u32[]{:S(2)}, u32[]{:S(2)}) %collective-permute-start.15) | collective-permute-done | bytes 524320 | tf_op jit(solution)/shard_map/ppermute | solution.py:57
  128.9 1.0 collective-permute-start.16
  129.9 8.3 %collective-permute-done.16 = bf16[1024,256]{1,0:T(8,128)(2,1)} collective-permute-done((bf16[1024,256]{1,0:T(8,128)(2,1)S(1)}, bf16[1024,256]{1,0:T(8,128)(2,1)}, u32[]{:S(2)}, u32[]{:S(2)}) %collective-permute-start.16) | collective-permute-done | bytes 524320 | tf_op jit(solution)/shard_map/ppermute | solution.py:57
  138.2 1.3 select_convert_fusion
  140.1 4.3 %collective-permute-done.17 = bf16[128,256]{1,0:T(8,128)(2,1)S(1)} collective-permute-done((bf16[128,256]{1,0:T(8,128)(2,1)S(1)}, bf16[128,256]{1,0:T(8,128)(2,1)S(1)}, u32[]{:S(2)}, u32[]{:S(2)}) %collective-permute-start.17) | collective-permute-done | bytes 65568 | tf_op jit(solution)/shard_map/ppermute | solution.py:57
  144.4 4.3 %collective-permute-done.18 = bf16[128,256]{1,0:T(8,128)(2,1)S(1)} collective-permute-done((bf16[128,256]{1,0:T(8,128)(2,1)S(1)}, bf16[128,256]{1,0:T(8,128)(2,1)S(1)}, u32[]{:S(2)}, u32[]{:S(2)}) %collective-permute-start.18) | collective-permute-done | bytes 65568 | tf_op jit(solution)/shard_map/ppermute | solution.py:57
  148.7 1.3 collective-permute-start.19
  150.0 4.4 %collective-permute-done.19 = bf16[128,256]{1,0:T(8,128)(2,1)S(1)} collective-permute-done((bf16[128,256]{1,0:T(8,128)(2,1)S(1)}, bf16[128,256]{1,0:T(8,128)(2,1)S(1)}, u32[]{:S(2)}, u32[]{:S(2)}) %collective-permute-start.19) | collective-permute-done | bytes 65568 | tf_op jit(solution)/shard_map/ppermute | solution.py:57
  154.4 3.2 %collective-permute-start.20 = (bf16[128,256]{1,0:T(8,128)(2,1)S(1)}, bf16[128,256]{1,0:T(8,128)(2,1)S(1)}, u32[]{:S(2)}, u32[]{:S(2)}) collective-permute-start(bf16[128,256]{1,0:T(8,128)(2,1)S(1)} %add_convert_fusion.6), channel_id=1, source_target_pairs={{0,224},{1,225},{2,226},{3,227},{4,228},{5,229},{6,230},{7,231},{8... | collective-permute-start | bytes 196616 | tf_op jit(solution)/shard_map/ppermute | solution.py:57
  157.6 3.1 %collective-permute-done.20 = bf16[128,256]{1,0:T(8,128)(2,1)S(1)} collective-permute-done((bf16[128,256]{1,0:T(8,128)(2,1)S(1)}, bf16[128,256]{1,0:T(8,128)(2,1)S(1)}, u32[]{:S(2)}, u32[]{:S(2)}) %collective-permute-start.20) | collective-permute-done | bytes 65568 | tf_op jit(solution)/shard_map/ppermute | solution.py:57
  160.8 4.3 %collective-permute-done.21 = bf16[128,256]{1,0:T(8,128)(2,1)S(1)} collective-permute-done((bf16[128,256]{1,0:T(8,128)(2,1)S(1)}, bf16[128,256]{1,0:T(8,128)(2,1)S(1)}, u32[]{:S(2)}, u32[]{:S(2)}) %collective-permute-start.21) | collective-permute-done | bytes 65568 | tf_op jit(solution)/shard_map/ppermute | solution.py:57
  (52 shorter events, 6.4 us)
Async XLA Ops:
  0.6 0.7 copy-start
  3.6 64.1 %copy-start.4 = (bf16[1024,256]{1,0:T(8,128)(2,1)}, bf16[1024,256]{1,0:T(8,128)(2,1)S(1)}, u32[]{:S(2)}) copy-start(bf16[1024,256]{1,0:T(8,128)(2,1)S(1)} %bitcast_select_fusion) | copy-start | bytes 1572868
  3.6 5.3 %collective-permute-start = (bf16[1024,256]{1,0:T(8,128)(2,1)S(1)}, bf16[1024,256]{1,0:T(8,128)(2,1)S(1)}, u32[]{:S(2)}, u32[]{:S(2)}) collective-permute-start(bf16[1024,256]{1,0:T(8,128)(2,1)S(1)} %bitcast_select_fusion), channel_id=1, source_target_pairs={{0,0},{1,16},{2,2},{3,18},{4,4},{5,20},{6,6},{7,22},{8,8},{9,24},{... | collective-permute-start | bytes 1572872 | tf_op jit(solution)/shard_map/ppermute | solution.py:57
  4.3 63.3 %collective-permute-start.6 = (bf16[1024,1024]{1,0:T(8,128)(2,1)}, bf16[1024,1024]{1,0:T(8,128)(2,1)S(1)}, u32[]{:S(2)}, u32[]{:S(2)}) collective-permute-start(bf16[1024,1024]{1,0:T(8,128)(2,1)} %refs_0_.1), channel_id=1, source_target_pairs={{0,16},{1,19},{2,18},{3,17},{4,20},{5,23},{6,22},{7,21},{8,24},{9,... | collective-permute-start | bytes 6291464 | tf_op jit(solution)/shard_map/ppermute | solution.py:57
  7.2 60.5 %collective-permute-start.7 = (bf16[1024,1024]{1,0:T(8,128)(2,1)}, bf16[1024,1024]{1,0:T(8,128)(2,1)}, u32[]{:S(2)}, u32[]{:S(2)}) collective-permute-start(bf16[1024,1024]{1,0:T(8,128)(2,1)} %refs_0_.1), channel_id=1, source_target_pairs={{0,18},{1,17},{2,16},{3,19},{4,22},{5,21},{6,20},{7,23},{8,26},{9,... | collective-permute-start | bytes 6291464 | tf_op jit(solution)/shard_map/ppermute | solution.py:57
  8.9 26.3 %collective-permute-start.1 = (bf16[1024,256]{1,0:T(8,128)(2,1)S(1)}, bf16[1024,256]{1,0:T(8,128)(2,1)S(1)}, u32[]{:S(2)}, u32[]{:S(2)}) collective-permute-start(bf16[1024,256]{1,0:T(8,128)(2,1)S(1)} %collective-permute-done), channel_id=1, source_target_pairs={{0,0},{1,1},{2,2},{3,3},{4,64},{5,65},{6,66},{7,67},{8,128},{9,129... | collective-permute-start | bytes 1572872 | tf_op jit(solution)/shard_map/ppermute | solution.py:57
  35.2 12.0 %collective-permute-start.4 = (bf16[1024,256]{1,0:T(8,128)(2,1)S(1)}, bf16[1024,256]{1,0:T(8,128)(2,1)S(1)}, u32[]{:S(2)}, u32[]{:S(2)}) collective-permute-start(bf16[1024,256]{1,0:T(8,128)(2,1)S(1)} %collective-permute-done.1.refs_2_.refs_4_), channel_id=1, source_target_pairs={{0,224},{1,33},{2,226},{3,35},{4,228},{5,37},{6,230},{7,39},{8,232... | collective-permute-start | bytes 1572872 | tf_op jit(solution)/shard_map/ppermute | solution.py:57
  35.2 18.1 %collective-permute-start.2 = (bf16[1024,256]{1,0:T(8,128)(2,1)S(1)}, bf16[1024,256]{1,0:T(8,128)(2,1)S(1)}, u32[]{:S(2)}, u32[]{:S(2)}) collective-permute-start(bf16[1024,256]{1,0:T(8,128)(2,1)S(1)} %collective-permute-done.1.refs_2_.refs_4_), channel_id=1, source_target_pairs={{0,32},{1,225},{2,34},{3,227},{4,36},{5,229},{6,38},{7,231},{8,40}... | collective-permute-start | bytes 1572872 | tf_op jit(solution)/shard_map/ppermute | solution.py:57
  47.2 14.8 %collective-permute-start.5 = (bf16[1024,256]{1,0:T(8,128)(2,1)S(1)}, bf16[1024,256]{1,0:T(8,128)(2,1)}, u32[]{:S(2)}, u32[]{:S(2)}) collective-permute-start(bf16[1024,256]{1,0:T(8,128)(2,1)S(1)} %collective-permute-done.4.refs_4_.refs_6_), channel_id=1, source_target_pairs={{0,224},{1,33},{2,226},{3,35},{4,228},{5,37},{6,230},{7,39},{8,232... | collective-permute-start | bytes 1572872 | tf_op jit(solution)/shard_map/ppermute | solution.py:57
  53.4 14.3 %collective-permute-start.3 = (bf16[1024,256]{1,0:T(8,128)(2,1)S(1)}, bf16[1024,256]{1,0:T(8,128)(2,1)}, u32[]{:S(2)}, u32[]{:S(2)}) collective-permute-start(bf16[1024,256]{1,0:T(8,128)(2,1)S(1)} %collective-permute-done.2.refs_3_.refs_5_), channel_id=1, source_target_pairs={{0,32},{1,225},{2,34},{3,227},{4,36},{5,229},{6,38},{7,231},{8,40}... | collective-permute-start | bytes 1572872 | tf_op jit(solution)/shard_map/ppermute | solution.py:57
  53.4 0.8 copy-start.2
  67.7 31.0 %collective-permute-start.8 = (bf16[1024,1024]{1,0:T(8,128)(2,1)}, bf16[1024,1024]{1,0:T(8,128)(2,1)}, u32[]{:S(2)}, u32[]{:S(2)}) collective-permute-start(bf16[1024,1024]{1,0:T(8,128)(2,1)} %collective-permute-done.7.refs_1_.refs_3_), channel_id=1, source_target_pairs={{0,16},{1,19},{2,18},{3,17},{4,20},{5,23},{6,22},{7,21},{8,24},{9,... | collective-permute-start | bytes 6291464 | tf_op jit(solution)/shard_map/ppermute | solution.py:57
  71.6 16.3 %collective-permute-start.9 = (bf16[1024,256]{1,0:T(8,128)(2,1)}, bf16[1024,256]{1,0:T(8,128)(2,1)}, u32[]{:S(2)}, u32[]{:S(2)}) collective-permute-start(bf16[1024,256]{1,0:T(8,128)(2,1)} %collective-permute-done.3.refs_5_.refs_7_), channel_id=1, source_target_pairs={{0,32},{1,225},{2,34},{3,227},{4,36},{5,229},{6,38},{7,231},{8,40}... | collective-permute-start | bytes 1572872 | tf_op jit(solution)/shard_map/ppermute | solution.py:57
  71.6 18.3 %collective-permute-start.10 = (bf16[1024,256]{1,0:T(8,128)(2,1)}, bf16[1024,256]{1,0:T(8,128)(2,1)}, u32[]{:S(2)}, u32[]{:S(2)}) collective-permute-start(bf16[1024,256]{1,0:T(8,128)(2,1)} %collective-permute-done.5.refs_6_.refs_8_), channel_id=1, source_target_pairs={{0,224},{1,33},{2,226},{3,35},{4,228},{5,37},{6,230},{7,39},{8,232... | collective-permute-start | bytes 1572872 | tf_op jit(solution)/shard_map/ppermute | solution.py:57
  87.9 10.7 %collective-permute-start.11 = (bf16[1024,256]{1,0:T(8,128)(2,1)}, bf16[1024,256]{1,0:T(8,128)(2,1)}, u32[]{:S(2)}, u32[]{:S(2)}) collective-permute-start(bf16[1024,256]{1,0:T(8,128)(2,1)} %collective-permute-done.9.refs_7_.refs_9_), channel_id=1, source_target_pairs={{0,32},{1,225},{2,34},{3,227},{4,36},{5,229},{6,38},{7,231},{8,40}... | collective-permute-start | bytes 1572872 | tf_op jit(solution)/shard_map/ppermute | solution.py:57
  89.9 8.7 %copy-start.1 = (bf16[1024,1024]{1,0:T(8,128)(2,1)S(1)}, bf16[1024,1024]{1,0:T(8,128)(2,1)}, u32[]{:S(2)}) copy-start(bf16[1024,1024]{1,0:T(8,128)(2,1)} %refs_0_.1) | copy-start | bytes 6291460
  89.9 1.2 copy-start.3
  110.1 4.2 %collective-permute-start.12 = (bf16[4,1024,256]{2,1,0:T(8,128)(2,1)S(1)}, bf16[4,1024,256]{2,1,0:T(8,128)(2,1)S(1)}, u32[]{:S(2)}, u32[]{:S(2)}) collective-permute-start(bf16[4,1024,256]{2,1,0:T(8,128)(2,1)S(1)} %get-tuple-element.24), channel_id=1, source_target_pairs={{0,1},{1,0},{2,3},{3,2},{4,5},{5,4},{6,7},{7,6},{8,9},{9,8},{10,11... | collective-permute-start | bytes 6291464 | tf_op jit(solution)/shard_map/ppermute | solution.py:57
  114.5 14.2 %collective-permute-start.15 = (bf16[1024,256]{1,0:T(8,128)(2,1)S(1)}, bf16[1024,256]{1,0:T(8,128)(2,1)S(1)}, u32[]{:S(2)}, u32[]{:S(2)}) collective-permute-start(bf16[1024,256]{1,0:T(8,128)(2,1)S(1)} %fusion), channel_id=1, source_target_pairs={{0,4},{1,13},{2,6},{3,15},{4,8},{5,1},{6,10},{7,3},{8,12},{9,5},{1... | collective-permute-start | bytes 1572872 | tf_op jit(solution)/shard_map/ppermute | solution.py:57
  116.0 23.6 %copy-start.5 = (bf16[1024,256]{1,0:T(8,128)(2,1)S(1)}, bf16[1024,256]{1,0:T(8,128)(2,1)}, u32[]{:S(2)}) copy-start(bf16[1024,256]{1,0:T(8,128)(2,1)} %copy-done.4) | copy-start | bytes 1572868
  116.0 13.9 %collective-permute-start.13 = (bf16[1024,256]{1,0:T(8,128)(2,1)S(1)}, bf16[1024,256]{1,0:T(8,128)(2,1)S(1)}, u32[]{:S(2)}, u32[]{:S(2)}) collective-permute-start(bf16[1024,256]{1,0:T(8,128)(2,1)S(1)} %get-tuple-element.27), channel_id=1, source_target_pairs={{0,12},{1,20},{2,14},{3,22},{4,0},{5,24},{6,2},{7,26},{8,4},{9,28}... | collective-permute-start | bytes 1572872 | tf_op jit(solution)/shard_map/ppermute | solution.py:57
  117.1 12.8 %collective-permute-start.14 = (bf16[1024,256]{1,0:T(8,128)(2,1)S(1)}, bf16[1024,256]{1,0:T(8,128)(2,1)S(1)}, u32[]{:S(2)}, u32[]{:S(2)}) collective-permute-start(bf16[1024,256]{1,0:T(8,128)(2,1)S(1)} %get-tuple-element.28), channel_id=1, source_target_pairs={{0,0},{1,16},{2,2},{3,18},{4,4},{5,20},{6,6},{7,22},{8,8},{9,24},{... | collective-permute-start | bytes 1572872 | tf_op jit(solution)/shard_map/ppermute | solution.py:57
  128.9 9.4 %collective-permute-start.16 = (bf16[1024,256]{1,0:T(8,128)(2,1)S(1)}, bf16[1024,256]{1,0:T(8,128)(2,1)}, u32[]{:S(2)}, u32[]{:S(2)}) collective-permute-start(bf16[1024,256]{1,0:T(8,128)(2,1)S(1)} %add_convert_fusion), channel_id=1, source_target_pairs={{0,4},{1,28},{2,6},{3,30},{4,8},{5,16},{6,10},{7,18},{8,12},{9,20}... | collective-permute-start | bytes 1572872 | tf_op jit(solution)/shard_map/ppermute | solution.py:57
  129.9 35.2 %copy-start.7 = (f32[1,256,256]{2,1,0:T(8,128)S(1)}, f32[1,256,256]{2,1,0:T(8,128)}, u32[]{:S(2)}) copy-start(f32[1,256,256]{2,1,0:T(8,128)} %param.7) | copy-start | bytes 786436
  139.6 26.3 %copy-start.6 = (bf16[1024,256]{1,0:T(8,128)(2,1)}, bf16[1024,256]{1,0:T(8,128)(2,1)S(1)}, u32[]{:S(2)}) copy-start(bf16[1024,256]{1,0:T(8,128)(2,1)S(1)} %select_convert_fusion) | copy-start | bytes 1572868
  140.0 4.4 %collective-permute-start.17 = (bf16[128,256]{1,0:T(8,128)(2,1)S(1)}, bf16[128,256]{1,0:T(8,128)(2,1)S(1)}, u32[]{:S(2)}, u32[]{:S(2)}) collective-permute-start(bf16[128,256]{1,0:T(8,128)(2,1)S(1)} %select_convert_fusion.1), channel_id=1, source_target_pairs={{0,16},{1,17},{2,18},{3,19},{4,20},{5,21},{6,22},{7,23},{8,24},{9,... | collective-permute-start | bytes 196616 | tf_op jit(solution)/shard_map/ppermute | solution.py:57
  144.3 4.4 %collective-permute-start.18 = (bf16[128,256]{1,0:T(8,128)(2,1)S(1)}, bf16[128,256]{1,0:T(8,128)(2,1)S(1)}, u32[]{:S(2)}, u32[]{:S(2)}) collective-permute-start(bf16[128,256]{1,0:T(8,128)(2,1)S(1)} %add_convert_fusion.8), channel_id=1, source_target_pairs={{0,32},{1,33},{2,34},{3,35},{4,36},{5,37},{6,38},{7,39},{8,40},{9,... | collective-permute-start | bytes 196616 | tf_op jit(solution)/shard_map/ppermute | solution.py:57
  148.7 5.7 %collective-permute-start.19 = (bf16[128,256]{1,0:T(8,128)(2,1)S(1)}, bf16[128,256]{1,0:T(8,128)(2,1)S(1)}, u32[]{:S(2)}, u32[]{:S(2)}) collective-permute-start(bf16[128,256]{1,0:T(8,128)(2,1)S(1)} %add_convert_fusion.7), channel_id=1, source_target_pairs={{0,64},{1,65},{2,66},{3,67},{4,68},{5,69},{6,70},{7,71},{8,72},{9,... | collective-permute-start | bytes 196616 | tf_op jit(solution)/shard_map/ppermute | solution.py:57
  154.4 6.3 %collective-permute-start.20 = (bf16[128,256]{1,0:T(8,128)(2,1)S(1)}, bf16[128,256]{1,0:T(8,128)(2,1)S(1)}, u32[]{:S(2)}, u32[]{:S(2)}) collective-permute-start(bf16[128,256]{1,0:T(8,128)(2,1)S(1)} %add_convert_fusion.6), channel_id=1, source_target_pairs={{0,224},{1,225},{2,226},{3,227},{4,228},{5,229},{6,230},{7,231},{8... | collective-permute-start | bytes 196616 | tf_op jit(solution)/shard_map/ppermute | solution.py:57
  160.7 4.4 %collective-permute-start.21 = (bf16[128,256]{1,0:T(8,128)(2,1)S(1)}, bf16[128,256]{1,0:T(8,128)(2,1)S(1)}, u32[]{:S(2)}, u32[]{:S(2)}) collective-permute-start(bf16[128,256]{1,0:T(8,128)(2,1)S(1)} %add_convert_fusion.5), channel_id=1, source_target_pairs={{0,16},{1,17},{2,18},{3,19},{4,20},{5,21},{6,22},{7,23},{8,24},{9,... | collective-permute-start | bytes 196616 | tf_op jit(solution)/shard_map/ppermute | solution.py:57

commit v6 on v5

--- a/solution.py
+++ b/solution.py
@@ -124,7 +124,7 @@
                 pltpu.make_async_copy(a_vmem.at[rows], a_vmem.at[rows], a_sem.at[tile]).wait()
             total = jnp.dot(a_vmem[rows], l_vmem[slot], preferred_element_type=F32)
             out_vmem[result, rows] = total.astype(BF16)
-        shift = jnp.where(slot == 1, sign, jnp.where(slot == 2, -sign, jnp.where(slot == 3, 2, 0)))
+        shift = (0, sign, -sign, 2)[slot]
         j = lax.rem((z // 2 + shift + 4) * order, 4)
         for choice, out in enumerate(outs):
             @pl.when(which == choice)
@@ -133,10 +133,12 @@
 
     if early:
         multiply(other_vmem, other_sem, 0, 0, other_order, other_out)
-        pl.loop(1, 3)(lambda slot: multiply(other_vmem, None, slot, slot, other_order, other_out))
+        for slot in range(1, 3):
+            multiply(other_vmem, None, slot, slot, other_order, other_out)
     else:
         multiply(own_vmem, own_sem, 0, 0, own_order, 1 - other_out)
-        pl.loop(1, 4)(lambda slot: multiply(own_vmem, None, slot, slot, own_order, 1 - other_out))
+        for slot in range(1, 4):
+            multiply(own_vmem, None, slot, slot, own_order, 1 - other_out)
         multiply(other_vmem, other_sem, 3, 4, other_order, other_out, wait_l=False)
     for result in range(3 if early else 5):
         pltpu.make_async_copy(out_vmem.at[result], outs[0].at[0], out_sem.at[result]).wait()

time: 168 us -> 168 us (level)
  no operation moved by 1% of the time
where the time goes in v6:
time: 168 us; the launch traced here: 166 us
  waiting for transfers between devices  103 us (61%)
  starting transfers between devices  33.4 us (20%)
  Pallas kernels  18.4 us (11%)
  other arithmetic  5.12 us (3%)
  local copies, waits for them, and re-layouts  3.44 us (2%)
  between operations  2.09 us (1%)
    ppermute x22, waiting for transfers between devices, move(): return lax.ppermute(value, AXES, pairs)  103 us
    ppermute x22, starting transfers between devices, move(): return lax.ppermute(value, AXES, pairs)  33.4 us
    pallas_call x2, Pallas kernels, product_call(): pl.pallas_call(functools.partial(product_kernel, early), in_specs=[pl.Blo...  18.4 us
  transfers between devices with their start and end apart: 22, of which 15 were waited for; matrix products, arithmetic and copies ran while one was open for 1% of the time, Pallas kernels for 4%

profile of v6, /device:TPU:2, one launch (start us, length us, event | category | flops | bytes accessed | tf_op | source)
XLA Modules:
  0.0 165.7 jit_solution(15063792040005770319)
XLA Ops:
  1.4 0.8 and_reduce_fusion
  2.4 1.2 bitcast_select_fusion
  4.3 2.9 %collective-permute-start.6 = (bf16[1024,1024]{1,0:T(8,128)(2,1)}, bf16[1024,1024]{1,0:T(8,128)(2,1)S(1)}, u32[]{:S(2)}, u32[]{:S(2)}) collective-permute-start(bf16[1024,1024]{1,0:T(8,128)(2,1)} %refs_0_.1), channel_id=1, source_target_pairs={{0,16},{1,19},{2,18},{3,17},{4,20},{5,23},{6,22},{7,21},{8,24},{9,... | collective-permute-start | bytes 6291464 | tf_op jit(solution)/shard_map/ppermute | solution.py:57
  7.2 1.7 %collective-permute-start.7 = (bf16[1024,1024]{1,0:T(8,128)(2,1)}, bf16[1024,1024]{1,0:T(8,128)(2,1)}, u32[]{:S(2)}, u32[]{:S(2)}) collective-permute-start(bf16[1024,1024]{1,0:T(8,128)(2,1)} %refs_0_.1), channel_id=1, source_target_pairs={{0,18},{1,17},{2,16},{3,19},{4,22},{5,21},{6,20},{7,23},{8,26},{9,... | collective-permute-start | bytes 6291464 | tf_op jit(solution)/shard_map/ppermute | solution.py:57
  8.9 5.1 %collective-permute-start.1 = (bf16[1024,256]{1,0:T(8,128)(2,1)S(1)}, bf16[1024,256]{1,0:T(8,128)(2,1)S(1)}, u32[]{:S(2)}, u32[]{:S(2)}) collective-permute-start(bf16[1024,256]{1,0:T(8,128)(2,1)S(1)} %collective-permute-done), channel_id=1, source_target_pairs={{0,0},{1,1},{2,2},{3,3},{4,64},{5,65},{6,66},{7,67},{8,128},{9,129... | collective-permute-start | bytes 1572872 | tf_op jit(solution)/shard_map/ppermute | solution.py:57
  14.1 21.1 %collective-permute-done.1.refs_2_.refs_4_ = bf16[1024,256]{1,0:T(8,128)(2,1)S(1)} collective-permute-done((bf16[1024,256]{1,0:T(8,128)(2,1)S(1)}, bf16[1024,256]{1,0:T(8,128)(2,1)S(1)}, u32[]{:S(2)}, u32[]{:S(2)}) %collective-permute-start.1) | collective-permute-done | bytes 524320 | tf_op jit(solution)/shard_map/ppermute | solution.py:57
  35.2 2.0 %collective-permute-start.2 = (bf16[1024,256]{1,0:T(8,128)(2,1)S(1)}, bf16[1024,256]{1,0:T(8,128)(2,1)S(1)}, u32[]{:S(2)}, u32[]{:S(2)}) collective-permute-start(bf16[1024,256]{1,0:T(8,128)(2,1)S(1)} %collective-permute-done.1.refs_2_.refs_4_), channel_id=1, source_target_pairs={{0,32},{1,225},{2,34},{3,227},{4,36},{5,229},{6,38},{7,231},{8,40}... | collective-permute-start | bytes 1572872 | tf_op jit(solution)/shard_map/ppermute | solution.py:57
  37.2 10.0 %collective-permute-done.4.refs_4_.refs_6_ = bf16[1024,256]{1,0:T(8,128)(2,1)S(1)} collective-permute-done((bf16[1024,256]{1,0:T(8,128)(2,1)S(1)}, bf16[1024,256]{1,0:T(8,128)(2,1)S(1)}, u32[]{:S(2)}, u32[]{:S(2)}) %collective-permute-start.4) | collective-permute-done | bytes 524320 | tf_op jit(solution)/shard_map/ppermute | solution.py:57
  47.2 4.9 %collective-permute-start.5 = (bf16[1024,256]{1,0:T(8,128)(2,1)S(1)}, bf16[1024,256]{1,0:T(8,128)(2,1)}, u32[]{:S(2)}, u32[]{:S(2)}) collective-permute-start(bf16[1024,256]{1,0:T(8,128)(2,1)S(1)} %collective-permute-done.4.refs_4_.refs_6_), channel_id=1, source_target_pairs={{0,224},{1,33},{2,226},{3,35},{4,228},{5,37},{6,230},{7,39},{8,232... | collective-permute-start | bytes 1572872 | tf_op jit(solution)/shard_map/ppermute | solution.py:57
  52.1 1.2 collective-permute-done.2.refs_3_.refs_5_
  54.2 7.8 %collective-permute-done.5.refs_6_.refs_8_ = bf16[1024,256]{1,0:T(8,128)(2,1)} collective-permute-done((bf16[1024,256]{1,0:T(8,128)(2,1)S(1)}, bf16[1024,256]{1,0:T(8,128)(2,1)}, u32[]{:S(2)}, u32[]{:S(2)}) %collective-permute-start.5) | collective-permute-done | bytes 524320 | tf_op jit(solution)/shard_map/ppermute | solution.py:57
  62.0 5.7 %collective-permute-done.3.refs_5_.refs_7_ = bf16[1024,256]{1,0:T(8,128)(2,1)} collective-permute-done((bf16[1024,256]{1,0:T(8,128)(2,1)S(1)}, bf16[1024,256]{1,0:T(8,128)(2,1)}, u32[]{:S(2)}, u32[]{:S(2)}) %collective-permute-start.3) | collective-permute-done | bytes 524320 | tf_op jit(solution)/shard_map/ppermute | solution.py:57
  67.7 4.0 %collective-permute-start.8 = (bf16[1024,1024]{1,0:T(8,128)(2,1)}, bf16[1024,1024]{1,0:T(8,128)(2,1)}, u32[]{:S(2)}, u32[]{:S(2)}) collective-permute-start(bf16[1024,1024]{1,0:T(8,128)(2,1)} %collective-permute-done.7.refs_1_.refs_3_), channel_id=1, source_target_pairs={{0,16},{1,19},{2,18},{3,17},{4,20},{5,23},{6,22},{7,21},{8,24},{9,... | collective-permute-start | bytes 6291464 | tf_op jit(solution)/shard_map/ppermute | solution.py:57
  71.6 3.2 %collective-permute-start.10 = (bf16[1024,256]{1,0:T(8,128)(2,1)}, bf16[1024,256]{1,0:T(8,128)(2,1)}, u32[]{:S(2)}, u32[]{:S(2)}) collective-permute-start(bf16[1024,256]{1,0:T(8,128)(2,1)} %collective-permute-done.5.refs_6_.refs_8_), channel_id=1, source_target_pairs={{0,224},{1,33},{2,226},{3,35},{4,228},{5,37},{6,230},{7,39},{8,232... | collective-permute-start | bytes 1572872 | tf_op jit(solution)/shard_map/ppermute | solution.py:57
  74.9 13.0 %collective-permute-done.9.refs_7_.refs_9_ = bf16[1024,256]{1,0:T(8,128)(2,1)} collective-permute-done((bf16[1024,256]{1,0:T(8,128)(2,1)}, bf16[1024,256]{1,0:T(8,128)(2,1)}, u32[]{:S(2)}, u32[]{:S(2)}) %collective-permute-start.9) | collective-permute-done | bytes 524320 | tf_op jit(solution)/shard_map/ppermute | solution.py:57
  89.9 1.2 copy-done.3
  91.1 7.2 %shard_map.68 = (bf16[4,1024,256]{2,1,0:T(8,128)(2,1)S(1)}, bf16[4,1024,256]{2,1,0:T(8,128)(2,1)S(1)}) custom-call(s32[7]{0:T(128)S(1)} %stack.40.scalars, bf16[1024,1024]{1,0:T(8,128)(2,1)S(1)} %collective-permute-done.6.refs_0_.refs_2_, bf16[1024,1024]{1,0:T(8,128)(2,1)} %collective-permute-done.7.refs_1_.refs_3_, ...), custom_call_target="tpu_custom_call" | custom-call | flops 3221225472 | bytes 10485760 | tf_op jit(solution)/shard_map/pallas_call | solution.py:151
  98.6 11.2 %shard_map.69 = (bf16[4,1024,256]{2,1,0:T(8,128)(2,1)S(1)}, bf16[4,1024,256]{2,1,0:T(8,128)(2,1)S(1)}) custom-call(s32[7]{0:T(128)S(1)} %stack.40.scalars, bf16[1024,1024]{1,0:T(8,128)(2,1)S(1)} %copy-done.1, bf16[1024,1024]{1,0:T(8,128)(2,1)} %collective-permute-done.8.refs_1_, ...), custom_call_target="tpu_custom_call", output_to_operand_aliasing={{0}: (13, {}), {1}: (14, {})} | custom-call | flops 5368709120 | bytes 10485760 | tf_op jit(solution)/shard_map/pallas_call | solution.py:151
  110.0 4.1 %collective-permute-done.12 = bf16[4,1024,256]{2,1,0:T(8,128)(2,1)S(1)} collective-permute-done((bf16[4,1024,256]{2,1,0:T(8,128)(2,1)S(1)}, bf16[4,1024,256]{2,1,0:T(8,128)(2,1)S(1)}, u32[]{:S(2)}, u32[]{:S(2)}) %collective-permute-start.12) | collective-permute-done | bytes 2097184 | tf_op jit(solution)/shard_map/ppermute | solution.py:57
  114.3 1.1 collective-permute-start.15
  115.8 1.1 collective-permute-start.13
  117.6 10.9 %collective-permute-done.15 = bf16[1024,256]{1,0:T(8,128)(2,1)S(1)} collective-permute-done((bf16[1024,256]{1,0:T(8,128)(2,1)S(1)}, bf16[1024,256]{1,0:T(8,128)(2,1)S(1)}, u32[]{:S(2)}, u32[]{:S(2)}) %collective-permute-start.15) | collective-permute-done | bytes 524320 | tf_op jit(solution)/shard_map/ppermute | solution.py:57
  128.6 1.0 collective-permute-start.16
  129.6 8.4 %collective-permute-done.16 = bf16[1024,256]{1,0:T(8,128)(2,1)} collective-permute-done((bf16[1024,256]{1,0:T(8,128)(2,1)S(1)}, bf16[1024,256]{1,0:T(8,128)(2,1)}, u32[]{:S(2)}, u32[]{:S(2)}) %collective-permute-start.16) | collective-permute-done | bytes 524320 | tf_op jit(solution)/shard_map/ppermute | solution.py:57
  138.0 1.3 select_convert_fusion
  139.8 4.3 %collective-permute-done.17 = bf16[128,256]{1,0:T(8,128)(2,1)S(1)} collective-permute-done((bf16[128,256]{1,0:T(8,128)(2,1)S(1)}, bf16[128,256]{1,0:T(8,128)(2,1)S(1)}, u32[]{:S(2)}, u32[]{:S(2)}) %collective-permute-start.17) | collective-permute-done | bytes 65568 | tf_op jit(solution)/shard_map/ppermute | solution.py:57
  144.2 4.3 %collective-permute-done.18 = bf16[128,256]{1,0:T(8,128)(2,1)S(1)} collective-permute-done((bf16[128,256]{1,0:T(8,128)(2,1)S(1)}, bf16[128,256]{1,0:T(8,128)(2,1)S(1)}, u32[]{:S(2)}, u32[]{:S(2)}) %collective-permute-start.18) | collective-permute-done | bytes 65568 | tf_op jit(solution)/shard_map/ppermute | solution.py:57
  148.5 1.3 collective-permute-start.19
  149.8 4.4 %collective-permute-done.19 = bf16[128,256]{1,0:T(8,128)(2,1)S(1)} collective-permute-done((bf16[128,256]{1,0:T(8,128)(2,1)S(1)}, bf16[128,256]{1,0:T(8,128)(2,1)S(1)}, u32[]{:S(2)}, u32[]{:S(2)}) %collective-permute-start.19) | collective-permute-done | bytes 65568 | tf_op jit(solution)/shard_map/ppermute | solution.py:57
  154.3 3.2 %collective-permute-start.20 = (bf16[128,256]{1,0:T(8,128)(2,1)S(1)}, bf16[128,256]{1,0:T(8,128)(2,1)S(1)}, u32[]{:S(2)}, u32[]{:S(2)}) collective-permute-start(bf16[128,256]{1,0:T(8,128)(2,1)S(1)} %add_convert_fusion.6), channel_id=1, source_target_pairs={{0,224},{1,225},{2,226},{3,227},{4,228},{5,229},{6,230},{7,231},{8... | collective-permute-start | bytes 196616 | tf_op jit(solution)/shard_map/ppermute | solution.py:57
  157.4 3.1 %collective-permute-done.20 = bf16[128,256]{1,0:T(8,128)(2,1)S(1)} collective-permute-done((bf16[128,256]{1,0:T(8,128)(2,1)S(1)}, bf16[128,256]{1,0:T(8,128)(2,1)S(1)}, u32[]{:S(2)}, u32[]{:S(2)}) %collective-permute-start.20) | collective-permute-done | bytes 65568 | tf_op jit(solution)/shard_map/ppermute | solution.py:57
  160.6 4.3 %collective-permute-done.21 = bf16[128,256]{1,0:T(8,128)(2,1)S(1)} collective-permute-done((bf16[128,256]{1,0:T(8,128)(2,1)S(1)}, bf16[128,256]{1,0:T(8,128)(2,1)S(1)}, u32[]{:S(2)}, u32[]{:S(2)}) %collective-permute-start.21) | collective-permute-done | bytes 65568 | tf_op jit(solution)/shard_map/ppermute | solution.py:57
  (52 shorter events, 6.4 us)
Async XLA Ops:
  0.6 0.7 copy-start
  3.6 64.1 %copy-start.4 = (bf16[1024,256]{1,0:T(8,128)(2,1)}, bf16[1024,256]{1,0:T(8,128)(2,1)S(1)}, u32[]{:S(2)}) copy-start(bf16[1024,256]{1,0:T(8,128)(2,1)S(1)} %bitcast_select_fusion) | copy-start | bytes 1572868
  3.6 5.3 %collective-permute-start = (bf16[1024,256]{1,0:T(8,128)(2,1)S(1)}, bf16[1024,256]{1,0:T(8,128)(2,1)S(1)}, u32[]{:S(2)}, u32[]{:S(2)}) collective-permute-start(bf16[1024,256]{1,0:T(8,128)(2,1)S(1)} %bitcast_select_fusion), channel_id=1, source_target_pairs={{0,0},{1,16},{2,2},{3,18},{4,4},{5,20},{6,6},{7,22},{8,8},{9,24},{... | collective-permute-start | bytes 1572872 | tf_op jit(solution)/shard_map/ppermute | solution.py:57
  4.3 63.3 %collective-permute-start.6 = (bf16[1024,1024]{1,0:T(8,128)(2,1)}, bf16[1024,1024]{1,0:T(8,128)(2,1)S(1)}, u32[]{:S(2)}, u32[]{:S(2)}) collective-permute-start(bf16[1024,1024]{1,0:T(8,128)(2,1)} %refs_0_.1), channel_id=1, source_target_pairs={{0,16},{1,19},{2,18},{3,17},{4,20},{5,23},{6,22},{7,21},{8,24},{9,... | collective-permute-start | bytes 6291464 | tf_op jit(solution)/shard_map/ppermute | solution.py:57
  7.2 60.5 %collective-permute-start.7 = (bf16[1024,1024]{1,0:T(8,128)(2,1)}, bf16[1024,1024]{1,0:T(8,128)(2,1)}, u32[]{:S(2)}, u32[]{:S(2)}) collective-permute-start(bf16[1024,1024]{1,0:T(8,128)(2,1)} %refs_0_.1), channel_id=1, source_target_pairs={{0,18},{1,17},{2,16},{3,19},{4,22},{5,21},{6,20},{7,23},{8,26},{9,... | collective-permute-start | bytes 6291464 | tf_op jit(solution)/shard_map/ppermute | solution.py:57
  8.9 26.3 %collective-permute-start.1 = (bf16[1024,256]{1,0:T(8,128)(2,1)S(1)}, bf16[1024,256]{1,0:T(8,128)(2,1)S(1)}, u32[]{:S(2)}, u32[]{:S(2)}) collective-permute-start(bf16[1024,256]{1,0:T(8,128)(2,1)S(1)} %collective-permute-done), channel_id=1, source_target_pairs={{0,0},{1,1},{2,2},{3,3},{4,64},{5,65},{6,66},{7,67},{8,128},{9,129... | collective-permute-start | bytes 1572872 | tf_op jit(solution)/shard_map/ppermute | solution.py:57
  35.2 12.0 %collective-permute-start.4 = (bf16[1024,256]{1,0:T(8,128)(2,1)S(1)}, bf16[1024,256]{1,0:T(8,128)(2,1)S(1)}, u32[]{:S(2)}, u32[]{:S(2)}) collective-permute-start(bf16[1024,256]{1,0:T(8,128)(2,1)S(1)} %collective-permute-done.1.refs_2_.refs_4_), channel_id=1, source_target_pairs={{0,224},{1,33},{2,226},{3,35},{4,228},{5,37},{6,230},{7,39},{8,232... | collective-permute-start | bytes 1572872 | tf_op jit(solution)/shard_map/ppermute | solution.py:57
  35.2 18.1 %collective-permute-start.2 = (bf16[1024,256]{1,0:T(8,128)(2,1)S(1)}, bf16[1024,256]{1,0:T(8,128)(2,1)S(1)}, u32[]{:S(2)}, u32[]{:S(2)}) collective-permute-start(bf16[1024,256]{1,0:T(8,128)(2,1)S(1)} %collective-permute-done.1.refs_2_.refs_4_), channel_id=1, source_target_pairs={{0,32},{1,225},{2,34},{3,227},{4,36},{5,229},{6,38},{7,231},{8,40}... | collective-permute-start | bytes 1572872 | tf_op jit(solution)/shard_map/ppermute | solution.py:57
  47.2 14.8 %collective-permute-start.5 = (bf16[1024,256]{1,0:T(8,128)(2,1)S(1)}, bf16[1024,256]{1,0:T(8,128)(2,1)}, u32[]{:S(2)}, u32[]{:S(2)}) collective-permute-start(bf16[1024,256]{1,0:T(8,128)(2,1)S(1)} %collective-permute-done.4.refs_4_.refs_6_), channel_id=1, source_target_pairs={{0,224},{1,33},{2,226},{3,35},{4,228},{5,37},{6,230},{7,39},{8,232... | collective-permute-start | bytes 1572872 | tf_op jit(solution)/shard_map/ppermute | solution.py:57
  53.4 14.3 %collective-permute-start.3 = (bf16[1024,256]{1,0:T(8,128)(2,1)S(1)}, bf16[1024,256]{1,0:T(8,128)(2,1)}, u32[]{:S(2)}, u32[]{:S(2)}) collective-permute-start(bf16[1024,256]{1,0:T(8,128)(2,1)S(1)} %collective-permute-done.2.refs_3_.refs_5_), channel_id=1, source_target_pairs={{0,32},{1,225},{2,34},{3,227},{4,36},{5,229},{6,38},{7,231},{8,40}... | collective-permute-start | bytes 1572872 | tf_op jit(solution)/shard_map/ppermute | solution.py:57
  53.4 0.8 copy-start.2
  67.7 31.0 %collective-permute-start.8 = (bf16[1024,1024]{1,0:T(8,128)(2,1)}, bf16[1024,1024]{1,0:T(8,128)(2,1)}, u32[]{:S(2)}, u32[]{:S(2)}) collective-permute-start(bf16[1024,1024]{1,0:T(8,128)(2,1)} %collective-permute-done.7.refs_1_.refs_3_), channel_id=1, source_target_pairs={{0,16},{1,19},{2,18},{3,17},{4,20},{5,23},{6,22},{7,21},{8,24},{9,... | collective-permute-start | bytes 6291464 | tf_op jit(solution)/shard_map/ppermute | solution.py:57
  71.6 16.3 %collective-permute-start.9 = (bf16[1024,256]{1,0:T(8,128)(2,1)}, bf16[1024,256]{1,0:T(8,128)(2,1)}, u32[]{:S(2)}, u32[]{:S(2)}) collective-permute-start(bf16[1024,256]{1,0:T(8,128)(2,1)} %collective-permute-done.3.refs_5_.refs_7_), channel_id=1, source_target_pairs={{0,32},{1,225},{2,34},{3,227},{4,36},{5,229},{6,38},{7,231},{8,40}... | collective-permute-start | bytes 1572872 | tf_op jit(solution)/shard_map/ppermute | solution.py:57
  71.6 18.3 %collective-permute-start.10 = (bf16[1024,256]{1,0:T(8,128)(2,1)}, bf16[1024,256]{1,0:T(8,128)(2,1)}, u32[]{:S(2)}, u32[]{:S(2)}) collective-permute-start(bf16[1024,256]{1,0:T(8,128)(2,1)} %collective-permute-done.5.refs_6_.refs_8_), channel_id=1, source_target_pairs={{0,224},{1,33},{2,226},{3,35},{4,228},{5,37},{6,230},{7,39},{8,232... | collective-permute-start | bytes 1572872 | tf_op jit(solution)/shard_map/ppermute | solution.py:57
  87.9 10.7 %collective-permute-start.11 = (bf16[1024,256]{1,0:T(8,128)(2,1)}, bf16[1024,256]{1,0:T(8,128)(2,1)}, u32[]{:S(2)}, u32[]{:S(2)}) collective-permute-start(bf16[1024,256]{1,0:T(8,128)(2,1)} %collective-permute-done.9.refs_7_.refs_9_), channel_id=1, source_target_pairs={{0,32},{1,225},{2,34},{3,227},{4,36},{5,229},{6,38},{7,231},{8,40}... | collective-permute-start | bytes 1572872 | tf_op jit(solution)/shard_map/ppermute | solution.py:57
  89.9 8.7 %copy-start.1 = (bf16[1024,1024]{1,0:T(8,128)(2,1)S(1)}, bf16[1024,1024]{1,0:T(8,128)(2,1)}, u32[]{:S(2)}) copy-start(bf16[1024,1024]{1,0:T(8,128)(2,1)} %refs_0_.1) | copy-start | bytes 6291460
  89.9 1.2 copy-start.3
  109.9 4.2 %collective-permute-start.12 = (bf16[4,1024,256]{2,1,0:T(8,128)(2,1)S(1)}, bf16[4,1024,256]{2,1,0:T(8,128)(2,1)S(1)}, u32[]{:S(2)}, u32[]{:S(2)}) collective-permute-start(bf16[4,1024,256]{2,1,0:T(8,128)(2,1)S(1)} %get-tuple-element.24), channel_id=1, source_target_pairs={{0,1},{1,0},{2,3},{3,2},{4,5},{5,4},{6,7},{7,6},{8,9},{9,8},{10,11... | collective-permute-start | bytes 6291464 | tf_op jit(solution)/shard_map/ppermute | solution.py:57
  114.3 14.2 %collective-permute-start.15 = (bf16[1024,256]{1,0:T(8,128)(2,1)S(1)}, bf16[1024,256]{1,0:T(8,128)(2,1)S(1)}, u32[]{:S(2)}, u32[]{:S(2)}) collective-permute-start(bf16[1024,256]{1,0:T(8,128)(2,1)S(1)} %fusion), channel_id=1, source_target_pairs={{0,4},{1,13},{2,6},{3,15},{4,8},{5,1},{6,10},{7,3},{8,12},{9,5},{1... | collective-permute-start | bytes 1572872 | tf_op jit(solution)/shard_map/ppermute | solution.py:57
  115.8 23.5 %copy-start.5 = (bf16[1024,256]{1,0:T(8,128)(2,1)S(1)}, bf16[1024,256]{1,0:T(8,128)(2,1)}, u32[]{:S(2)}) copy-start(bf16[1024,256]{1,0:T(8,128)(2,1)} %copy-done.4) | copy-start | bytes 1572868
  115.8 13.8 %collective-permute-start.13 = (bf16[1024,256]{1,0:T(8,128)(2,1)S(1)}, bf16[1024,256]{1,0:T(8,128)(2,1)S(1)}, u32[]{:S(2)}, u32[]{:S(2)}) collective-permute-start(bf16[1024,256]{1,0:T(8,128)(2,1)S(1)} %get-tuple-element.27), channel_id=1, source_target_pairs={{0,12},{1,20},{2,14},{3,22},{4,0},{5,24},{6,2},{7,26},{8,4},{9,28}... | collective-permute-start | bytes 1572872 | tf_op jit(solution)/shard_map/ppermute | solution.py:57
  116.9 12.7 %collective-permute-start.14 = (bf16[1024,256]{1,0:T(8,128)(2,1)S(1)}, bf16[1024,256]{1,0:T(8,128)(2,1)S(1)}, u32[]{:S(2)}, u32[]{:S(2)}) collective-permute-start(bf16[1024,256]{1,0:T(8,128)(2,1)S(1)} %get-tuple-element.28), channel_id=1, source_target_pairs={{0,0},{1,16},{2,2},{3,18},{4,4},{5,20},{6,6},{7,22},{8,8},{9,24},{... | collective-permute-start | bytes 1572872 | tf_op jit(solution)/shard_map/ppermute | solution.py:57
  128.6 9.4 %collective-permute-start.16 = (bf16[1024,256]{1,0:T(8,128)(2,1)S(1)}, bf16[1024,256]{1,0:T(8,128)(2,1)}, u32[]{:S(2)}, u32[]{:S(2)}) collective-permute-start(bf16[1024,256]{1,0:T(8,128)(2,1)S(1)} %add_convert_fusion), channel_id=1, source_target_pairs={{0,4},{1,28},{2,6},{3,30},{4,8},{5,16},{6,10},{7,18},{8,12},{9,20}... | collective-permute-start | bytes 1572872 | tf_op jit(solution)/shard_map/ppermute | solution.py:57
  129.6 35.3 %copy-start.7 = (f32[1,256,256]{2,1,0:T(8,128)S(1)}, f32[1,256,256]{2,1,0:T(8,128)}, u32[]{:S(2)}) copy-start(f32[1,256,256]{2,1,0:T(8,128)} %param.7) | copy-start | bytes 786436
  139.3 26.3 %copy-start.6 = (bf16[1024,256]{1,0:T(8,128)(2,1)}, bf16[1024,256]{1,0:T(8,128)(2,1)S(1)}, u32[]{:S(2)}) copy-start(bf16[1024,256]{1,0:T(8,128)(2,1)S(1)} %select_convert_fusion) | copy-start | bytes 1572868
  139.7 4.4 %collective-permute-start.17 = (bf16[128,256]{1,0:T(8,128)(2,1)S(1)}, bf16[128,256]{1,0:T(8,128)(2,1)S(1)}, u32[]{:S(2)}, u32[]{:S(2)}) collective-permute-start(bf16[128,256]{1,0:T(8,128)(2,1)S(1)} %select_convert_fusion.1), channel_id=1, source_target_pairs={{0,16},{1,17},{2,18},{3,19},{4,20},{5,21},{6,22},{7,23},{8,24},{9,... | collective-permute-start | bytes 196616 | tf_op jit(solution)/shard_map/ppermute | solution.py:57
  144.1 4.4 %collective-permute-start.18 = (bf16[128,256]{1,0:T(8,128)(2,1)S(1)}, bf16[128,256]{1,0:T(8,128)(2,1)S(1)}, u32[]{:S(2)}, u32[]{:S(2)}) collective-permute-start(bf16[128,256]{1,0:T(8,128)(2,1)S(1)} %add_convert_fusion.8), channel_id=1, source_target_pairs={{0,32},{1,33},{2,34},{3,35},{4,36},{5,37},{6,38},{7,39},{8,40},{9,... | collective-permute-start | bytes 196616 | tf_op jit(solution)/shard_map/ppermute | solution.py:57
  148.5 5.7 %collective-permute-start.19 = (bf16[128,256]{1,0:T(8,128)(2,1)S(1)}, bf16[128,256]{1,0:T(8,128)(2,1)S(1)}, u32[]{:S(2)}, u32[]{:S(2)}) collective-permute-start(bf16[128,256]{1,0:T(8,128)(2,1)S(1)} %add_convert_fusion.7), channel_id=1, source_target_pairs={{0,64},{1,65},{2,66},{3,67},{4,68},{5,69},{6,70},{7,71},{8,72},{9,... | collective-permute-start | bytes 196616 | tf_op jit(solution)/shard_map/ppermute | solution.py:57
  154.3 6.3 %collective-permute-start.20 = (bf16[128,256]{1,0:T(8,128)(2,1)S(1)}, bf16[128,256]{1,0:T(8,128)(2,1)S(1)}, u32[]{:S(2)}, u32[]{:S(2)}) collective-permute-start(bf16[128,256]{1,0:T(8,128)(2,1)S(1)} %add_convert_fusion.6), channel_id=1, source_target_pairs={{0,224},{1,225},{2,226},{3,227},{4,228},{5,229},{6,230},{7,231},{8... | collective-permute-start | bytes 196616 | tf_op jit(solution)/shard_map/ppermute | solution.py:57
  160.5 4.4 %collective-permute-start.21 = (bf16[128,256]{1,0:T(8,128)(2,1)S(1)}, bf16[128,256]{1,0:T(8,128)(2,1)S(1)}, u32[]{:S(2)}, u32[]{:S(2)}) collective-permute-start(bf16[128,256]{1,0:T(8,128)(2,1)S(1)} %add_convert_fusion.5), channel_id=1, source_target_pairs={{0,16},{1,17},{2,18},{3,19},{4,20},{5,21},{6,22},{7,23},{8,24},{9,... | collective-permute-start | bytes 196616 | tf_op jit(solution)/shard_map/ppermute | solution.py:57
